TPU v7x, 32 devices: a whole 2x2x4 slice. The times are simulated.
32 devices in a mesh: ctx: 8 (over y, x, core), head: 4 (over z).
Axes of the slice: x: 2, y: 2, z: 4, core: 2. Of those that a mesh axis runs over, the one named last changes fastest.
Arguments:
- block_order: int32 [16], replicated, may hold values from 0 to 15, each once
- queries: bfloat16 [1792, 32, 576], P('ctx', 'head'), may hold values from -10 to 10
- keys: bfloat16 [1792, 576], P('ctx'), may hold values from -4 to 4
- dout: bfloat16 [1792, 32, 512], P('ctx', 'head'), may hold values from -6 to 6
Outputs:
- grad_queries: bfloat16 [1792, 32, 576], P('ctx', 'head')
- grad_keys: float32 [1792, 576], P('ctx')
Inputs may be any that keep to these rules, and one draw needn't show every extreme that they name: block_order holds each of 0 to 15 once.
All inputs are finite; a program needn't handle non-finite values.
Results may differ from a plain program's by a relative error of at most 0.0048.
Values may be sent and summed in bfloat16 or wider, within the bound.
No kernel may reach another device: no remote copies, remote signals or barrier semaphores. Data moves between devices by JAX's collectives and lax.ppermute only.
A program may use at most 64 MiB of HBM per device.

v0:
```python
import jax
import jax.numpy as jnp
from jax import lax
from jax.sharding import PartitionSpec as P

softmax_scale = 0.1352
masked_value = -1e30


def per_device(block_order, queries, keys, dout):
    token_count, head_count, key_width = queries.shape
    latent_width = dout.shape[2]
    block_rows = token_count // 2
    ctx_index = lax.axis_index("ctx")
    offsets = jnp.arange(block_rows, dtype=jnp.int32)
    all_positions = (block_order[:, None] * block_rows + offsets[None, :]).reshape(-1)
    own_positions = lax.dynamic_slice_in_dim(all_positions, ctx_index * token_count, token_count)
    row_positions = jnp.repeat(own_positions, head_count)
    query_last = jnp.max(own_positions)
    query_rows = queries.reshape(token_count * head_count, key_width)
    grad_rows = dout.reshape(token_count * head_count, latent_width)
    row_count = query_rows.shape[0]
    seq_length = token_count * lax.axis_size("ctx")
    contract_rows = (((0,), (0,)), ((), ()))

    def block_scores(key_block, key_pos):
        scores = (
            jnp.dot(query_rows, key_block.T, preferred_element_type=jnp.float32) * softmax_scale
        )
        return jnp.where(key_pos[None, :] <= row_positions[:, None], scores, masked_value)

    def split_piece(piece):
        count = piece.shape[0] // token_count
        return (
            piece.reshape(count, token_count, key_width),
            all_positions.reshape(count, token_count),
        )

    def make_second(peak, total, delta):

        def second_fold(carry, piece, start):
            grad_query, grad_keys = carry
            blocks, positions = split_piece(piece)

            def second_visit(accum, items):
                key_block, key_pos = items

                def second_compute(accum):
                    scores = block_scores(key_block, key_pos)
                    probs = jnp.exp(scores - peak[:, None]) / total[:, None]
                    grad_probs = jnp.dot(
                        grad_rows, key_block[:, :latent_width].T, preferred_element_type=jnp.float32
                    )
                    grad_scores = (probs * (grad_probs - delta[:, None])).astype(jnp.bfloat16)
                    probs_half = probs.astype(jnp.bfloat16)
                    accum = (
                        accum
                        + jnp.dot(grad_scores, key_block, preferred_element_type=jnp.float32)
                        * softmax_scale
                    )
                    key_part = (
                        lax.dot_general(
                            grad_scores,
                            query_rows,
                            contract_rows,
                            preferred_element_type=jnp.float32,
                        )
                        * softmax_scale
                    )
                    value_part = lax.dot_general(
                        probs_half, grad_rows, contract_rows, preferred_element_type=jnp.float32
                    )
                    return (
                        accum,
                        key_part + jnp.pad(value_part, ((0, 0), (0, key_width - latent_width))),
                    )

                def skip(accum):
                    return (accum, jnp.zeros((token_count, key_width), jnp.float32))

                return lax.cond(jnp.min(key_pos) <= query_last, second_compute, skip, accum)

            grad_query, key_terms = lax.scan(second_visit, grad_query, (blocks, positions))
            length = piece.shape[0]
            grad_keys = key_terms.reshape(length, key_width)
            return (grad_query, grad_keys)

        return second_fold

    start_state = (
        jnp.full((row_count,), masked_value, jnp.float32),
        jnp.zeros((row_count,), jnp.float32),
        jnp.zeros((row_count,), jnp.float32),
    )
    second_start = (
        jnp.zeros((row_count, key_width), jnp.float32),
        jnp.zeros((seq_length, key_width), jnp.float32),
    )
    carry = start_state
    blocks, positions = split_piece(lax.all_gather(keys, "ctx", axis=0, tiled=True))

    def first_visit(state, items):
        key_block, key_pos = items

        def first_compute(state):
            peak, total, weighted = state
            scores = block_scores(key_block, key_pos)
            grad_probs = jnp.dot(
                grad_rows, key_block[:, :latent_width].T, preferred_element_type=jnp.float32
            )
            new_peak = jnp.maximum(peak, jnp.max(scores, axis=1))
            factor = jnp.exp(peak - new_peak)
            weights = jnp.exp(scores - new_peak[:, None])
            total = total * factor + jnp.sum(weights, axis=1)
            weighted = weighted * factor + jnp.sum(weights * grad_probs, axis=1)
            return (new_peak, total, weighted)

        def keep(state):
            return state

        return (lax.cond(jnp.min(key_pos) <= query_last, first_compute, keep, state), None)

    carry, unused = lax.scan(first_visit, carry, (blocks, positions))
    peak, total, weighted = carry
    second_fold = make_second(peak, total, weighted / total)
    grad_query, grad_keys = second_fold(
        second_start, lax.all_gather(keys, "ctx", axis=0, tiled=True), jnp.int32(0)
    )
    grad_queries = grad_query.reshape(token_count, head_count, key_width).astype(jnp.bfloat16)
    own_terms = lax.psum_scatter(grad_keys, "ctx", scatter_dimension=0, tiled=True)
    key_result = lax.psum(own_terms, "head")
    return (grad_queries, key_result)


def solution(mesh):
    placed = (P(), P("ctx", "head", None), P("ctx", None), P("ctx", "head", None))
    return jax.shard_map(
        per_device,
        mesh=mesh,
        in_specs=placed,
        out_specs=(P("ctx", "head", None), P("ctx", None)),
        check_vma=False,
    )
```

profile of v0, /device:TPU:0, one launch (start us, length us, event | category | flops | bytes accessed | tf_op | source)
XLA Modules:
  0.0 316.6 jit_solution(14750420894000511195)
XLA Ops:
  9.8 31.5 %all-gather.2.cloned.1.call-done = bf16[1792,576]{1,0:T(8,128)(2,1)} async-done(((bf16[224,576]{1,0:T(8,128)(2,1)}), bf16[1792,576]{1,0:T(8,128)(2,1)}) %all-gather.2.cloned.1.call-update) | async-done | bytes 2064400 | tf_op jit(solution)/shard_map/all_gather | solution.py:127
  41.4 45.7 %while.31 = (s32[]{:T(128)}, f32[1792]{0:T(1024)S(1)}, f32[1792]{0:T(1024)S(1)}, f32[1792]{0:T(1024)S(1)}, s32[8,224]{1,0:T(8,128)S(1)}, /*index=5*/s32[]{:T(128...) while((s32[]{:T(128)}, f32[1792]{0:T(1024)S(1)}, ...), condition=%wide.region_8.9_spmd.clone, body=%wide.region_1.8_spmd.clone.sunk | while | flops 877082112 | bytes 17222444 | solution.py:123
  43.3 5.0 %conditional.6 = ((f32[1792]{0:T(1024)S(1)}, f32[1792]{0:T(1024)S(1)}, f32[1792]{0:T(1024)S(1)})) conditional(s32[]{:T(128)} %convert_element_type.31, (f32[1792]{0:T(1024)S(1)}, f32[1792]{0:T(1024)S(1)}, f32[1792]{0:T(1024)S(1)}) %tuple.75, (s32[1,224]{1,0:T(1,128)S(1)}, s32[224]{0:T(256)S(1)}, bf16[8,224,576]{2,1,0:T(8,128)(2,1)}, s32[]{:T(128)}, ...), branch_computations={%region_3.3_spmd, %region_4.7_spmd} | conditional | flops 877081856 | bytes 17220416 | solution.py:121
  43.5 1.0 dynamic-slice_bitcast_fusion
  44.5 2.7 fusion.26
  52.3 5.0 %conditional.6 = ((f32[1792]{0:T(1024)S(1)}, f32[1792]{0:T(1024)S(1)}, f32[1792]{0:T(1024)S(1)})) conditional(s32[]{:T(128)} %convert_element_type.31, (f32[1792]{0:T(1024)S(1)}, f32[1792]{0:T(1024)S(1)}, f32[1792]{0:T(1024)S(1)}) %tuple.75, (s32[1,224]{1,0:T(1,128)S(1)}, s32[224]{0:T(256)S(1)}, bf16[8,224,576]{2,1,0:T(8,128)(2,1)}, s32[]{:T(128)}, ...), branch_computations={%region_3.3_spmd, %region_4.7_spmd} | conditional | flops 877081856 | bytes 17220416 | solution.py:121
  52.5 1.0 dynamic-slice_bitcast_fusion
  53.5 2.7 fusion.26
  61.2 5.0 %conditional.6 = ((f32[1792]{0:T(1024)S(1)}, f32[1792]{0:T(1024)S(1)}, f32[1792]{0:T(1024)S(1)})) conditional(s32[]{:T(128)} %convert_element_type.31, (f32[1792]{0:T(1024)S(1)}, f32[1792]{0:T(1024)S(1)}, f32[1792]{0:T(1024)S(1)}) %tuple.75, (s32[1,224]{1,0:T(1,128)S(1)}, s32[224]{0:T(256)S(1)}, bf16[8,224,576]{2,1,0:T(8,128)(2,1)}, s32[]{:T(128)}, ...), branch_computations={%region_3.3_spmd, %region_4.7_spmd} | conditional | flops 877081856 | bytes 17220416 | solution.py:121
  61.4 1.0 dynamic-slice_bitcast_fusion
  62.4 2.7 fusion.26
  68.1 5.0 %conditional.6 = ((f32[1792]{0:T(1024)S(1)}, f32[1792]{0:T(1024)S(1)}, f32[1792]{0:T(1024)S(1)})) conditional(s32[]{:T(128)} %convert_element_type.31, (f32[1792]{0:T(1024)S(1)}, f32[1792]{0:T(1024)S(1)}, f32[1792]{0:T(1024)S(1)}) %tuple.75, (s32[1,224]{1,0:T(1,128)S(1)}, s32[224]{0:T(256)S(1)}, bf16[8,224,576]{2,1,0:T(8,128)(2,1)}, s32[]{:T(128)}, ...), branch_computations={%region_3.3_spmd, %region_4.7_spmd} | conditional | flops 877081856 | bytes 17220416 | solution.py:121
  68.4 1.0 dynamic-slice_bitcast_fusion
  69.4 2.7 fusion.26
  75.1 5.0 %conditional.6 = ((f32[1792]{0:T(1024)S(1)}, f32[1792]{0:T(1024)S(1)}, f32[1792]{0:T(1024)S(1)})) conditional(s32[]{:T(128)} %convert_element_type.31, (f32[1792]{0:T(1024)S(1)}, f32[1792]{0:T(1024)S(1)}, f32[1792]{0:T(1024)S(1)}) %tuple.75, (s32[1,224]{1,0:T(1,128)S(1)}, s32[224]{0:T(256)S(1)}, bf16[8,224,576]{2,1,0:T(8,128)(2,1)}, s32[]{:T(128)}, ...), branch_computations={%region_3.3_spmd, %region_4.7_spmd} | conditional | flops 877081856 | bytes 17220416 | solution.py:121
  75.3 1.0 dynamic-slice_bitcast_fusion
  76.3 2.7 fusion.26
  82.0 5.0 %conditional.6 = ((f32[1792]{0:T(1024)S(1)}, f32[1792]{0:T(1024)S(1)}, f32[1792]{0:T(1024)S(1)})) conditional(s32[]{:T(128)} %convert_element_type.31, (f32[1792]{0:T(1024)S(1)}, f32[1792]{0:T(1024)S(1)}, f32[1792]{0:T(1024)S(1)}) %tuple.75, (s32[1,224]{1,0:T(1,128)S(1)}, s32[224]{0:T(256)S(1)}, bf16[8,224,576]{2,1,0:T(8,128)(2,1)}, s32[]{:T(128)}, ...), branch_computations={%region_3.3_spmd, %region_4.7_spmd} | conditional | flops 877081856 | bytes 17220416 | solution.py:121
  82.3 1.0 dynamic-slice_bitcast_fusion
  83.3 2.7 fusion.26
  87.1 2.3 broadcast_in_dim.38
  89.3 91.3 %while.32 = (s32[]{:T(128)}, f32[1792,576]{0,1:T(8,128)}, f32[8,224,576]{2,1,0:T(8,128)}, s32[8,224]{1,0:T(8,128)S(1)}, s32[]{:T(128)}, /*index=5*/bf16[8,224,57...) while((s32[]{:T(128)}, f32[1792,576]{0,1:T(8,128)}, ...), condition=%wide.region_13.14_spmd.clone, body=%wide.region_9.13_spmd.clone.sunk | while | flops 2215284992 | bytes 68409680 | solution.py:83
  91.2 11.5 %conditional.7 = (f32[1792,576]{0,1:T(8,128)}, f32[1,224,576]{2,1,0:T(8,128)S(1)}) conditional(s32[]{:T(128)} %convert_element_type.32, f32[1792,576]{0,1:T(8,128)} %get-tuple-element.560, (s32[1,224]{1,0:T(1,128)S(1)}, s32[224]{0:T(256)S(1)}, bf16[8,224,576]{2,1,0:T(8,128)(2,1)}, s32[]{:T(128)}, bf16[1792,576]{1,0:T(8,128)(2,1)}, ...), branch_computations={%region_11.11_spmd, %region_12.12_spmd} | conditional | flops 2215284736 | bytes 67317608 | solution.py:81
  91.4 1.0 dynamic-slice_bitcast_fusion.1
  92.4 2.6 fusion.17
  98.1 1.4 copy-done
  99.4 1.3 multiply_add_fusion.2
  100.8 2.0 copy-done.1
  108.3 11.5 %conditional.7 = (f32[1792,576]{0,1:T(8,128)}, f32[1,224,576]{2,1,0:T(8,128)S(1)}) conditional(s32[]{:T(128)} %convert_element_type.32, f32[1792,576]{0,1:T(8,128)} %get-tuple-element.560, (s32[1,224]{1,0:T(1,128)S(1)}, s32[224]{0:T(256)S(1)}, bf16[8,224,576]{2,1,0:T(8,128)(2,1)}, s32[]{:T(128)}, bf16[1792,576]{1,0:T(8,128)(2,1)}, ...), branch_computations={%region_11.11_spmd, %region_12.12_spmd} | conditional | flops 2215284736 | bytes 67317608 | solution.py:81
  108.5 1.0 dynamic-slice_bitcast_fusion.1
  109.5 2.6 fusion.17
  115.1 1.4 copy-done
  116.5 1.3 multiply_add_fusion.2
  117.8 2.0 copy-done.1
  119.8 0.9 constant_dynamic-update-slice_fusion.2
  125.4 11.5 %conditional.7 = (f32[1792,576]{0,1:T(8,128)}, f32[1,224,576]{2,1,0:T(8,128)S(1)}) conditional(s32[]{:T(128)} %convert_element_type.32, f32[1792,576]{0,1:T(8,128)} %get-tuple-element.560, (s32[1,224]{1,0:T(1,128)S(1)}, s32[224]{0:T(256)S(1)}, bf16[8,224,576]{2,1,0:T(8,128)(2,1)}, s32[]{:T(128)}, bf16[1792,576]{1,0:T(8,128)(2,1)}, ...), branch_computations={%region_11.11_spmd, %region_12.12_spmd} | conditional | flops 2215284736 | bytes 67317608 | solution.py:81
  125.6 1.0 dynamic-slice_bitcast_fusion.1
  126.6 2.6 fusion.17
  132.3 1.4 copy-done
  133.6 1.3 multiply_add_fusion.2
  135.0 2.0 copy-done.1
  139.7 11.5 %conditional.7 = (f32[1792,576]{0,1:T(8,128)}, f32[1,224,576]{2,1,0:T(8,128)S(1)}) conditional(s32[]{:T(128)} %convert_element_type.32, f32[1792,576]{0,1:T(8,128)} %get-tuple-element.560, (s32[1,224]{1,0:T(1,128)S(1)}, s32[224]{0:T(256)S(1)}, bf16[8,224,576]{2,1,0:T(8,128)(2,1)}, s32[]{:T(128)}, bf16[1792,576]{1,0:T(8,128)(2,1)}, ...), branch_computations={%region_11.11_spmd, %region_12.12_spmd} | conditional | flops 2215284736 | bytes 67317608 | solution.py:81
  139.9 1.0 dynamic-slice_bitcast_fusion.1
  140.9 2.6 fusion.17
  146.6 1.4 copy-done
  147.9 1.3 multiply_add_fusion.2
  149.3 2.0 copy-done.1
  154.0 11.5 %conditional.7 = (f32[1792,576]{0,1:T(8,128)}, f32[1,224,576]{2,1,0:T(8,128)S(1)}) conditional(s32[]{:T(128)} %convert_element_type.32, f32[1792,576]{0,1:T(8,128)} %get-tuple-element.560, (s32[1,224]{1,0:T(1,128)S(1)}, s32[224]{0:T(256)S(1)}, bf16[8,224,576]{2,1,0:T(8,128)(2,1)}, s32[]{:T(128)}, bf16[1792,576]{1,0:T(8,128)(2,1)}, ...), branch_computations={%region_11.11_spmd, %region_12.12_spmd} | conditional | flops 2215284736 | bytes 67317608 | solution.py:81
  154.2 1.0 dynamic-slice_bitcast_fusion.1
  155.2 2.6 fusion.17
  160.8 1.4 copy-done
  162.2 1.3 multiply_add_fusion.2
  163.5 2.0 copy-done.1
  168.3 11.5 %conditional.7 = (f32[1792,576]{0,1:T(8,128)}, f32[1,224,576]{2,1,0:T(8,128)S(1)}) conditional(s32[]{:T(128)} %convert_element_type.32, f32[1792,576]{0,1:T(8,128)} %get-tuple-element.560, (s32[1,224]{1,0:T(1,128)S(1)}, s32[224]{0:T(256)S(1)}, bf16[8,224,576]{2,1,0:T(8,128)(2,1)}, s32[]{:T(128)}, bf16[1792,576]{1,0:T(8,128)(2,1)}, ...), branch_computations={%region_11.11_spmd, %region_12.12_spmd} | conditional | flops 2215284736 | bytes 67317608 | solution.py:81
  168.5 1.0 dynamic-slice_bitcast_fusion.1
  169.5 2.6 fusion.17
  175.1 1.4 copy-done
  176.5 1.3 multiply_add_fusion.2
  177.8 2.0 copy-done.1
  180.7 86.2 %reduce-scatter.2.cloned.1.call-done = f32[224,576]{1,0:T(8,128)} async-done(((f32[1792,576]{1,0:T(8,128)}), f32[224,576]{1,0:T(8,128)}) %reduce-scatter.2.cloned.1.call-update) | async-done | bytes 516112 | tf_op jit(solution)/shard_map/reduce_scatter | solution.py:130
  266.9 2.4 convert_element_type.22
  269.3 2.6 copy.7
  271.8 36.4 %all-reduce.3.cloned.1.call-done = f32[224,576]{1,0:T(8,128)} async-done(((f32[224,576]{1,0:T(8,128)}), f32[224,576]{1,0:T(8,128)}) %all-reduce.3.cloned.1.call-update) | async-done | bytes 516112 | tf_op jit(solution)/shard_map/psum | solution.py:131
  308.2 1.9 copy.43
  (160 shorter events, 46.5 us)
Async XLA Ops:
  7.2 34.2 %all-gather.2.cloned.1.call-start = ((), (), s32[]{:S(2)}) async-start(), calls=%async_computation.1 | async-start | bytes 2580480 | tf_op jit(solution)/shard_map/all_gather | solution.py:127
  7.9 259.0 %reduce-scatter.2.cloned.1.call-start = ((), (), s32[]{:S(2)}) async-start(), calls=%async_computation.2 | async-start | bytes 5160960 | tf_op jit(solution)/shard_map/reduce_scatter | solution.py:130
  44.5 2.7 copy-start.2
  53.5 2.7 copy-start.2
  62.4 2.7 copy-start.2
  69.4 2.7 copy-start.2
  76.3 2.7 copy-start.2
  83.2 2.7 copy-start.2
  87.0 2.3 copy-start.3
  95.6 1.6 copy-start.4
  97.3 2.2 copy-start
  100.8 2.0 copy-start.1
  112.7 1.6 copy-start.4
  114.3 2.2 copy-start
  117.8 2.0 copy-start.1
  129.8 1.6 copy-start.4
  131.5 2.2 copy-start
  135.0 2.0 copy-start.1
  144.1 1.6 copy-start.4
  145.8 2.2 copy-start
  149.2 2.0 copy-start.1
  158.4 1.6 copy-start.4
  160.0 2.2 copy-start
  163.5 2.0 copy-start.1
  172.7 1.6 copy-start.4
  174.3 2.2 copy-start
  177.8 2.0 copy-start.1
  180.6 127.6 %all-reduce.3.cloned.1.call-start = ((), (), s32[]{:S(2)}) async-start(), calls=%async_computation.3 | async-start | bytes 1146880 | tf_op jit(solution)/shard_map/psum | solution.py:131
Sparse Core Ops, SparseCore 0:
  9.9 31.4 all-gather.1
  180.8 86.0 reduce-scatter.1
  269.2 38.9 all-reduce.2
where the time goes:
time: 318 us; the launch traced here: 317 us
  waiting for transfers between devices  155 us (49%)
  matrix products  57.1 us (18%)
  local copies, waits for them, and re-layouts  53.5 us (17%)
  loops' own time  21.1 us (7%)
  other arithmetic  16.2 us (5%)
  between operations  13.8 us (4%)
    reduce_scatter x1, waiting for transfers between devices, per_device(): lax.psum_scatter(grad_keys, 'ctx', scatter_dimension=0, tiled=True)  86.2 us
    psum x1, waiting for transfers between devices, per_device(): key_result = lax.psum(own_terms, 'head')  36.4 us
    dot_general x12, matrix products, block_scores(): jnp.dot(query_rows, key_block.T, preferred_element_type=jnp.float32)  31.5 us
    all_gather x1, waiting for transfers between devices, per_device(): lax.all_gather(keys, 'ctx', axis=0, tiled=True)  31.5 us
    cond x54, local copies, waits for them, and re-layouts  25.3 us
    squeeze x12, local copies, waits for them, and re-layouts, per_device(): carry, unused = lax.scan(first_visit, carry, (blocks, positions))  11.9 us
    another operation x1, loops' own time, per_device(): carry, unused = lax.scan(first_visit, carry, (blocks, positions))  10.2 us
    another operation x1, loops' own time, second_fold(): lax.scan(second_visit, grad_query, (blocks, positions))  9.89 us
  transfers between devices with their start and end apart: 3, of which 3 were waited for; matrix products, arithmetic and copies ran while one was open for 2% of the time, Pallas kernels for 0%

commit v1 on v0

v1 whole, which is shorter than its diff:
```python
import functools

import jax
import jax.numpy as jnp
from jax import lax
from jax.experimental import pallas as pl
from jax.experimental.pallas import tpu as pltpu
from jax.sharding import PartitionSpec as P

softmax_scale = 0.1352
masked_value = -1e30
log2_e = 1.4426950408889634
tile = 256
nt_dims = (((1,), (1,)), ((), ()))


def attention_kernel(
    ctx_size, block_rows, heads, order_ref, q_ref, do_ref, qt_ref, dot_ref, *rest
):
    key_refs = rest[:ctx_size]
    dq_ref, keep_ref, send_ref = rest[ctx_size : ctx_size + 3]
    keys, scores, gprobs, peak, total, weighted, dq_acc, dkt, stage, in_sem, keep_sem, send_sem = rest[
        ctx_size + 3 :
    ]
    seq, width = keys.shape
    latent = do_ref.shape[1]
    rows = block_rows * heads
    me = lax.axis_index("ctx")

    def position(mask, sub):
        return order_ref[2 * jnp.bitwise_xor(me, mask) + sub]

    def sorted_rows(mask, sub):
        start = pl.multiple_of(position(mask, sub) * block_rows, 16)
        return pl.ds(start, block_rows)

    loads = []
    for mask in range(ctx_size):
        for sub in range(2):
            copy = pltpu.make_async_copy(
                key_refs[mask].at[pl.ds(sub * block_rows, block_rows), :],
                keys.at[sorted_rows(mask, sub), :],
                in_sem.at[2 * mask + sub],
            )
            copy.start()
            loads.append(copy)
    dkt[...] = jnp.zeros_like(dkt)
    for copy in loads:
        copy.wait()

    def key_tile(j):
        return pl.ds(pl.multiple_of(j * tile, tile), tile)

    for b in range(2):
        place = position(0, b)
        span = pl.ds(b * rows, rows)
        count = ((place + 1) * block_rows + tile - 1) // tile
        peak[...] = jnp.full_like(peak, masked_value)
        row_pos = place * block_rows + lax.broadcasted_iota(jnp.int32, (rows, tile), 0) // heads

        @pl.loop(0, count)
        def _(j):
            block = keys[key_tile(j), :]
            s = lax.dot_general(q_ref[span, :], block, nt_dims, preferred_element_type=jnp.float32)
            key_pos = j * tile + lax.broadcasted_iota(jnp.int32, (rows, tile), 1)
            s = jnp.where(key_pos <= row_pos, s, masked_value)
            scores[j] = s
            peak[...] = jnp.maximum(peak[...], jnp.maximum(s[:, :128], s[:, 128:]))
            gprobs[j] = lax.dot_general(
                do_ref[span, :], block[:, :latent], nt_dims, preferred_element_type=jnp.float32
            )

        peak[...] = jnp.broadcast_to(jnp.max(peak[...], axis=1, keepdims=True), peak.shape)
        total[...] = jnp.zeros_like(total)
        weighted[...] = jnp.zeros_like(weighted)

        @pl.loop(0, count)
        def _(j):
            m = peak[...]
            for half in range(2):
                cols = slice(half * 128, half * 128 + 128)
                p = jnp.exp2((scores[j, :, cols] - m) * (softmax_scale * log2_e))
                scores[j, :, cols] = p
                total[...] += p
                weighted[...] += p * gprobs[j, :, cols]

        inverse = 1.0 / jnp.sum(total[...], axis=1, keepdims=True)
        delta = jnp.sum(weighted[...], axis=1, keepdims=True) * inverse
        total[...] = jnp.broadcast_to(inverse, total.shape)
        weighted[...] = jnp.broadcast_to(delta, weighted.shape)
        dq_acc[...] = jnp.zeros_like(dq_acc)

        @pl.loop(0, count)
        def _(j):
            inv = jnp.concatenate([total[...]] * 2, axis=1)
            dlt = jnp.concatenate([weighted[...]] * 2, axis=1)
            p = scores[j] * inv
            ds = (p * (gprobs[j] - dlt)).astype(jnp.bfloat16)
            ph = p.astype(jnp.bfloat16)
            dq_acc[...] += jnp.dot(ds, keys[key_tile(j), :], preferred_element_type=jnp.float32)
            dkt[j] += (
                jnp.dot(qt_ref[:, span], ds, preferred_element_type=jnp.float32) * softmax_scale
            )
            dkt[j, :latent, :] += jnp.dot(
                dot_ref[:, span], ph, preferred_element_type=jnp.float32
            )

        dq_ref[span, :] = (dq_acc[...] * softmax_scale).astype(jnp.bfloat16)

    @pl.loop(0, seq // tile)
    def _(j):
        stage[key_tile(j), :] = dkt[j].T

    copies = []
    for mask in range(ctx_size):
        for sub in range(2):
            out = keep_ref if mask % 2 == 0 else send_ref
            sem = keep_sem if mask % 2 == 0 else send_sem
            copy = pltpu.make_async_copy(
                stage.at[sorted_rows(mask, sub), :],
                out.at[mask // 2, pl.ds(sub * block_rows, block_rows), :],
                sem.at[2 * (mask // 2) + sub],
            )
            copy.start()
            copies.append(copy)
    for copy in copies:
        copy.wait()


def attention(order, q, do, qt, dot, key_list, ctx_size, block_rows, heads):
    total_rows, width = q.shape
    latent = do.shape[1]
    rows = block_rows * heads
    seq = 2 * block_rows * ctx_size
    half = ctx_size // 2
    tiles = seq // tile
    vmem = pl.BlockSpec(memory_space=pltpu.VMEM)
    anywhere = pl.BlockSpec(memory_space=pl.ANY)
    return pl.pallas_call(
        functools.partial(attention_kernel, ctx_size, block_rows, heads),
        out_shape=(
            jax.ShapeDtypeStruct((total_rows, width), jnp.bfloat16),
            jax.ShapeDtypeStruct((half, 2 * block_rows, width), jnp.float32),
            jax.ShapeDtypeStruct((half, 2 * block_rows, width), jnp.float32),
        ),
        in_specs=[pl.BlockSpec(memory_space=pltpu.SMEM)] + [vmem] * 4 + [anywhere] * ctx_size,
        out_specs=(vmem, anywhere, anywhere),
        scratch_shapes=[
            pltpu.VMEM((seq, width), jnp.bfloat16),
            pltpu.VMEM((tiles, rows, tile), jnp.float32),
            pltpu.VMEM((tiles, rows, tile), jnp.float32),
            pltpu.VMEM((rows, 128), jnp.float32),
            pltpu.VMEM((rows, 128), jnp.float32),
            pltpu.VMEM((rows, 128), jnp.float32),
            pltpu.VMEM((rows, width), jnp.float32),
            pltpu.VMEM((tiles, width, tile), jnp.float32),
            pltpu.VMEM((seq, width), jnp.float32),
            pltpu.SemaphoreType.DMA((2 * ctx_size,)),
            pltpu.SemaphoreType.DMA((ctx_size,)),
            pltpu.SemaphoreType.DMA((ctx_size,)),
        ],
        compiler_params=pltpu.CompilerParams(vmem_limit_bytes=62 * 1024 * 1024),
        name="attention_backward",
    )(order, q, do, qt, dot, *key_list)


def per_device(block_order, queries, keys, dout):
    token_count, head_count, key_width = queries.shape
    latent_width = dout.shape[2]
    block_rows = token_count // 2
    ctx_size = lax.axis_size("ctx")
    head_size = lax.axis_size("head")

    def swap(x, axis, mask):
        size = lax.axis_size(axis)
        return lax.ppermute(x, axis, [(i, i ^ mask) for i in range(size)])

    query_rows = queries.reshape(token_count * head_count, key_width)
    grad_rows = dout.reshape(token_count * head_count, latent_width)
    same_core = [keys] + [swap(keys, "ctx", mask) for mask in range(2, ctx_size, 2)]
    key_list = []
    for block in same_core:
        key_list += [block, swap(block, "ctx", 1)]
    grad_query, keep, send = attention(
        block_order,
        query_rows,
        grad_rows,
        query_rows.T,
        grad_rows.T,
        key_list,
        ctx_size,
        block_rows,
        head_count,
    )
    grad_queries = grad_query.reshape(token_count, head_count, key_width)
    sums = keep + swap(send.astype(jnp.bfloat16), "ctx", 1).astype(jnp.float32)
    own = sums[0]
    parts = [
        swap(sums[mask // 2].astype(jnp.bfloat16), "ctx", mask) for mask in range(2, ctx_size, 2)
    ]
    for part in parts:
        own = own + part.astype(jnp.float32)
    own = lax.optimization_barrier(own.astype(jnp.bfloat16))
    level = [own] + [swap(own, "head", mask) for mask in range(1, head_size)]
    level = [x.astype(jnp.float32) for x in level]
    while len(level) > 1:
        level = [level[i] + level[i + 1] for i in range(0, len(level), 2)]
    return (grad_queries, level[0])


def solution(mesh):
    placed = (P(), P("ctx", "head", None), P("ctx", None), P("ctx", "head", None))
    return jax.shard_map(
        per_device,
        mesh=mesh,
        in_specs=placed,
        out_specs=(P("ctx", "head", None), P("ctx", None)),
        check_vma=False,
    )
```

time: 318 us -> 116 us (0.36)
  waiting for transfers between devices: 155 us -> 51.7 us
  matrix products: 57.1 us -> 0 us
  local copies, waits for them, and re-layouts: 53.5 us -> 7.63 us
  Pallas kernels: 0 us -> 32.3 us
  loops' own time: 21.1 us -> 0 us
  starting transfers between devices: 0.12 us -> 19.1 us
  between operations: 13.8 us -> 0.74 us
  other arithmetic: 16.2 us -> 3.28 us
    reduce_scatter x1 -> x0, waiting for transfers between devices: 86.2 us -> none  [per_device(): lax.psum_scatter(grad_keys, 'ctx', scatter_dimension=0, tiled=True)]
    dot_general x42 -> x0, matrix products: 57.1 us -> none  [the longest x12 31.5 us: block_scores(): jnp.dot(query_rows, key_block.T, preferred_element_type=jnp.float32)]
    ppermute x0 -> x14, waiting for transfers between devices: none -> 51.7 us  [swap(): return lax.ppermute(x, axis, [(i, i ^ mask) for i in range(size)])]
    psum x1 -> x0, waiting for transfers between devices: 36.4 us -> none  [per_device(): key_result = lax.psum(own_terms, 'head')]
    pallas_call x0 -> x1, Pallas kernels: none -> 32.3 us  [attention(): pl.pallas_call(functools.partial(attention_kernel, ctx_size, block_rows,...]
    all_gather x1 -> x0, waiting for transfers between devices: 31.5 us -> none  [per_device(): lax.all_gather(keys, 'ctx', axis=0, tiled=True)]
    cond x54 -> x0, local copies, waits for them, and re-layouts: 25.3 us -> none
    another operation x18 -> x0, loops' own time: 21.1 us -> none  [the longest x1 10.2 us: per_device(): carry, unused = lax.scan(first_visit, carry, (blocks, positions))]
  transfers between devices with their start and end apart: 3 -> 14, of which waited for: 3 -> 9; matrix products, arithmetic and copies ran while one was open for 2% -> 6% of each run, Pallas kernels for 0% -> 0%
where the time goes in v1:
time: 116 us; the launch traced here: 115 us
  waiting for transfers between devices  51.7 us (45%)
  Pallas kernels  32.3 us (28%)
  starting transfers between devices  19.1 us (16%)
  local copies, waits for them, and re-layouts  7.63 us (7%)
  other arithmetic  3.28 us (3%)
    ppermute x14, waiting for transfers between devices, swap(): return lax.ppermute(x, axis, [(i, i ^ mask) for i in range(size)])  51.7 us
    pallas_call x1, Pallas kernels, attention(): pl.pallas_call(functools.partial(attention_kernel, ctx_size, block_rows,...  32.3 us
    ppermute x14, starting transfers between devices, swap(): return lax.ppermute(x, axis, [(i, i ^ mask) for i in range(size)])  19.1 us
    reshape x1, local copies, waits for them, and re-layouts, per_device(): grad_rows = dout.reshape(token_count * head_count, latent_width)  3.96 us
    reshape x1, local copies, waits for them, and re-layouts, per_device(): query_rows = queries.reshape(token_count * head_count, key_width)  2.89 us
  transfers between devices with their start and end apart: 14, of which 9 were waited for; matrix products, arithmetic and copies ran while one was open for 6% of the time, Pallas kernels for 0%

profile of v1, /device:TPU:0, one launch (start us, length us, event | category | flops | bytes accessed | tf_op | source)
XLA Modules:
  0.0 114.8 jit_solution(2117157607275428644)
XLA Ops:
  0.6 0.0 copy-start
  0.6 3.0 %collective-permute-start.3 = (bf16[224,576]{1,0:T(8,128)(2,1)}, bf16[224,576]{1,0:T(8,128)(2,1)S(1)}, u32[]{:S(2)}, u32[]{:S(2)}) collective-permute-start(bf16[224,576]{1,0:T(8,128)(2,1)} %rest_0_.1), channel_id=1, source_target_pairs={{0,16},{4,20},{8,24},{12,28},{16,0},{20,4},{24,8},{28,12},{1,17},{... | collective-permute-start | bytes 774152 | tf_op jit(solution)/shard_map/ppermute | solution.py:176
  3.7 1.5 %collective-permute-start.1 = (bf16[224,576]{1,0:T(8,128)(2,1)}, bf16[224,576]{1,0:T(8,128)(2,1)S(1)}, u32[]{:S(2)}, u32[]{:S(2)}) collective-permute-start(bf16[224,576]{1,0:T(8,128)(2,1)} %rest_0_.1), channel_id=1, source_target_pairs={{0,8},{4,12},{8,0},{12,4},{16,24},{20,28},{24,16},{28,20},{1,9},{5... | collective-permute-start | bytes 774152 | tf_op jit(solution)/shard_map/ppermute | solution.py:176
  5.2 0.1 collective-permute-start.5
  5.2 0.0 collective-permute-start
  5.2 5.5 %collective-permute-done.3.rest_4_ = bf16[224,576]{1,0:T(8,128)(2,1)S(1)} collective-permute-done((bf16[224,576]{1,0:T(8,128)(2,1)}, bf16[224,576]{1,0:T(8,128)(2,1)S(1)}, u32[]{:S(2)}, u32[]{:S(2)}) %collective-permute-start.3) | collective-permute-done | bytes 258080 | tf_op jit(solution)/shard_map/ppermute | solution.py:176
  10.7 0.0 copy-start.2
  10.7 0.0 collective-permute-start.4
  10.7 2.9 %collective-permute-done.1.rest_2_ = bf16[224,576]{1,0:T(8,128)(2,1)S(1)} collective-permute-done((bf16[224,576]{1,0:T(8,128)(2,1)}, bf16[224,576]{1,0:T(8,128)(2,1)S(1)}, u32[]{:S(2)}, u32[]{:S(2)}) %collective-permute-start.1) | collective-permute-done | bytes 258080 | tf_op jit(solution)/shard_map/ppermute | solution.py:176
  13.6 0.0 copy-start.3
  13.6 0.0 collective-permute-start.2
  13.6 4.5 %collective-permute-done.5.rest_6_ = bf16[224,576]{1,0:T(8,128)(2,1)S(1)} collective-permute-done((bf16[224,576]{1,0:T(8,128)(2,1)}, bf16[224,576]{1,0:T(8,128)(2,1)S(1)}, u32[]{:S(2)}, u32[]{:S(2)}) %collective-permute-start.5) | collective-permute-done | bytes 258080 | tf_op jit(solution)/shard_map/ppermute | solution.py:176
  18.1 0.0 copy-start.4
  18.1 0.0 collective-permute-start.6
  18.1 4.0 %copy.11 = bf16[1792,512]{0,1:T(8,128)(2,1)} copy(bf16[1792,512]{1,0:T(8,128)(2,1)} %bitcast.24) | data formatting | bytes 3670016 | tf_op jit(solution)/shard_map/reshape | solution.py:179
  22.1 0.0 copy-done
  22.1 2.9 %copy.10 = bf16[1792,576]{0,1:T(8,128)(2,1)} copy(bf16[1792,576]{1,0:T(8,128)(2,1)S(1)} %bitcast.22) | data formatting | bytes 4128768 | tf_op jit(solution)/shard_map/reshape | solution.py:178
  25.0 0.0 copy-done.2
  25.0 0.0 copy-done.3
  25.0 0.0 copy-done.4
  25.0 0.0 collective-permute-done.rest_1_
  25.0 0.0 copy-start.5
  25.0 0.0 collective-permute-done.4.rest_5_
  25.0 0.0 collective-permute-done.2.rest_3_
  25.0 0.0 collective-permute-done.6.rest_7_
  25.0 0.7 copy-done.5
  25.7 32.3 %attention_backward.1 = (bf16[1792,576]{1,0:T(8,128)(2,1)}, f32[4,224,576]{2,1,0:T(8,128)}, f32[4,224,576]{2,1,0:T(8,128)}) custom-call(s32[16]{0:T(128)} %order_ref.1, bf16[1792,576]{1,0:T(8,128)(2,1)} %bitcast.21, bf16[1792,512]{1,0:T(8,128)(2,1)} %bitcast.25, bf16[576,1792]{1,0:T(8,128)(2,1)} %bitcast.23, bf16[512,1792]{1,0:T(8,128)(2,1)} %bitcast.26, ...), custom_call_target="tpu_custom_call" | custom-call | tf_op jit(solution)/shard_map/attention_backward/pallas_call | solution.py:139
  58.1 0.0 copy-start.1
  58.1 1.9 %convert_element_type.42 = bf16[4,224,576]{2,1,0:T(8,128)(2,1)S(1)} convert(f32[4,224,576]{2,1,0:T(8,128)} %get-tuple-element.7) | non-fusion elementwise | flops 516096 | bytes 3096576 | tf_op jit(solution)/shard_map/convert_element_type | solution.py:196
  60.0 0.1 collective-permute-start.7
  60.1 2.8 %collective-permute-done.7 = bf16[4,224,576]{2,1,0:T(8,128)(2,1)S(1)} collective-permute-done((bf16[4,224,576]{2,1,0:T(8,128)(2,1)S(1)}, bf16[4,224,576]{2,1,0:T(8,128)(2,1)S(1)}, u32[]{:S(2)}, u32[]{:S(2)}) %collective-permute-start.7) | collective-permute-done | bytes 1032224 | tf_op jit(solution)/shard_map/ppermute | solution.py:176
  62.9 0.0 copy-done.1
  62.9 0.3 fusion.4
  63.1 0.1 slice_bitcast_fusion.3
  63.2 8.5 %collective-permute-start.8 = (bf16[224,576]{1,0:T(8,128)(2,1)S(1)}, bf16[224,576]{1,0:T(8,128)(2,1)S(1)}, u32[]{:S(2)}, u32[]{:S(2)}) collective-permute-start(bf16[224,576]{1,0:T(8,128)(2,1)S(1)} %get-tuple-element.10), channel_id=1, source_target_pairs={{0,8},{4,12},{8,0},{12,4},{16,24},{20,28},{24,16},{28,20},{1,9},{5... | collective-permute-start | bytes 774152 | tf_op jit(solution)/shard_map/ppermute | solution.py:176
  71.7 0.0 collective-permute-start.10
  71.7 1.5 %collective-permute-start.9 = (bf16[224,576]{1,0:T(8,128)(2,1)S(1)}, bf16[224,576]{1,0:T(8,128)(2,1)S(1)}, u32[]{:S(2)}, u32[]{:S(2)}) collective-permute-start(bf16[224,576]{1,0:T(8,128)(2,1)S(1)} %get-tuple-element.12), channel_id=1, source_target_pairs={{0,16},{4,20},{8,24},{12,28},{16,0},{20,4},{24,8},{28,12},{1,17},{... | collective-permute-start | bytes 774152 | tf_op jit(solution)/shard_map/ppermute | solution.py:176
  73.2 6.1 %collective-permute-done.8 = bf16[224,576]{1,0:T(8,128)(2,1)S(1)} collective-permute-done((bf16[224,576]{1,0:T(8,128)(2,1)S(1)}, bf16[224,576]{1,0:T(8,128)(2,1)S(1)}, u32[]{:S(2)}, u32[]{:S(2)}) %collective-permute-start.8) | collective-permute-done | bytes 258080 | tf_op jit(solution)/shard_map/ppermute | solution.py:176
  79.3 5.0 %collective-permute-done.10 = bf16[224,576]{1,0:T(8,128)(2,1)S(1)} collective-permute-done((bf16[224,576]{1,0:T(8,128)(2,1)S(1)}, bf16[224,576]{1,0:T(8,128)(2,1)S(1)}, u32[]{:S(2)}, u32[]{:S(2)}) %collective-permute-start.10) | collective-permute-done | bytes 258080 | tf_op jit(solution)/shard_map/ppermute | solution.py:176
  84.3 2.2 %collective-permute-done.9 = bf16[224,576]{1,0:T(8,128)(2,1)S(1)} collective-permute-done((bf16[224,576]{1,0:T(8,128)(2,1)S(1)}, bf16[224,576]{1,0:T(8,128)(2,1)S(1)}, u32[]{:S(2)}, u32[]{:S(2)}) %collective-permute-start.9) | collective-permute-done | bytes 258080 | tf_op jit(solution)/shard_map/ppermute | solution.py:176
  86.4 0.2 fusion.3
  86.6 3.7 %collective-permute-start.13 = (bf16[224,576]{1,0:T(8,128)(2,1)S(1)}, bf16[224,576]{1,0:T(8,128)(2,1)S(1)}, u32[]{:S(2)}, u32[]{:S(2)}) collective-permute-start(bf16[224,576]{1,0:T(8,128)(2,1)S(1)} %fusion.3), channel_id=1, source_target_pairs={{0,3},{1,2},{2,1},{3,0},{4,7},{5,6},{6,5},{7,4},{8,11},{9,10},{10,... | collective-permute-start | bytes 774152 | tf_op jit(solution)/shard_map/ppermute | solution.py:176
  90.2 0.0 collective-permute-start.12
  90.2 0.8 collective-permute-start.11
  91.0 7.3 %collective-permute-done.13 = bf16[224,576]{1,0:T(8,128)(2,1)S(1)} collective-permute-done((bf16[224,576]{1,0:T(8,128)(2,1)S(1)}, bf16[224,576]{1,0:T(8,128)(2,1)S(1)}, u32[]{:S(2)}, u32[]{:S(2)}) %collective-permute-start.13) | collective-permute-done | bytes 258080 | tf_op jit(solution)/shard_map/ppermute | solution.py:176
  98.3 15.5 %collective-permute-done.12 = bf16[224,576]{1,0:T(8,128)(2,1)S(1)} collective-permute-done((bf16[224,576]{1,0:T(8,128)(2,1)S(1)}, bf16[224,576]{1,0:T(8,128)(2,1)S(1)}, u32[]{:S(2)}, u32[]{:S(2)}) %collective-permute-start.12) | collective-permute-done | bytes 258080 | tf_op jit(solution)/shard_map/ppermute | solution.py:176
  113.8 0.0 collective-permute-done.11
  113.8 0.9 add_add_fusion
Async XLA Ops:
  0.6 21.5 %copy-start = (bf16[224,8,576]{2,1,0:T(8,128)(2,1)S(1)}, bf16[224,8,576]{2,1,0:T(8,128)(2,1)}, u32[]{:S(2)}) copy-start(bf16[224,8,576]{2,1,0:T(8,128)(2,1)} %param.5) | copy-start | bytes 6193156
  0.6 10.1 %collective-permute-start.3 = (bf16[224,576]{1,0:T(8,128)(2,1)}, bf16[224,576]{1,0:T(8,128)(2,1)S(1)}, u32[]{:S(2)}, u32[]{:S(2)}) collective-permute-start(bf16[224,576]{1,0:T(8,128)(2,1)} %rest_0_.1), channel_id=1, source_target_pairs={{0,16},{4,20},{8,24},{12,28},{16,0},{20,4},{24,8},{28,12},{1,17},{... | collective-permute-start | bytes 774152 | tf_op jit(solution)/shard_map/ppermute | solution.py:176
  3.7 10.0 %collective-permute-start.1 = (bf16[224,576]{1,0:T(8,128)(2,1)}, bf16[224,576]{1,0:T(8,128)(2,1)S(1)}, u32[]{:S(2)}, u32[]{:S(2)}) collective-permute-start(bf16[224,576]{1,0:T(8,128)(2,1)} %rest_0_.1), channel_id=1, source_target_pairs={{0,8},{4,12},{8,0},{12,4},{16,24},{20,28},{24,16},{28,20},{1,9},{5... | collective-permute-start | bytes 774152 | tf_op jit(solution)/shard_map/ppermute | solution.py:176
  5.2 13.0 %collective-permute-start.5 = (bf16[224,576]{1,0:T(8,128)(2,1)}, bf16[224,576]{1,0:T(8,128)(2,1)S(1)}, u32[]{:S(2)}, u32[]{:S(2)}) collective-permute-start(bf16[224,576]{1,0:T(8,128)(2,1)} %rest_0_.1), channel_id=1, source_target_pairs={{0,24},{4,28},{8,16},{12,20},{16,8},{20,12},{24,0},{28,4},{1,25},{... | collective-permute-start | bytes 774152 | tf_op jit(solution)/shard_map/ppermute | solution.py:176
  5.2 19.8 %collective-permute-start = (bf16[224,576]{1,0:T(8,128)(2,1)}, bf16[224,576]{1,0:T(8,128)(2,1)S(1)}, u32[]{:S(2)}, u32[]{:S(2)}) collective-permute-start(bf16[224,576]{1,0:T(8,128)(2,1)} %rest_0_.1), channel_id=1, source_target_pairs={{0,4},{4,0},{8,12},{12,8},{16,20},{20,16},{24,28},{28,24},{1,5},{5... | collective-permute-start | bytes 774152 | tf_op jit(solution)/shard_map/ppermute | solution.py:176
  10.7 14.3 %copy-start.2 = (bf16[224,576]{1,0:T(8,128)(2,1)}, bf16[224,576]{1,0:T(8,128)(2,1)S(1)}, u32[]{:S(2)}) copy-start(bf16[224,576]{1,0:T(8,128)(2,1)S(1)} %collective-permute-done.3.rest_4_) | copy-start | bytes 774148
  10.7 14.3 %collective-permute-start.4 = (bf16[224,576]{1,0:T(8,128)(2,1)S(1)}, bf16[224,576]{1,0:T(8,128)(2,1)}, u32[]{:S(2)}, u32[]{:S(2)}) collective-permute-start(bf16[224,576]{1,0:T(8,128)(2,1)S(1)} %collective-permute-done.3.rest_4_), channel_id=1, source_target_pairs={{0,4},{4,0},{8,12},{12,8},{16,20},{20,16},{24,28},{28,24},{1,5},{5... | collective-permute-start | bytes 774152 | tf_op jit(solution)/shard_map/ppermute | solution.py:176
  13.6 11.3 %copy-start.3 = (bf16[224,576]{1,0:T(8,128)(2,1)}, bf16[224,576]{1,0:T(8,128)(2,1)S(1)}, u32[]{:S(2)}) copy-start(bf16[224,576]{1,0:T(8,128)(2,1)S(1)} %collective-permute-done.1.rest_2_) | copy-start | bytes 774148
  13.6 11.4 %collective-permute-start.2 = (bf16[224,576]{1,0:T(8,128)(2,1)S(1)}, bf16[224,576]{1,0:T(8,128)(2,1)}, u32[]{:S(2)}, u32[]{:S(2)}) collective-permute-start(bf16[224,576]{1,0:T(8,128)(2,1)S(1)} %collective-permute-done.1.rest_2_), channel_id=1, source_target_pairs={{0,4},{4,0},{8,12},{12,8},{16,20},{20,16},{24,28},{28,24},{1,5},{5... | collective-permute-start | bytes 774152 | tf_op jit(solution)/shard_map/ppermute | solution.py:176
  18.1 6.9 %copy-start.4 = (bf16[224,576]{1,0:T(8,128)(2,1)}, bf16[224,576]{1,0:T(8,128)(2,1)S(1)}, u32[]{:S(2)}) copy-start(bf16[224,576]{1,0:T(8,128)(2,1)S(1)} %collective-permute-done.5.rest_6_) | copy-start | bytes 774148
  18.1 6.9 %collective-permute-start.6 = (bf16[224,576]{1,0:T(8,128)(2,1)S(1)}, bf16[224,576]{1,0:T(8,128)(2,1)}, u32[]{:S(2)}, u32[]{:S(2)}) collective-permute-start(bf16[224,576]{1,0:T(8,128)(2,1)S(1)} %collective-permute-done.5.rest_6_), channel_id=1, source_target_pairs={{0,4},{4,0},{8,12},{12,8},{16,20},{20,16},{24,28},{28,24},{1,5},{5... | collective-permute-start | bytes 774152 | tf_op jit(solution)/shard_map/ppermute | solution.py:176
  25.0 0.7 copy-start.5
  58.1 4.8 %copy-start.1 = (f32[4,224,576]{2,1,0:T(8,128)S(1)}, f32[4,224,576]{2,1,0:T(8,128)}, u32[]{:S(2)}) copy-start(f32[4,224,576]{2,1,0:T(8,128)} %get-tuple-element.6) | copy-start | bytes 6193156
  60.0 2.9 %collective-permute-start.7 = (bf16[4,224,576]{2,1,0:T(8,128)(2,1)S(1)}, bf16[4,224,576]{2,1,0:T(8,128)(2,1)S(1)}, u32[]{:S(2)}, u32[]{:S(2)}) collective-permute-start(bf16[4,224,576]{2,1,0:T(8,128)(2,1)S(1)} %convert_element_type.42), channel_id=1, source_target_pairs={{0,4},{4,0},{8,12},{12,8},{16,20},{20,16},{24,28},{28,24},{1,5},{5... | collective-permute-start | bytes 3096584 | tf_op jit(solution)/shard_map/ppermute | solution.py:176
  63.2 16.1 %collective-permute-start.8 = (bf16[224,576]{1,0:T(8,128)(2,1)S(1)}, bf16[224,576]{1,0:T(8,128)(2,1)S(1)}, u32[]{:S(2)}, u32[]{:S(2)}) collective-permute-start(bf16[224,576]{1,0:T(8,128)(2,1)S(1)} %get-tuple-element.10), channel_id=1, source_target_pairs={{0,8},{4,12},{8,0},{12,4},{16,24},{20,28},{24,16},{28,20},{1,9},{5... | collective-permute-start | bytes 774152 | tf_op jit(solution)/shard_map/ppermute | solution.py:176
  71.7 12.6 %collective-permute-start.10 = (bf16[224,576]{1,0:T(8,128)(2,1)S(1)}, bf16[224,576]{1,0:T(8,128)(2,1)S(1)}, u32[]{:S(2)}, u32[]{:S(2)}) collective-permute-start(bf16[224,576]{1,0:T(8,128)(2,1)S(1)} %get-tuple-element.11), channel_id=1, source_target_pairs={{0,24},{4,28},{8,16},{12,20},{16,8},{20,12},{24,0},{28,4},{1,25},{... | collective-permute-start | bytes 774152 | tf_op jit(solution)/shard_map/ppermute | solution.py:176
  71.7 14.7 %collective-permute-start.9 = (bf16[224,576]{1,0:T(8,128)(2,1)S(1)}, bf16[224,576]{1,0:T(8,128)(2,1)S(1)}, u32[]{:S(2)}, u32[]{:S(2)}) collective-permute-start(bf16[224,576]{1,0:T(8,128)(2,1)S(1)} %get-tuple-element.12), channel_id=1, source_target_pairs={{0,16},{4,20},{8,24},{12,28},{16,0},{20,4},{24,8},{28,12},{1,17},{... | collective-permute-start | bytes 774152 | tf_op jit(solution)/shard_map/ppermute | solution.py:176
  86.6 11.7 %collective-permute-start.13 = (bf16[224,576]{1,0:T(8,128)(2,1)S(1)}, bf16[224,576]{1,0:T(8,128)(2,1)S(1)}, u32[]{:S(2)}, u32[]{:S(2)}) collective-permute-start(bf16[224,576]{1,0:T(8,128)(2,1)S(1)} %fusion.3), channel_id=1, source_target_pairs={{0,3},{1,2},{2,1},{3,0},{4,7},{5,6},{6,5},{7,4},{8,11},{9,10},{10,... | collective-permute-start | bytes 774152 | tf_op jit(solution)/shard_map/ppermute | solution.py:176
  90.2 23.6 %collective-permute-start.12 = (bf16[224,576]{1,0:T(8,128)(2,1)S(1)}, bf16[224,576]{1,0:T(8,128)(2,1)S(1)}, u32[]{:S(2)}, u32[]{:S(2)}) collective-permute-start(bf16[224,576]{1,0:T(8,128)(2,1)S(1)} %fusion.3), channel_id=1, source_target_pairs={{0,2},{1,3},{2,0},{3,1},{4,6},{5,7},{6,4},{7,5},{8,10},{9,11},{10,... | collective-permute-start | bytes 774152 | tf_op jit(solution)/shard_map/ppermute | solution.py:176
  90.2 23.6 %collective-permute-start.11 = (bf16[224,576]{1,0:T(8,128)(2,1)S(1)}, bf16[224,576]{1,0:T(8,128)(2,1)S(1)}, u32[]{:S(2)}, u32[]{:S(2)}) collective-permute-start(bf16[224,576]{1,0:T(8,128)(2,1)S(1)} %fusion.3), channel_id=1, source_target_pairs={{0,1},{1,0},{2,3},{3,2},{4,5},{5,4},{6,7},{7,6},{8,9},{9,8},{10,11... | collective-permute-start | bytes 774152 | tf_op jit(solution)/shard_map/ppermute | solution.py:176

commit v2 on v0

v2 whole, which is shorter than its diff:
```python
import functools

import jax
import jax.numpy as jnp
from jax import lax
from jax.experimental import pallas as pl
from jax.experimental.pallas import tpu as pltpu
from jax.sharding import PartitionSpec as P

softmax_scale = 0.1352
masked_value = -1e30
log2_e = 1.4426950408889634
tile = 256
lanes = 128
mebibyte = 1024 * 1024
nt_dims = (((1,), (1,)), ((), ()))


def padded(width):
    return -(-width // lanes) * lanes


def chip_axes(core, ctx_size):
    bits = ctx_size.bit_length() - 2
    return [2 << (t + core) % bits for t in range(bits)]


def chip_mask(label, core, ctx_size):
    return sum(axis for t, axis in enumerate(chip_axes(core, ctx_size)) if label >> t & 1)


def layout_kernel(rows, q_ref, do_ref, qp_ref, qt_ref, dot_ref):
    width = q_ref.shape[1]
    qp_ref[:, :width] = q_ref[...]
    qp_ref[:, width:] = jnp.zeros((qp_ref.shape[0], qp_ref.shape[1] - width), qp_ref.dtype)
    for b in range(2):
        span = slice(b * rows, b * rows + rows)
        qt_ref[b] = q_ref[span, :].T
        dot_ref[b] = do_ref[span, :].T


def attention_kernel(direct, ctx_size, block_rows, heads, latent, width, order_ref, *rest):
    q, do, qt, dot = rest[:4]
    key_refs = rest[4 : 4 + ctx_size]
    dq_ref, keep_ref, send_ref = rest[4 + ctx_size : 7 + ctx_size]
    (keys, stage, probs, gprobs, marks, peak, total, weighted, dq_acc, dkt, move_sem) = rest[7 + ctx_size :]
    seq = keys.shape[0]
    tiles = seq // tile
    rows = block_rows * heads
    me = lax.axis_index("ctx")

    def sorted_rows(mask, sub):
        position = order_ref[2 * jnp.bitwise_xor(me, mask) + sub]
        return pl.ds(pl.multiple_of(position * block_rows, 16), block_rows)

    def move(pairs):
        if direct:
            for source, target in pairs:
                target[...] = source[...]
            return
        copies = [
            pltpu.make_async_copy(source, target, move_sem.at[i])
            for i, (source, target) in enumerate(pairs)
        ]
        for copy in copies:
            copy.start()
        for copy in copies:
            copy.wait()

    blocks = [(mask, sub) for mask in range(ctx_size) for sub in range(2)]

    def sub_rows(sub):
        return pl.ds(sub * block_rows, block_rows)

    move(
        [
            (key_refs[mask].at[sub_rows(sub), :], keys.at[sorted_rows(mask, sub), :])
            for mask, sub in blocks
        ]
    )

    first = jnp.where(order_ref[2 * me] < order_ref[2 * me + 1], 0, 1)
    order = (first, 1 - first)
    places = [order_ref[2 * me + b] for b in order]
    counts = [((place + 1) * block_rows + tile - 1) // tile for place in places]

    @pl.loop(counts[0], counts[1])
    def _(j):
        dkt[j] = jnp.zeros(dkt.shape[1:], dkt.dtype)


    def key_rows(j, count):
        return pl.ds(pl.multiple_of(j * tile, tile), count * tile)

    def visits(count, visit):
        @pl.loop(0, count // 2)
        def _(i):
            visit(2 * i, 2)

        @pl.when(count % 2 == 1)
        def _():
            visit(count - 1, 1)

    def piece(h):
        return slice(h % 2 * lanes, h % 2 * lanes + lanes)

    for turn in range(2):
        b, place = order[turn], places[turn]
        span = pl.ds(pl.multiple_of(b * rows, rows), rows)
        peak[...] = jnp.full_like(peak, masked_value)
        total[...] = jnp.zeros_like(total)
        weighted[...] = jnp.zeros_like(weighted)

        def score_visit(j, n):
            block = keys[key_rows(j, n), :]
            s = lax.dot_general(q[span, :], block, nt_dims, preferred_element_type=jnp.float32)
            g = lax.dot_general(
                do[span, :], block[:, :latent], nt_dims, preferred_element_type=jnp.float32
            )
            row_pos = (
                place * block_rows
                - j * tile
                + lax.broadcasted_iota(jnp.int32, (rows, lanes), 0) // heads
            )
            col = lax.broadcasted_iota(jnp.int32, (rows, lanes), 1)
            parts = []
            for h in range(2 * n):
                u = s[:, h * lanes : h * lanes + lanes] * (softmax_scale * log2_e)
                parts.append(jnp.where(col + h * lanes <= row_pos, u, masked_value))
            old = peak[...]
            m = functools.reduce(jnp.maximum, parts, old)
            alpha = jnp.exp2(old - m)
            acc = total[...] * alpha
            wacc = weighted[...] * alpha
            for h in range(2 * n):
                p = jnp.exp2(parts[h] - m)
                gh = g[:, h * lanes : h * lanes + lanes]
                probs[j + h // 2, :, piece(h)] = p
                gprobs[j + h // 2, :, piece(h)] = gh
                acc += p
                wacc += p * gh
            peak[...] = m
            marks[j // 2] = m
            total[...] = acc
            weighted[...] = wacc

        visits(counts[turn], score_visit)

        top = jnp.max(peak[...], axis=1, keepdims=True)
        share = jnp.exp2(peak[...] - top)
        inverse = 1.0 / jnp.sum(total[...] * share, axis=1, keepdims=True)
        delta = jnp.sum(weighted[...] * share, axis=1, keepdims=True) * inverse
        peak[...] = jnp.broadcast_to(top, peak.shape)
        total[...] = jnp.broadcast_to(inverse, total.shape)
        weighted[...] = jnp.broadcast_to(delta, weighted.shape)
        dq_acc[...] = jnp.zeros_like(dq_acc)

        def grad_visit(j, n):
            factor = jnp.exp2(marks[j // 2] - peak[...]) * total[...]
            delta = weighted[...]
            halves, grads = [], []
            for h in range(2 * n):
                p = probs[j + h // 2, :, piece(h)] * factor
                g = gprobs[j + h // 2, :, piece(h)]
                halves.append(p.astype(jnp.bfloat16))
                grads.append((p * (g - delta)).astype(jnp.bfloat16))
            ds = jnp.concatenate(grads, axis=1)
            ph = jnp.concatenate(halves, axis=1)
            dq_acc[...] += jnp.dot(
                ds, keys[key_rows(j, n), :], preferred_element_type=jnp.float32
            )
            kt = jnp.dot(qt[b], ds, preferred_element_type=jnp.float32) * softmax_scale
            vt = jnp.dot(dot[b], ph, preferred_element_type=jnp.float32)
            for t in range(n):
                cols = slice(t * tile, t * tile + tile)
                low = kt[:latent, cols] + vt[:, cols]
                high = kt[latent:, cols]
                if turn == 0:
                    dkt[j + t, :latent, :] = low
                    dkt[j + t, latent:, :] = high
                else:
                    low = low + dkt[j + t, :latent, :]
                    high = high + dkt[j + t, latent:, :]
                    stage[key_rows(j + t, 1), :latent] = low.T.astype(jnp.bfloat16)
                    stage[key_rows(j + t, 1), latent:width] = high.T.astype(jnp.bfloat16)
                    stage[key_rows(j + t, 1), width:] = jnp.zeros(
                        (tile, stage.shape[1] - width), stage.dtype
                    )

        visits(counts[turn], grad_visit)
        dq_ref[span, :] = (dq_acc[:, :width] * softmax_scale).astype(jnp.bfloat16)

    @pl.loop(counts[1], tiles)
    def _(j):
        stage[key_rows(j, 1), :] = jnp.zeros((tile, stage.shape[1]), stage.dtype)

    core = me % 2
    leaving = []
    for label in range(ctx_size // 2):
        masks = [chip_mask(label, c, ctx_size) for c in range(2)]
        kept = jnp.where(core == 0, masks[0], masks[1])
        sent = jnp.where(core == 0, masks[1], masks[0]) + 1
        for mask, out in ((kept, keep_ref), (sent, send_ref)):
            for sub in range(2):
                source = stage.at[sorted_rows(mask, sub), :]
                leaving.append((source, out.at[label, sub_rows(sub), :]))
    move(leaving)


def row_layouts(q, do, rows):
    total_rows, width = q.shape
    latent = do.shape[1]
    vmem = pl.BlockSpec(memory_space=pltpu.VMEM)
    return pl.pallas_call(
        functools.partial(layout_kernel, rows),
        out_shape=(
            jax.ShapeDtypeStruct((total_rows, padded(width)), q.dtype),
            jax.ShapeDtypeStruct((2, width, rows), q.dtype),
            jax.ShapeDtypeStruct((2, latent, rows), q.dtype),
        ),
        in_specs=[vmem] * 2,
        out_specs=(vmem,) * 3,
        compiler_params=pltpu.CompilerParams(vmem_limit_bytes=24 * mebibyte),
        name="row_layouts",
    )(q, do)


def attention(order, qp, do, qt, dot, key_list, block_rows, heads, width):
    ctx_size = len(key_list)
    total_rows = qp.shape[0]
    latent = do.shape[1]
    rows = block_rows * heads
    seq = 2 * block_rows * ctx_size
    half = ctx_size // 2
    tiles = seq // tile
    vmem = pl.BlockSpec(memory_space=pltpu.VMEM)
    f32, bf16 = jnp.float32, jnp.bfloat16
    buffers = [
        ((seq, padded(width)), bf16),
        ((seq, padded(width)), bf16),
        ((tiles, rows, tile), f32),
        ((tiles, rows, tile), f32),
        (((tiles + 1) // 2, rows, lanes), f32),
        ((rows, lanes), f32),
        ((rows, lanes), f32),
        ((rows, lanes), f32),
        ((rows, padded(width)), f32),
        ((tiles, width, tile), f32),
    ]
    direct = seq <= 2048
    blocks = vmem if direct else pl.BlockSpec(memory_space=pl.ANY)
    limit = 42 if direct else 63
    return pl.pallas_call(
        functools.partial(attention_kernel, direct, ctx_size, block_rows, heads, latent, width),
        out_shape=(
            jax.ShapeDtypeStruct((total_rows, width), bf16),
            jax.ShapeDtypeStruct((half, 2 * block_rows, padded(width)), bf16),
            jax.ShapeDtypeStruct((half, 2 * block_rows, padded(width)), bf16),
        ),
        in_specs=[pl.BlockSpec(memory_space=pltpu.SMEM)] + [vmem] * 4 + [blocks] * ctx_size,
        out_specs=(vmem, blocks, blocks),
        scratch_shapes=[pltpu.VMEM(shape, dtype) for shape, dtype in buffers]
        + [pltpu.SemaphoreType.DMA((2 * ctx_size,))],
        compiler_params=pltpu.CompilerParams(vmem_limit_bytes=limit * mebibyte),
        name="attention_backward",
    )(order, qp, do, qt, dot, *key_list)


def swap(x, axis, mask):
    size = lax.axis_size(axis)
    return lax.ppermute(x, axis, [(i, i ^ mask) for i in range(size)])


def sum_over_heads(own):
    size = lax.axis_size("head")
    place = lax.axis_index("head")
    half = own.shape[0] // 2
    low = place % 2 == 0
    mine = jnp.where(low, own[:half], own[half:])
    other = jnp.where(low, own[half:], own[:half]).astype(jnp.bfloat16)
    part = mine + swap(other, "head", 1).astype(jnp.float32)
    mask = 2
    while mask < size:
        sent = lax.optimization_barrier(part.astype(jnp.bfloat16))
        part = sent.astype(jnp.float32) + swap(sent, "head", mask).astype(jnp.float32)
        mask *= 2
    done = lax.optimization_barrier(part.astype(jnp.bfloat16))
    back = swap(done, "head", 1)
    upper = jnp.where(low, done, back)
    lower = jnp.where(low, back, done)
    return jnp.concatenate([upper, lower]).astype(jnp.float32)


def per_device(block_order, queries, keys, dout):
    token_count, head_count, key_width = queries.shape
    latent_width = dout.shape[2]
    block_rows = token_count // 2
    ctx_size = lax.axis_size("ctx")

    query_rows = queries.reshape(token_count * head_count, key_width)
    grad_rows = dout.reshape(token_count * head_count, latent_width)
    qp, qt, dot = row_layouts(query_rows, grad_rows, block_rows * head_count)
    extra = padded(key_width) - key_width
    keys = jnp.pad(keys, ((0, 0), (0, extra)))
    same_core = [keys] + [swap(keys, "ctx", mask) for mask in range(2, ctx_size, 2)]
    same_core[-1], qp, qt, dot = lax.optimization_barrier((same_core[-1], qp, qt, dot))
    key_list = []
    for block in same_core:
        key_list += [block, swap(block, "ctx", 1)]
    grad_query, keep, send = attention(
        block_order, qp, grad_rows, qt, dot, key_list, block_rows, head_count, key_width
    )
    grad_queries = grad_query.reshape(token_count, head_count, key_width)
    sums = keep.astype(jnp.float32) + swap(send, "ctx", 1).astype(jnp.float32)
    while sums.shape[0] > 1:
        half = sums.shape[0] // 2
        step = half.bit_length() - 1
        pairs = [(i, i ^ chip_axes(i % 2, ctx_size)[step]) for i in range(ctx_size)]
        sums = sums[:half] + lax.ppermute(sums[half:].astype(jnp.bfloat16), "ctx", pairs).astype(
            jnp.float32
        )
    own = sums[0]
    return (grad_queries, sum_over_heads(own)[:, :key_width])


def solution(mesh):
    placed = (P(), P("ctx", "head", None), P("ctx", None), P("ctx", "head", None))
    return jax.shard_map(
        per_device,
        mesh=mesh,
        in_specs=placed,
        out_specs=(P("ctx", "head", None), P("ctx", None)),
        check_vma=False,
    )
```

time: 318 us -> 86.8 us (0.27)
  waiting for transfers between devices: 155 us -> 39.4 us
  matrix products: 57.1 us -> 0 us
  local copies, waits for them, and re-layouts: 53.5 us -> 5.65 us
  starting transfers between devices: 0.12 us -> 23.9 us
  loops' own time: 21.1 us -> 0 us
  Pallas kernels: 0 us -> 16.3 us
  other arithmetic: 16.2 us -> 1.44 us
  between operations: 13.8 us -> 0.72 us
    reduce_scatter x1 -> x0, waiting for transfers between devices: 86.2 us -> none  [per_device(): lax.psum_scatter(grad_keys, 'ctx', scatter_dimension=0, tiled=True)]
    dot_general x42 -> x0, matrix products: 57.1 us -> none  [the longest x12 31.5 us: block_scores(): jnp.dot(query_rows, key_block.T, preferred_element_type=jnp.float32)]
    ppermute x0 -> x13, waiting for transfers between devices: none -> 39.4 us  [the longest x11 23.7 us: swap(): return lax.ppermute(x, axis, [(i, i ^ mask) for i in range(size)])]
    psum x1 -> x0, waiting for transfers between devices: 36.4 us -> none  [per_device(): key_result = lax.psum(own_terms, 'head')]
    all_gather x1 -> x0, waiting for transfers between devices: 31.5 us -> none  [per_device(): lax.all_gather(keys, 'ctx', axis=0, tiled=True)]
    cond x54 -> x0, local copies, waits for them, and re-layouts: 25.3 us -> none
    ppermute x0 -> x13, starting transfers between devices: none -> 23.9 us  [the longest x11 23 us: swap(): return lax.ppermute(x, axis, [(i, i ^ mask) for i in range(size)])]
    another operation x18 -> x0, loops' own time: 21.1 us -> none  [the longest x1 10.2 us: per_device(): carry, unused = lax.scan(first_visit, carry, (blocks, positions))]
  transfers between devices with their start and end apart: 3 -> 13, of which waited for: 3 -> 10; matrix products, arithmetic and copies ran while one was open for 2% -> 0% of each run, Pallas kernels for 0% -> 2%
where the time goes in v2:
time: 86.8 us; the launch traced here: 87.4 us
  waiting for transfers between devices  39.4 us (45%)
  starting transfers between devices  23.9 us (28%)
  Pallas kernels  16.3 us (19%)
  local copies, waits for them, and re-layouts  5.65 us (7%)
  other arithmetic  1.44 us (2%)
    ppermute x11, waiting for transfers between devices, swap(): return lax.ppermute(x, axis, [(i, i ^ mask) for i in range(size)])  23.7 us
    ppermute x11, starting transfers between devices, swap(): return lax.ppermute(x, axis, [(i, i ^ mask) for i in range(size)])  23 us
    ppermute x2, waiting for transfers between devices, per_device(): lax.ppermute(sums[half:].astype(jnp.bfloat16), 'ctx', pairs)  15.6 us
    pallas_call x1, Pallas kernels, attention(): pl.pallas_call(functools.partial(attention_kernel, direct, ctx_size, bloc...  15 us
    unnamed x10, local copies, waits for them, and re-layouts  4.57 us
  transfers between devices with their start and end apart: 13, of which 10 were waited for; matrix products, arithmetic and copies ran while one was open for 0% of the time, Pallas kernels for 2%

profile of v2, /device:TPU:0, one launch (start us, length us, event | category | flops | bytes accessed | tf_op | source)
XLA Modules:
  0.0 87.4 jit_solution(8142304173286863937)
XLA Ops:
  0.6 1.0 %pad.4.rest_4_ = bf16[224,640]{1,0:T(8,128)(2,1)S(1)} pad(bf16[224,576]{1,0:T(8,128)(2,1)} %param.6, bf16[]{:T(256)} %constant.15.clone.1), padding=0_0x0_64 | pad | bytes 544770 | tf_op jit(solution)/shard_map/jit(_pad)/pad | solution.py:304
  1.6 4.0 %collective-permute-start = (bf16[224,640]{1,0:T(8,128)(2,1)S(1)}, bf16[224,640]{1,0:T(8,128)(2,1)S(1)}, u32[]{:S(2)}, u32[]{:S(2)}) collective-permute-start(bf16[224,640]{1,0:T(8,128)(2,1)S(1)} %pad.4.rest_4_), channel_id=1, source_target_pairs={{0,24},{4,28},{8,16},{12,20},{16,8},{20,12},{24,0},{28,4},{1,25},{... | collective-permute-start | bytes 860168 | tf_op jit(solution)/shard_map/ppermute | solution.py:271
  5.6 0.5 collective-permute-start.2
  6.1 0.1 collective-permute-start.4
  6.2 0.0 collective-permute-start.1
  6.2 0.0 copy-start
  6.2 1.5 %copy-done = bf16[224,8,512]{2,1,0:T(8,128)(2,1)S(1)} copy-done((bf16[224,8,512]{2,1,0:T(8,128)(2,1)S(1)}, bf16[224,8,512]{2,1,0:T(8,128)(2,1)}, u32[]{:S(2)}) %copy-start) | copy-done | bytes 1835032
  7.7 0.0 copy-start.3
  7.7 1.6 %copy-done.3 = bf16[224,8,576]{2,1,0:T(8,128)(2,1)S(1)} copy-done((bf16[224,8,576]{2,1,0:T(8,128)(2,1)S(1)}, bf16[224,8,576]{2,1,0:T(8,128)(2,1)}, u32[]{:S(2)}) %copy-start.3) | copy-done | bytes 2064408
  9.4 0.0 copy-start.1
  9.4 0.0 copy-start.4
  9.4 1.3 %row_layouts.1 = (bf16[1792,640]{1,0:T(8,128)(2,1)S(1)}, bf16[2,576,896]{2,1,0:T(8,128)(2,1)S(1)}, bf16[2,512,896]{2,1,0:T(8,128)(2,1)S(1)}) custom-call(bf16[1792,576]{1,0:T(8,128)(2,1)S(1)} %bitcast.11, bf16[1792,512]{1,0:T(8,128)(2,1)S(1)} %bitcast.9), custom_call_target="tpu_custom_call" | custom-call | tf_op jit(solution)/shard_map/row_layouts/pallas_call | solution.py:214
  10.7 0.0 copy-start.2
  10.7 1.4 %copy-done.2 = bf16[1792,640]{1,0:T(8,128)(2,1)} copy-done((bf16[1792,640]{1,0:T(8,128)(2,1)}, bf16[1792,640]{1,0:T(8,128)(2,1)S(1)}, u32[]{:S(2)}) %copy-start.2) | copy-done | bytes 2293784
  12.1 1.2 %collective-permute-done.rest_10_ = bf16[224,640]{1,0:T(8,128)(2,1)S(1)} collective-permute-done((bf16[224,640]{1,0:T(8,128)(2,1)S(1)}, bf16[224,640]{1,0:T(8,128)(2,1)S(1)}, u32[]{:S(2)}, u32[]{:S(2)}) %collective-permute-start) | collective-permute-done | bytes 286752 | tf_op jit(solution)/shard_map/ppermute | solution.py:271
  13.3 0.0 collective-permute-start.6
  13.3 5.6 %collective-permute-done.2.rest_6_ = bf16[224,640]{1,0:T(8,128)(2,1)S(1)} collective-permute-done((bf16[224,640]{1,0:T(8,128)(2,1)S(1)}, bf16[224,640]{1,0:T(8,128)(2,1)S(1)}, u32[]{:S(2)}, u32[]{:S(2)}) %collective-permute-start.2) | collective-permute-done | bytes 286752 | tf_op jit(solution)/shard_map/ppermute | solution.py:271
  18.9 0.0 collective-permute-start.3
  18.9 0.0 collective-permute-done.4.rest_8_
  18.9 0.5 collective-permute-start.5
  19.4 0.0 collective-permute-done.1.rest_5_
  19.4 0.0 collective-permute-done.6.rest_11_
  19.4 1.1 %collective-permute-done.3.rest_7_ = bf16[224,640]{1,0:T(8,128)(2,1)S(1)} collective-permute-done((bf16[224,640]{1,0:T(8,128)(2,1)S(1)}, bf16[224,640]{1,0:T(8,128)(2,1)S(1)}, u32[]{:S(2)}, u32[]{:S(2)}) %collective-permute-start.3) | collective-permute-done | bytes 286752 | tf_op jit(solution)/shard_map/ppermute | solution.py:271
  20.4 0.4 collective-permute-done.5.rest_9_
  20.8 0.0 copy-done.1
  20.8 0.0 copy-done.4
  20.8 15.0 %attention_backward.1 = (bf16[1792,576]{1,0:T(8,128)(2,1)}, bf16[4,224,640]{2,1,0:T(8,128)(2,1)S(1)}, bf16[4,224,640]{2,1,0:T(8,128)(2,1)S(1)}) custom-call(s32[16]{0:T(128)S(1)} %copy-done.4, bf16[1792,640]{1,0:T(8,128)(2,1)} %copy-done.2, bf16[1792,512]{1,0:T(8,128)(2,1)S(1)} %bitcast.10, bf16[2,576,896]{2,1,0:T(8,128)(2,1)S(1)} %get-tuple-element.16.rest_2_, ...), custom_call_target="tpu_custom_call" | custom-call | tf_op jit(solution)/shard_map/attention_backward/pallas_call | solution.py:253
  35.8 13.0 %collective-permute-start.7 = (bf16[4,224,640]{2,1,0:T(8,128)(2,1)S(1)}, bf16[4,224,640]{2,1,0:T(8,128)(2,1)S(1)}, u32[]{:S(2)}, u32[]{:S(2)}) collective-permute-start(bf16[4,224,640]{2,1,0:T(8,128)(2,1)S(1)} %get-tuple-element.21), channel_id=1, source_target_pairs={{0,4},{4,0},{8,12},{12,8},{16,20},{20,16},{24,28},{28,24},{1,5},{5... | collective-permute-start | bytes 3440648 | tf_op jit(solution)/shard_map/ppermute | solution.py:271
  48.8 2.4 %collective-permute-done.7 = bf16[4,224,640]{2,1,0:T(8,128)(2,1)S(1)} collective-permute-done((bf16[4,224,640]{2,1,0:T(8,128)(2,1)S(1)}, bf16[4,224,640]{2,1,0:T(8,128)(2,1)S(1)}, u32[]{:S(2)}, u32[]{:S(2)}) %collective-permute-start.7) | collective-permute-done | bytes 1146912 | tf_op jit(solution)/shard_map/ppermute | solution.py:271
  51.3 0.2 convert_add_fusion
  51.5 0.1 slice.57
  51.6 0.1 collective-permute-start.8
  51.7 9.7 %collective-permute-done.8 = bf16[2,224,640]{2,1,0:T(8,128)(2,1)S(1)} collective-permute-done((bf16[2,224,640]{2,1,0:T(8,128)(2,1)S(1)}, bf16[2,224,640]{2,1,0:T(8,128)(2,1)S(1)}, u32[]{:S(2)}, u32[]{:S(2)}) %collective-permute-start.8) | collective-permute-done | bytes 573472 | tf_op jit(solution)/shard_map/ppermute | solution.py:319
  61.3 0.1 slice_add_fusion
  61.5 0.8 collective-permute-start.9
  62.3 5.9 %collective-permute-done.9 = bf16[1,224,640]{2,1,0:T(8,128)(2,1)S(1)} collective-permute-done((bf16[1,224,640]{2,1,0:T(8,128)(2,1)S(1)}, bf16[1,224,640]{2,1,0:T(8,128)(2,1)S(1)}, u32[]{:S(2)}, u32[]{:S(2)}) %collective-permute-start.9) | collective-permute-done | bytes 286752 | tf_op jit(solution)/shard_map/ppermute | solution.py:319
  68.2 0.1 slice_add_fusion.1
  68.3 1.6 %collective-permute-start.10 = (bf16[112,640]{1,0:T(8,128)(2,1)S(1)}, bf16[112,640]{1,0:T(8,128)(2,1)S(1)}, u32[]{:S(2)}, u32[]{:S(2)}) collective-permute-start(bf16[112,640]{1,0:T(8,128)(2,1)S(1)} %fusion.2), channel_id=1, source_target_pairs={{0,1},{1,0},{2,3},{3,2},{4,5},{5,4},{6,7},{7,6},{8,9},{9,8},{10,11... | collective-permute-start | bytes 430088 | tf_op jit(solution)/shard_map/ppermute | solution.py:271
  70.0 3.5 %collective-permute-done.10 = bf16[112,640]{1,0:T(8,128)(2,1)S(1)} collective-permute-done((bf16[112,640]{1,0:T(8,128)(2,1)S(1)}, bf16[112,640]{1,0:T(8,128)(2,1)S(1)}, u32[]{:S(2)}, u32[]{:S(2)}) %collective-permute-start.10) | collective-permute-done | bytes 143392 | tf_op jit(solution)/shard_map/ppermute | solution.py:271
  73.6 2.6 %collective-permute-start.11 = (bf16[112,640]{1,0:T(8,128)(2,1)S(1)}, bf16[112,640]{1,0:T(8,128)(2,1)S(1)}, u32[]{:S(2)}, u32[]{:S(2)}) collective-permute-start(bf16[112,640]{1,0:T(8,128)(2,1)S(1)} %fusion.1), channel_id=1, source_target_pairs={{0,2},{1,3},{2,0},{3,1},{4,6},{5,7},{6,4},{7,5},{8,10},{9,11},{10,... | collective-permute-start | bytes 430088 | tf_op jit(solution)/shard_map/ppermute | solution.py:271
  76.2 5.1 %collective-permute-done.11 = bf16[112,640]{1,0:T(8,128)(2,1)S(1)} collective-permute-done((bf16[112,640]{1,0:T(8,128)(2,1)S(1)}, bf16[112,640]{1,0:T(8,128)(2,1)S(1)}, u32[]{:S(2)}, u32[]{:S(2)}) %collective-permute-start.11) | collective-permute-done | bytes 143392 | tf_op jit(solution)/shard_map/ppermute | solution.py:271
  81.3 0.6 collective-permute-start.12
  81.9 4.5 %collective-permute-done.12 = bf16[112,640]{1,0:T(8,128)(2,1)S(1)} collective-permute-done((bf16[112,640]{1,0:T(8,128)(2,1)S(1)}, bf16[112,640]{1,0:T(8,128)(2,1)S(1)}, u32[]{:S(2)}, u32[]{:S(2)}) %collective-permute-start.12) | collective-permute-done | bytes 143392 | tf_op jit(solution)/shard_map/ppermute | solution.py:271
  86.5 0.8 fusion
  (5 shorter events, 0.2 us)
Async XLA Ops:
  1.6 11.7 %collective-permute-start = (bf16[224,640]{1,0:T(8,128)(2,1)S(1)}, bf16[224,640]{1,0:T(8,128)(2,1)S(1)}, u32[]{:S(2)}, u32[]{:S(2)}) collective-permute-start(bf16[224,640]{1,0:T(8,128)(2,1)S(1)} %pad.4.rest_4_), channel_id=1, source_target_pairs={{0,24},{4,28},{8,16},{12,20},{16,8},{20,12},{24,0},{28,4},{1,25},{... | collective-permute-start | bytes 860168 | tf_op jit(solution)/shard_map/ppermute | solution.py:271
  5.6 13.3 %collective-permute-start.2 = (bf16[224,640]{1,0:T(8,128)(2,1)S(1)}, bf16[224,640]{1,0:T(8,128)(2,1)S(1)}, u32[]{:S(2)}, u32[]{:S(2)}) collective-permute-start(bf16[224,640]{1,0:T(8,128)(2,1)S(1)} %pad.4.rest_4_), channel_id=1, source_target_pairs={{0,8},{4,12},{8,0},{12,4},{16,24},{20,28},{24,16},{28,20},{1,9},{5... | collective-permute-start | bytes 860168 | tf_op jit(solution)/shard_map/ppermute | solution.py:271
  6.1 12.7 %collective-permute-start.4 = (bf16[224,640]{1,0:T(8,128)(2,1)S(1)}, bf16[224,640]{1,0:T(8,128)(2,1)S(1)}, u32[]{:S(2)}, u32[]{:S(2)}) collective-permute-start(bf16[224,640]{1,0:T(8,128)(2,1)S(1)} %pad.4.rest_4_), channel_id=1, source_target_pairs={{0,16},{4,20},{8,24},{12,28},{16,0},{20,4},{24,8},{28,12},{1,17},{... | collective-permute-start | bytes 860168 | tf_op jit(solution)/shard_map/ppermute | solution.py:271
  6.2 13.1 %collective-permute-start.1 = (bf16[224,640]{1,0:T(8,128)(2,1)S(1)}, bf16[224,640]{1,0:T(8,128)(2,1)S(1)}, u32[]{:S(2)}, u32[]{:S(2)}) collective-permute-start(bf16[224,640]{1,0:T(8,128)(2,1)S(1)} %pad.4.rest_4_), channel_id=1, source_target_pairs={{0,4},{4,0},{8,12},{12,8},{16,20},{20,16},{24,28},{28,24},{1,5},{5... | collective-permute-start | bytes 860168 | tf_op jit(solution)/shard_map/ppermute | solution.py:271
  6.2 1.5 %copy-start = (bf16[224,8,512]{2,1,0:T(8,128)(2,1)S(1)}, bf16[224,8,512]{2,1,0:T(8,128)(2,1)}, u32[]{:S(2)}) copy-start(bf16[224,8,512]{2,1,0:T(8,128)(2,1)} %param.7) | copy-start | bytes 5505028
  7.7 1.6 %copy-start.3 = (bf16[224,8,576]{2,1,0:T(8,128)(2,1)S(1)}, bf16[224,8,576]{2,1,0:T(8,128)(2,1)}, u32[]{:S(2)}) copy-start(bf16[224,8,576]{2,1,0:T(8,128)(2,1)} %param.5) | copy-start | bytes 6193156
  9.4 11.5 %copy-start.1 = (bf16[224,8,512]{2,1,0:T(8,128)(2,1)S(1)}, bf16[224,8,512]{2,1,0:T(8,128)(2,1)}, u32[]{:S(2)}) copy-start(bf16[224,8,512]{2,1,0:T(8,128)(2,1)} %param.7) | copy-start | bytes 5505028
  9.4 11.5 %copy-start.4 = (s32[16]{0:T(128)S(1)}, s32[16]{0:T(128)}, u32[]{:S(2)}) copy-start(s32[16]{0:T(128)} %order_ref.1) | copy-start | bytes 196
  10.7 1.4 %copy-start.2 = (bf16[1792,640]{1,0:T(8,128)(2,1)}, bf16[1792,640]{1,0:T(8,128)(2,1)S(1)}, u32[]{:S(2)}) copy-start(bf16[1792,640]{1,0:T(8,128)(2,1)S(1)} %get-tuple-element.15.rest_0_) | copy-start | bytes 6881284
  13.3 6.1 %collective-permute-start.6 = (bf16[224,640]{1,0:T(8,128)(2,1)S(1)}, bf16[224,640]{1,0:T(8,128)(2,1)S(1)}, u32[]{:S(2)}, u32[]{:S(2)}) collective-permute-start(bf16[224,640]{1,0:T(8,128)(2,1)S(1)} %collective-permute-done.rest_10_), channel_id=1, source_target_pairs={{0,4},{4,0},{8,12},{12,8},{16,20},{20,16},{24,28},{28,24},{1,5},{5... | collective-permute-start | bytes 860168 | tf_op jit(solution)/shard_map/ppermute | solution.py:271
  18.9 1.6 %collective-permute-start.3 = (bf16[224,640]{1,0:T(8,128)(2,1)S(1)}, bf16[224,640]{1,0:T(8,128)(2,1)S(1)}, u32[]{:S(2)}, u32[]{:S(2)}) collective-permute-start(bf16[224,640]{1,0:T(8,128)(2,1)S(1)} %collective-permute-done.2.rest_6_), channel_id=1, source_target_pairs={{0,4},{4,0},{8,12},{12,8},{16,20},{20,16},{24,28},{28,24},{1,5},{5... | collective-permute-start | bytes 860168 | tf_op jit(solution)/shard_map/ppermute | solution.py:271
  18.9 2.0 %collective-permute-start.5 = (bf16[224,640]{1,0:T(8,128)(2,1)S(1)}, bf16[224,640]{1,0:T(8,128)(2,1)S(1)}, u32[]{:S(2)}, u32[]{:S(2)}) collective-permute-start(bf16[224,640]{1,0:T(8,128)(2,1)S(1)} %collective-permute-done.4.rest_8_), channel_id=1, source_target_pairs={{0,4},{4,0},{8,12},{12,8},{16,20},{20,16},{24,28},{28,24},{1,5},{5... | collective-permute-start | bytes 860168 | tf_op jit(solution)/shard_map/ppermute | solution.py:271
  35.8 15.4 %collective-permute-start.7 = (bf16[4,224,640]{2,1,0:T(8,128)(2,1)S(1)}, bf16[4,224,640]{2,1,0:T(8,128)(2,1)S(1)}, u32[]{:S(2)}, u32[]{:S(2)}) collective-permute-start(bf16[4,224,640]{2,1,0:T(8,128)(2,1)S(1)} %get-tuple-element.21), channel_id=1, source_target_pairs={{0,4},{4,0},{8,12},{12,8},{16,20},{20,16},{24,28},{28,24},{1,5},{5... | collective-permute-start | bytes 3440648 | tf_op jit(solution)/shard_map/ppermute | solution.py:271
  51.6 9.8 %collective-permute-start.8 = (bf16[2,224,640]{2,1,0:T(8,128)(2,1)S(1)}, bf16[2,224,640]{2,1,0:T(8,128)(2,1)S(1)}, u32[]{:S(2)}, u32[]{:S(2)}) collective-permute-start(bf16[2,224,640]{2,1,0:T(8,128)(2,1)S(1)} %slice.57), channel_id=1, source_target_pairs={{0,16},{4,12},{8,24},{12,4},{16,0},{20,28},{24,8},{28,20},{1,17},{... | collective-permute-start | bytes 1720328 | tf_op jit(solution)/shard_map/ppermute | solution.py:319
  61.5 6.7 %collective-permute-start.9 = (bf16[1,224,640]{2,1,0:T(8,128)(2,1)S(1)}, bf16[1,224,640]{2,1,0:T(8,128)(2,1)S(1)}, u32[]{:S(2)}, u32[]{:S(2)}) collective-permute-start(bf16[1,224,640]{2,1,0:T(8,128)(2,1)S(1)} %slice.58), channel_id=1, source_target_pairs={{0,8},{4,20},{8,0},{12,28},{16,24},{20,4},{24,16},{28,12},{1,9},{5... | collective-permute-start | bytes 860168 | tf_op jit(solution)/shard_map/ppermute | solution.py:319
  68.3 5.2 %collective-permute-start.10 = (bf16[112,640]{1,0:T(8,128)(2,1)S(1)}, bf16[112,640]{1,0:T(8,128)(2,1)S(1)}, u32[]{:S(2)}, u32[]{:S(2)}) collective-permute-start(bf16[112,640]{1,0:T(8,128)(2,1)S(1)} %fusion.2), channel_id=1, source_target_pairs={{0,1},{1,0},{2,3},{3,2},{4,5},{5,4},{6,7},{7,6},{8,9},{9,8},{10,11... | collective-permute-start | bytes 430088 | tf_op jit(solution)/shard_map/ppermute | solution.py:271
  73.6 7.7 %collective-permute-start.11 = (bf16[112,640]{1,0:T(8,128)(2,1)S(1)}, bf16[112,640]{1,0:T(8,128)(2,1)S(1)}, u32[]{:S(2)}, u32[]{:S(2)}) collective-permute-start(bf16[112,640]{1,0:T(8,128)(2,1)S(1)} %fusion.1), channel_id=1, source_target_pairs={{0,2},{1,3},{2,0},{3,1},{4,6},{5,7},{6,4},{7,5},{8,10},{9,11},{10,... | collective-permute-start | bytes 430088 | tf_op jit(solution)/shard_map/ppermute | solution.py:271
  81.3 5.2 %collective-permute-start.12 = (bf16[112,640]{1,0:T(8,128)(2,1)S(1)}, bf16[112,640]{1,0:T(8,128)(2,1)S(1)}, u32[]{:S(2)}, u32[]{:S(2)}) collective-permute-start(bf16[112,640]{1,0:T(8,128)(2,1)S(1)} %add_convert_fusion), channel_id=1, source_target_pairs={{0,1},{1,0},{2,3},{3,2},{4,5},{5,4},{6,7},{7,6},{8,9},{9,8},{10,11... | collective-permute-start | bytes 430088 | tf_op jit(solution)/shard_map/ppermute | solution.py:271

commit v3 on v2

--- a/solution.py
+++ b/solution.py
@@ -27,6 +27,33 @@
 
 def chip_mask(label, core, ctx_size):
     return sum(axis for t, axis in enumerate(chip_axes(core, ctx_size)) if label >> t & 1)
+
+
+def key_rows(j, count):
+    return pl.ds(pl.multiple_of(j * tile, tile), count * tile)
+
+
+def visits(count, visit, largest):
+    @pl.loop(0, count // largest)
+    def _(i):
+        visit(i * largest, largest)
+
+    size = largest // 2
+    while size:
+
+        @pl.when(count // size % 2 == 1)
+        def _(size=size):
+            visit(count // (2 * size) * (2 * size), size)
+
+        size //= 2
+
+
+def query_blocks(order_ref, me, block_rows):
+    first = jnp.where(order_ref[2 * me] < order_ref[2 * me + 1], 0, 1)
+    order = (first, 1 - first)
+    places = [order_ref[2 * me + b] for b in order]
+    counts = [((place + 1) * block_rows + tile - 1) // tile for place in places]
+    return order, places, counts
 
 
 def layout_kernel(rows, q_ref, do_ref, qp_ref, qt_ref, dot_ref):
@@ -42,8 +69,15 @@
 def attention_kernel(direct, ctx_size, block_rows, heads, latent, width, order_ref, *rest):
     q, do, qt, dot = rest[:4]
     key_refs = rest[4 : 4 + ctx_size]
-    dq_ref, keep_ref, send_ref = rest[4 + ctx_size : 7 + ctx_size]
-    (keys, stage, probs, gprobs, marks, peak, total, weighted, dq_acc, dkt, move_sem) = rest[7 + ctx_size :]
+    keep_ref, send_ref = rest[4 + ctx_size : 6 + ctx_size]
+    if direct:
+        keys, *ds_refs = rest[6 + ctx_size : 9 + ctx_size]
+        stage, probs, gprobs, marks, peak, total, weighted, dkt = rest[9 + ctx_size :]
+    else:
+        dq_ref = rest[6 + ctx_size]
+        stage, probs, gprobs, marks, peak, total, weighted, dkt, keys, dq_acc, move_sem = rest[
+            7 + ctx_size :
+        ]
     seq = keys.shape[0]
     tiles = seq // tile
     rows = block_rows * heads
@@ -72,34 +106,24 @@
     def sub_rows(sub):
         return pl.ds(sub * block_rows, block_rows)
 
-    move(
-        [
-            (key_refs[mask].at[sub_rows(sub), :], keys.at[sorted_rows(mask, sub), :])
-            for mask, sub in blocks
-        ]
-    )
-
-    first = jnp.where(order_ref[2 * me] < order_ref[2 * me + 1], 0, 1)
-    order = (first, 1 - first)
-    places = [order_ref[2 * me + b] for b in order]
-    counts = [((place + 1) * block_rows + tile - 1) // tile for place in places]
+    if direct:
+        keys[:, width:] = jnp.zeros((seq, keys.shape[1] - width), keys.dtype)
+        for mask, sub in blocks:
+            keys[sorted_rows(mask, sub), :width] = key_refs[mask][sub_rows(sub), :]
+    else:
+        move(
+            [
+                (key_refs[mask].at[sub_rows(sub), :], keys.at[sorted_rows(mask, sub), :])
+                for mask, sub in blocks
+            ]
+        )
+
+    order, places, counts = query_blocks(order_ref, me, block_rows)
 
     @pl.loop(counts[0], counts[1])
     def _(j):
         dkt[j] = jnp.zeros(dkt.shape[1:], dkt.dtype)
 
-
-    def key_rows(j, count):
-        return pl.ds(pl.multiple_of(j * tile, tile), count * tile)
-
-    def visits(count, visit):
-        @pl.loop(0, count // 2)
-        def _(i):
-            visit(2 * i, 2)
-
-        @pl.when(count % 2 == 1)
-        def _():
-            visit(count - 1, 1)
 
     def piece(h):
         return slice(h % 2 * lanes, h % 2 * lanes + lanes)
@@ -144,7 +168,7 @@
             total[...] = acc
             weighted[...] = wacc
 
-        visits(counts[turn], score_visit)
+        visits(counts[turn], score_visit, 2)
 
         top = jnp.max(peak[...], axis=1, keepdims=True)
         share = jnp.exp2(peak[...] - top)
@@ -153,7 +177,8 @@
         peak[...] = jnp.broadcast_to(top, peak.shape)
         total[...] = jnp.broadcast_to(inverse, total.shape)
         weighted[...] = jnp.broadcast_to(delta, weighted.shape)
-        dq_acc[...] = jnp.zeros_like(dq_acc)
+        if not direct:
+            dq_acc[...] = jnp.zeros_like(dq_acc)
 
         def grad_visit(j, n):
             factor = jnp.exp2(marks[j // 2] - peak[...]) * total[...]
@@ -166,9 +191,13 @@
                 grads.append((p * (g - delta)).astype(jnp.bfloat16))
             ds = jnp.concatenate(grads, axis=1)
             ph = jnp.concatenate(halves, axis=1)
-            dq_acc[...] += jnp.dot(
-                ds, keys[key_rows(j, n), :], preferred_element_type=jnp.float32
-            )
+            if direct:
+                for t in range(n):
+                    ds_refs[turn][j + t] = ds[:, t * tile : t * tile + tile]
+            else:
+                dq_acc[...] += jnp.dot(
+                    ds, keys[key_rows(j, n), :], preferred_element_type=jnp.float32
+                )
             kt = jnp.dot(qt[b], ds, preferred_element_type=jnp.float32) * softmax_scale
             vt = jnp.dot(dot[b], ph, preferred_element_type=jnp.float32)
             for t in range(n):
@@ -187,8 +216,9 @@
                         (tile, stage.shape[1] - width), stage.dtype
                     )
 
-        visits(counts[turn], grad_visit)
-        dq_ref[span, :] = (dq_acc[:, :width] * softmax_scale).astype(jnp.bfloat16)
+        visits(counts[turn], grad_visit, 2)
+        if not direct:
+            dq_ref[span, :] = (dq_acc[:, :width] * softmax_scale).astype(jnp.bfloat16)
 
     @pl.loop(counts[1], tiles)
     def _(j):
@@ -225,7 +255,40 @@
     )(q, do)
 
 
-def attention(order, qp, do, qt, dot, key_list, block_rows, heads, width):
+def query_kernel(block_rows, heads, order_ref, keys, ds0, ds1, dq_ref, acc):
+    rows = block_rows * heads
+    width = dq_ref.shape[1]
+    order, places, counts = query_blocks(order_ref, lax.axis_index("ctx"), block_rows)
+    for turn in range(2):
+        acc[...] = jnp.zeros_like(acc)
+
+        def visit(j, n, ds=(ds0, ds1)[turn]):
+            left = jnp.concatenate([ds[j + t] for t in range(n)], axis=1)
+            acc[...] += jnp.dot(left, keys[key_rows(j, n), :], preferred_element_type=jnp.float32)
+
+        visits(counts[turn], visit, 4)
+        span = pl.ds(pl.multiple_of(order[turn] * rows, rows), rows)
+        dq_ref[span, :] = (acc[:, :width] * softmax_scale).astype(jnp.bfloat16)
+
+
+def query_gradient(order, keys, ds0, ds1, block_rows, heads, width):
+    total_rows = 2 * block_rows * heads
+    vmem = pl.BlockSpec(memory_space=pltpu.VMEM)
+    return pl.pallas_call(
+        functools.partial(query_kernel, block_rows, heads),
+        out_shape=jax.ShapeDtypeStruct((total_rows, width), jnp.bfloat16),
+        in_specs=[pl.BlockSpec(memory_space=pltpu.SMEM)] + [vmem] * 3,
+        out_specs=vmem,
+        scratch_shapes=[pltpu.VMEM((block_rows * heads, keys.shape[1]), jnp.float32)],
+        compiler_params=pltpu.CompilerParams(vmem_limit_bytes=24 * mebibyte),
+        cost_estimate=pl.CostEstimate(
+            flops=2 * total_rows * keys.shape[0] * width, bytes_accessed=0, transcendentals=0
+        ),
+        name="query_gradient",
+    )(order, keys, ds0, ds1)
+
+
+def attention(order, qp, do, qt, dot, key_list, block_rows, heads, width, direct):
     ctx_size = len(key_list)
     total_rows = qp.shape[0]
     latent = do.shape[1]
@@ -235,33 +298,39 @@
     tiles = seq // tile
     vmem = pl.BlockSpec(memory_space=pltpu.VMEM)
     f32, bf16 = jnp.float32, jnp.bfloat16
+    wide = padded(width)
     buffers = [
-        ((seq, padded(width)), bf16),
-        ((seq, padded(width)), bf16),
+        ((seq, wide), bf16),
         ((tiles, rows, tile), f32),
         ((tiles, rows, tile), f32),
         (((tiles + 1) // 2, rows, lanes), f32),
         ((rows, lanes), f32),
         ((rows, lanes), f32),
         ((rows, lanes), f32),
-        ((rows, padded(width)), f32),
         ((tiles, width, tile), f32),
     ]
-    direct = seq <= 2048
+    out_shape = [jax.ShapeDtypeStruct((half, 2 * block_rows, wide), bf16)] * 2
+    if direct:
+        out_shape += [
+            jax.ShapeDtypeStruct((seq, wide), bf16),
+            jax.ShapeDtypeStruct((tiles, rows, tile), bf16),
+            jax.ShapeDtypeStruct((tiles, rows, tile), bf16),
+        ]
+        scratch = []
+    else:
+        out_shape += [jax.ShapeDtypeStruct((total_rows, width), bf16)]
+        buffers += [((seq, wide), bf16), ((rows, wide), f32)]
+        scratch = [pltpu.SemaphoreType.DMA((2 * ctx_size,))]
     blocks = vmem if direct else pl.BlockSpec(memory_space=pl.ANY)
-    limit = 42 if direct else 63
     return pl.pallas_call(
         functools.partial(attention_kernel, direct, ctx_size, block_rows, heads, latent, width),
-        out_shape=(
-            jax.ShapeDtypeStruct((total_rows, width), bf16),
-            jax.ShapeDtypeStruct((half, 2 * block_rows, padded(width)), bf16),
-            jax.ShapeDtypeStruct((half, 2 * block_rows, padded(width)), bf16),
+        out_shape=tuple(out_shape),
+        in_specs=[pl.BlockSpec(memory_space=pltpu.SMEM)] + [vmem] * 4 + [blocks] * ctx_size,
+        out_specs=(blocks, blocks) + (vmem,) * (len(out_shape) - 2),
+        scratch_shapes=[pltpu.VMEM(shape, dtype) for shape, dtype in buffers] + scratch,
+        compiler_params=pltpu.CompilerParams(
+            vmem_limit_bytes=(32 if direct else 63) * mebibyte
         ),
-        in_specs=[pl.BlockSpec(memory_space=pltpu.SMEM)] + [vmem] * 4 + [blocks] * ctx_size,
-        out_specs=(vmem, blocks, blocks),
-        scratch_shapes=[pltpu.VMEM(shape, dtype) for shape, dtype in buffers]
-        + [pltpu.SemaphoreType.DMA((2 * ctx_size,))],
-        compiler_params=pltpu.CompilerParams(vmem_limit_bytes=limit * mebibyte),
         name="attention_backward",
     )(order, qp, do, qt, dot, *key_list)
 
@@ -300,26 +369,33 @@
     query_rows = queries.reshape(token_count * head_count, key_width)
     grad_rows = dout.reshape(token_count * head_count, latent_width)
     qp, qt, dot = row_layouts(query_rows, grad_rows, block_rows * head_count)
-    extra = padded(key_width) - key_width
-    keys = jnp.pad(keys, ((0, 0), (0, extra)))
+    direct = token_count * ctx_size <= 2048
+    if not direct:
+        keys = jnp.pad(keys, ((0, 0), (0, padded(key_width) - key_width)))
     same_core = [keys] + [swap(keys, "ctx", mask) for mask in range(2, ctx_size, 2)]
     same_core[-1], qp, qt, dot = lax.optimization_barrier((same_core[-1], qp, qt, dot))
     key_list = []
     for block in same_core:
         key_list += [block, swap(block, "ctx", 1)]
-    grad_query, keep, send = attention(
-        block_order, qp, grad_rows, qt, dot, key_list, block_rows, head_count, key_width
+    keep, send, *found = attention(
+        block_order, qp, grad_rows, qt, dot, key_list, block_rows, head_count, key_width, direct
     )
-    grad_queries = grad_query.reshape(token_count, head_count, key_width)
     sums = keep.astype(jnp.float32) + swap(send, "ctx", 1).astype(jnp.float32)
+    if direct:
+        sums, *found = lax.optimization_barrier((sums, *found))
+        grad_query = query_gradient(block_order, *found, block_rows, head_count, key_width)
+    else:
+        grad_query = found[0]
     while sums.shape[0] > 1:
         half = sums.shape[0] // 2
         step = half.bit_length() - 1
         pairs = [(i, i ^ chip_axes(i % 2, ctx_size)[step]) for i in range(ctx_size)]
-        sums = sums[:half] + lax.ppermute(sums[half:].astype(jnp.bfloat16), "ctx", pairs).astype(
-            jnp.float32
-        )
+        arrived = lax.ppermute(sums[half:].astype(jnp.bfloat16), "ctx", pairs)
+        if direct and sums.shape[0] == ctx_size // 2:
+            arrived, grad_query = lax.optimization_barrier((arrived, grad_query))
+        sums = sums[:half] + arrived.astype(jnp.float32)
     own = sums[0]
+    grad_queries = grad_query.reshape(token_count, head_count, key_width)
     return (grad_queries, sum_over_heads(own)[:, :key_width])
 
 

time: 86.8 us -> 81.1 us (0.934)
  waiting for transfers between devices: 39.4 us -> 32.8 us
  starting transfers between devices: 23.9 us -> 26.4 us
  local copies, waits for them, and re-layouts: 5.65 us -> 3.25 us
    ppermute x2, starting transfers between devices: 0.85 us -> 10.2 us  [per_device(): arrived = lax.ppermute(sums[half:].astype(jnp.bfloat16), 'ctx', pairs)]
    ppermute x2, waiting for transfers between devices: 15.6 us -> 7.44 us  [per_device(): arrived = lax.ppermute(sums[half:].astype(jnp.bfloat16), 'ctx', pairs)]
    ppermute x11, starting transfers between devices: 23 us -> 16.2 us  [swap(): return lax.ppermute(x, axis, [(i, i ^ mask) for i in range(size)])]
    pallas_call x0 -> x1, Pallas kernels: none -> 4.87 us  [query_gradient(): pl.pallas_call(functools.partial(query_kernel, block_rows, heads), out_sh...]
    pallas_call x1, Pallas kernels: 15 us -> 10.2 us  [attention(): pl.pallas_call(functools.partial(attention_kernel, direct, ctx_size, bloc...]
    ppermute x11, waiting for transfers between devices: 23.7 us -> 25.4 us  [swap(): return lax.ppermute(x, axis, [(i, i ^ mask) for i in range(size)])]
    unnamed x10, local copies, waits for them, and re-layouts: 4.57 us -> 3.16 us
    pad x1 -> x0, local copies, waits for them, and re-layouts: 0.99 us -> none  [per_device(): keys = jnp.pad(keys, ((0, 0), (0, extra)))]
  transfers between devices with their start and end apart: 13 -> 13, of which waited for: 10 -> 10; matrix products, arithmetic and copies ran while one was open for 0% -> 0% of each run, Pallas kernels for 2% -> 8%
where the time goes in v3:
time: 81.1 us; the launch traced here: 80.9 us
  waiting for transfers between devices  32.8 us (40%)
  starting transfers between devices  26.4 us (33%)
  Pallas kernels  16.3 us (20%)
  local copies, waits for them, and re-layouts  3.25 us (4%)
  other arithmetic  1.39 us (2%)
    ppermute x11, waiting for transfers between devices, swap(): return lax.ppermute(x, axis, [(i, i ^ mask) for i in range(size)])  25.4 us
    ppermute x11, starting transfers between devices, swap(): return lax.ppermute(x, axis, [(i, i ^ mask) for i in range(size)])  16.2 us
    ppermute x2, starting transfers between devices, per_device(): arrived = lax.ppermute(sums[half:].astype(jnp.bfloat16), 'ctx', pairs)  10.2 us
    pallas_call x1, Pallas kernels, attention(): pl.pallas_call(functools.partial(attention_kernel, direct, ctx_size, bloc...  10.2 us
    ppermute x2, waiting for transfers between devices, per_device(): arrived = lax.ppermute(sums[half:].astype(jnp.bfloat16), 'ctx', pairs)  7.44 us
    pallas_call x1, Pallas kernels, query_gradient(): pl.pallas_call(functools.partial(query_kernel, block_rows, heads), out_sh...  4.87 us
    unnamed x10, local copies, waits for them, and re-layouts  3.16 us
  transfers between devices with their start and end apart: 13, of which 10 were waited for; matrix products, arithmetic and copies ran while one was open for 0% of the time, Pallas kernels for 8%

profile of v3, /device:TPU:0, one launch (start us, length us, event | category | flops | bytes accessed | tf_op | source)
XLA Modules:
  0.0 80.9 jit_solution(640727467186548405)
XLA Ops:
  0.6 4.0 %collective-permute-start = (bf16[224,576]{1,0:T(8,128)(2,1)}, bf16[224,576]{1,0:T(8,128)(2,1)S(1)}, u32[]{:S(2)}, u32[]{:S(2)}) collective-permute-start(bf16[224,576]{1,0:T(8,128)(2,1)} %rest_4_.1), channel_id=1, source_target_pairs={{0,24},{4,28},{8,16},{12,20},{16,8},{20,12},{24,0},{28,4},{1,25},{... | collective-permute-start | bytes 774152 | tf_op jit(solution)/shard_map/ppermute | solution.py:340
  4.6 0.5 collective-permute-start.2
  5.1 0.1 collective-permute-start.4
  5.2 0.0 collective-permute-start.1
  5.2 0.0 copy-start
  5.2 1.5 %copy-done = bf16[224,8,512]{2,1,0:T(8,128)(2,1)S(1)} copy-done((bf16[224,8,512]{2,1,0:T(8,128)(2,1)S(1)}, bf16[224,8,512]{2,1,0:T(8,128)(2,1)}, u32[]{:S(2)}) %copy-start) | copy-done | bytes 1835032
  6.7 0.0 copy-start.2
  6.7 1.6 %copy-done.2 = bf16[224,8,576]{2,1,0:T(8,128)(2,1)S(1)} copy-done((bf16[224,8,576]{2,1,0:T(8,128)(2,1)S(1)}, bf16[224,8,576]{2,1,0:T(8,128)(2,1)}, u32[]{:S(2)}) %copy-start.2) | copy-done | bytes 2064408
  8.4 0.0 copy-start.1
  8.4 0.0 copy-start.3
  8.4 0.0 copy-start.4
  8.4 1.3 %row_layouts.1 = (bf16[1792,640]{1,0:T(8,128)(2,1)S(1)}, bf16[2,576,896]{2,1,0:T(8,128)(2,1)S(1)}, bf16[2,512,896]{2,1,0:T(8,128)(2,1)S(1)}) custom-call(bf16[1792,576]{1,0:T(8,128)(2,1)S(1)} %bitcast.11, bf16[1792,512]{1,0:T(8,128)(2,1)S(1)} %bitcast.9), custom_call_target="tpu_custom_call" | custom-call | tf_op jit(solution)/shard_map/row_layouts/pallas_call | solution.py:244
  9.7 2.8 %collective-permute-done.rest_10_ = bf16[224,576]{1,0:T(8,128)(2,1)S(1)} collective-permute-done((bf16[224,576]{1,0:T(8,128)(2,1)}, bf16[224,576]{1,0:T(8,128)(2,1)S(1)}, u32[]{:S(2)}, u32[]{:S(2)}) %collective-permute-start) | collective-permute-done | bytes 258080 | tf_op jit(solution)/shard_map/ppermute | solution.py:340
  12.5 0.0 collective-permute-start.6
  12.5 5.6 %collective-permute-done.2.rest_6_ = bf16[224,576]{1,0:T(8,128)(2,1)S(1)} collective-permute-done((bf16[224,576]{1,0:T(8,128)(2,1)}, bf16[224,576]{1,0:T(8,128)(2,1)S(1)}, u32[]{:S(2)}, u32[]{:S(2)}) %collective-permute-start.2) | collective-permute-done | bytes 258080 | tf_op jit(solution)/shard_map/ppermute | solution.py:340
  18.1 0.0 collective-permute-start.3
  18.1 0.0 collective-permute-done.4.rest_8_
  18.1 0.5 collective-permute-start.5
  18.6 0.0 collective-permute-done.1.rest_5_
  18.6 0.0 collective-permute-done.6.rest_11_
  18.6 1.1 %collective-permute-done.3.rest_7_ = bf16[224,576]{1,0:T(8,128)(2,1)S(1)} collective-permute-done((bf16[224,576]{1,0:T(8,128)(2,1)S(1)}, bf16[224,576]{1,0:T(8,128)(2,1)S(1)}, u32[]{:S(2)}, u32[]{:S(2)}) %collective-permute-start.3) | collective-permute-done | bytes 258080 | tf_op jit(solution)/shard_map/ppermute | solution.py:340
  19.6 0.4 collective-permute-done.5.rest_9_
  20.1 0.0 copy-done.1
  20.1 0.0 copy-done.3
  20.1 0.0 copy-done.4
  20.1 10.2 %attention_backward.1 = (bf16[4,224,640]{2,1,0:T(8,128)(2,1)S(1)}, bf16[4,224,640]{2,1,0:T(8,128)(2,1)S(1)}, bf16[1792,640]{1,0:T(8,128)(2,1)S(1)}, bf16[7,896,2...) custom-call(s32[16]{0:T(128)S(1)} %copy-done.4, bf16[1792,640]{1,0:T(8,128)(2,1)S(1)} %get-tuple-element.23.rest_0_, ...), custom_call_target="tpu_custom_call" | custom-call | tf_op jit(solution)/shard_map/attention_backward/pallas_call | solution.py:325
  30.2 6.2 %collective-permute-start.7 = (bf16[4,224,640]{2,1,0:T(8,128)(2,1)S(1)}, bf16[4,224,640]{2,1,0:T(8,128)(2,1)S(1)}, u32[]{:S(2)}, u32[]{:S(2)}) collective-permute-start(bf16[4,224,640]{2,1,0:T(8,128)(2,1)S(1)} %get-tuple-element.28), channel_id=1, source_target_pairs={{0,4},{4,0},{8,12},{12,8},{16,20},{20,16},{24,28},{28,24},{1,5},{5... | collective-permute-start | bytes 3440648 | tf_op jit(solution)/shard_map/ppermute | solution.py:340
  36.4 2.4 %collective-permute-done.7 = bf16[4,224,640]{2,1,0:T(8,128)(2,1)S(1)} collective-permute-done((bf16[4,224,640]{2,1,0:T(8,128)(2,1)S(1)}, bf16[4,224,640]{2,1,0:T(8,128)(2,1)S(1)}, u32[]{:S(2)}, u32[]{:S(2)}) %collective-permute-start.7) | collective-permute-done | bytes 1146912 | tf_op jit(solution)/shard_map/ppermute | solution.py:340
  38.8 0.2 convert_add_fusion
  39.0 0.1 slice.56
  39.1 6.0 %collective-permute-start.8 = (bf16[2,224,640]{2,1,0:T(8,128)(2,1)S(1)}, bf16[2,224,640]{2,1,0:T(8,128)(2,1)S(1)}, u32[]{:S(2)}, u32[]{:S(2)}) collective-permute-start(bf16[2,224,640]{2,1,0:T(8,128)(2,1)S(1)} %slice.56), channel_id=1, source_target_pairs={{0,16},{4,12},{8,24},{12,4},{16,0},{20,28},{24,8},{28,20},{1,17},{... | collective-permute-start | bytes 1720328 | tf_op jit(solution)/shard_map/ppermute | solution.py:393
  45.2 4.9 %query_gradient.1 = bf16[1792,576]{1,0:T(8,128)(2,1)} custom-call(s32[16]{0:T(128)S(1)} %copy-done.4, bf16[1792,640]{1,0:T(8,128)(2,1)S(1)} %get-tuple-element.33.keys, bf16[7,896,256]{2,1,0:T(8,128)(2,1)S(1)} %get-tuple-element.34.ds0, bf16[7,896,256]{2,1,0:T(8,128)(2,1)S(1)} %get-tuple-element.35.ds1), custom_call_target="tpu_custom_call" | custom-call | flops 3699376128 | tf_op jit(solution)/shard_map/query_gradient/pallas_call | solution.py:277
  50.0 2.8 %collective-permute-done.8 = bf16[2,224,640]{2,1,0:T(8,128)(2,1)S(1)} collective-permute-done((bf16[2,224,640]{2,1,0:T(8,128)(2,1)S(1)}, bf16[2,224,640]{2,1,0:T(8,128)(2,1)S(1)}, u32[]{:S(2)}, u32[]{:S(2)}) %collective-permute-start.8) | collective-permute-done | bytes 573472 | tf_op jit(solution)/shard_map/ppermute | solution.py:393
  52.8 0.1 convert_add_fusion.1
  53.0 4.2 %collective-permute-start.9 = (bf16[1,224,640]{2,1,0:T(8,128)(2,1)S(1)}, bf16[1,224,640]{2,1,0:T(8,128)(2,1)S(1)}, u32[]{:S(2)}, u32[]{:S(2)}) collective-permute-start(bf16[1,224,640]{2,1,0:T(8,128)(2,1)S(1)} %slice.57), channel_id=1, source_target_pairs={{0,8},{4,20},{8,0},{12,28},{16,24},{20,4},{24,16},{28,12},{1,9},{5... | collective-permute-start | bytes 860168 | tf_op jit(solution)/shard_map/ppermute | solution.py:393
  57.2 4.6 %collective-permute-done.9 = bf16[1,224,640]{2,1,0:T(8,128)(2,1)S(1)} collective-permute-done((bf16[1,224,640]{2,1,0:T(8,128)(2,1)S(1)}, bf16[1,224,640]{2,1,0:T(8,128)(2,1)S(1)}, u32[]{:S(2)}, u32[]{:S(2)}) %collective-permute-start.9) | collective-permute-done | bytes 286752 | tf_op jit(solution)/shard_map/ppermute | solution.py:393
  61.8 0.1 slice_add_fusion
  61.9 1.6 %collective-permute-start.10 = (bf16[112,640]{1,0:T(8,128)(2,1)S(1)}, bf16[112,640]{1,0:T(8,128)(2,1)S(1)}, u32[]{:S(2)}, u32[]{:S(2)}) collective-permute-start(bf16[112,640]{1,0:T(8,128)(2,1)S(1)} %fusion.2), channel_id=1, source_target_pairs={{0,1},{1,0},{2,3},{3,2},{4,5},{5,4},{6,7},{7,6},{8,9},{9,8},{10,11... | collective-permute-start | bytes 430088 | tf_op jit(solution)/shard_map/ppermute | solution.py:340
  63.5 3.5 %collective-permute-done.10 = bf16[112,640]{1,0:T(8,128)(2,1)S(1)} collective-permute-done((bf16[112,640]{1,0:T(8,128)(2,1)S(1)}, bf16[112,640]{1,0:T(8,128)(2,1)S(1)}, u32[]{:S(2)}, u32[]{:S(2)}) %collective-permute-start.10) | collective-permute-done | bytes 143392 | tf_op jit(solution)/shard_map/ppermute | solution.py:340
  67.1 2.7 %collective-permute-start.11 = (bf16[112,640]{1,0:T(8,128)(2,1)S(1)}, bf16[112,640]{1,0:T(8,128)(2,1)S(1)}, u32[]{:S(2)}, u32[]{:S(2)}) collective-permute-start(bf16[112,640]{1,0:T(8,128)(2,1)S(1)} %fusion.1), channel_id=1, source_target_pairs={{0,2},{1,3},{2,0},{3,1},{4,6},{5,7},{6,4},{7,5},{8,10},{9,11},{10,... | collective-permute-start | bytes 430088 | tf_op jit(solution)/shard_map/ppermute | solution.py:340
  69.8 5.1 %collective-permute-done.11 = bf16[112,640]{1,0:T(8,128)(2,1)S(1)} collective-permute-done((bf16[112,640]{1,0:T(8,128)(2,1)S(1)}, bf16[112,640]{1,0:T(8,128)(2,1)S(1)}, u32[]{:S(2)}, u32[]{:S(2)}) %collective-permute-start.11) | collective-permute-done | bytes 143392 | tf_op jit(solution)/shard_map/ppermute | solution.py:340
  74.8 0.6 collective-permute-start.12
  75.5 4.5 %collective-permute-done.12 = bf16[112,640]{1,0:T(8,128)(2,1)S(1)} collective-permute-done((bf16[112,640]{1,0:T(8,128)(2,1)S(1)}, bf16[112,640]{1,0:T(8,128)(2,1)S(1)}, u32[]{:S(2)}, u32[]{:S(2)}) %collective-permute-start.12) | collective-permute-done | bytes 143392 | tf_op jit(solution)/shard_map/ppermute | solution.py:340
  80.1 0.8 %fusion = f32[224,576]{1,0:T(8,128)} fusion(bf16[112,640]{1,0:T(8,128)(2,1)S(1)} %get-tuple-element.39, bf16[112,640]{1,0:T(8,128)(2,1)S(1)} %get-tuple-element.38), kind=kLoop, calls=%fused_computation.6 | loop fusion | flops 516096 | bytes 802816 | tf_op jit(solution)/shard_map/slice | solution.py:399
  (5 shorter events, 0.2 us)
Async XLA Ops:
  0.6 11.9 %collective-permute-start = (bf16[224,576]{1,0:T(8,128)(2,1)}, bf16[224,576]{1,0:T(8,128)(2,1)S(1)}, u32[]{:S(2)}, u32[]{:S(2)}) collective-permute-start(bf16[224,576]{1,0:T(8,128)(2,1)} %rest_4_.1), channel_id=1, source_target_pairs={{0,24},{4,28},{8,16},{12,20},{16,8},{20,12},{24,0},{28,4},{1,25},{... | collective-permute-start | bytes 774152 | tf_op jit(solution)/shard_map/ppermute | solution.py:340
  4.6 13.5 %collective-permute-start.2 = (bf16[224,576]{1,0:T(8,128)(2,1)}, bf16[224,576]{1,0:T(8,128)(2,1)S(1)}, u32[]{:S(2)}, u32[]{:S(2)}) collective-permute-start(bf16[224,576]{1,0:T(8,128)(2,1)} %rest_4_.1), channel_id=1, source_target_pairs={{0,8},{4,12},{8,0},{12,4},{16,24},{20,28},{24,16},{28,20},{1,9},{5... | collective-permute-start | bytes 774152 | tf_op jit(solution)/shard_map/ppermute | solution.py:340
  5.1 12.9 %collective-permute-start.4 = (bf16[224,576]{1,0:T(8,128)(2,1)}, bf16[224,576]{1,0:T(8,128)(2,1)S(1)}, u32[]{:S(2)}, u32[]{:S(2)}) collective-permute-start(bf16[224,576]{1,0:T(8,128)(2,1)} %rest_4_.1), channel_id=1, source_target_pairs={{0,16},{4,20},{8,24},{12,28},{16,0},{20,4},{24,8},{28,12},{1,17},{... | collective-permute-start | bytes 774152 | tf_op jit(solution)/shard_map/ppermute | solution.py:340
  5.2 13.4 %collective-permute-start.1 = (bf16[224,576]{1,0:T(8,128)(2,1)}, bf16[224,576]{1,0:T(8,128)(2,1)S(1)}, u32[]{:S(2)}, u32[]{:S(2)}) collective-permute-start(bf16[224,576]{1,0:T(8,128)(2,1)} %rest_4_.1), channel_id=1, source_target_pairs={{0,4},{4,0},{8,12},{12,8},{16,20},{20,16},{24,28},{28,24},{1,5},{5... | collective-permute-start | bytes 774152 | tf_op jit(solution)/shard_map/ppermute | solution.py:340
  5.2 1.5 %copy-start = (bf16[224,8,512]{2,1,0:T(8,128)(2,1)S(1)}, bf16[224,8,512]{2,1,0:T(8,128)(2,1)}, u32[]{:S(2)}) copy-start(bf16[224,8,512]{2,1,0:T(8,128)(2,1)} %param.7) | copy-start | bytes 5505028
  6.7 1.6 %copy-start.2 = (bf16[224,8,576]{2,1,0:T(8,128)(2,1)S(1)}, bf16[224,8,576]{2,1,0:T(8,128)(2,1)}, u32[]{:S(2)}) copy-start(bf16[224,8,576]{2,1,0:T(8,128)(2,1)} %param.5) | copy-start | bytes 6193156
  8.4 11.7 %copy-start.1 = (bf16[224,8,512]{2,1,0:T(8,128)(2,1)S(1)}, bf16[224,8,512]{2,1,0:T(8,128)(2,1)}, u32[]{:S(2)}) copy-start(bf16[224,8,512]{2,1,0:T(8,128)(2,1)} %param.7) | copy-start | bytes 5505028
  8.4 11.7 %copy-start.3 = (bf16[224,576]{1,0:T(8,128)(2,1)S(1)}, bf16[224,576]{1,0:T(8,128)(2,1)}, u32[]{:S(2)}) copy-start(bf16[224,576]{1,0:T(8,128)(2,1)} %rest_4_.1) | copy-start | bytes 774148
  8.4 11.7 %copy-start.4 = (s32[16]{0:T(128)S(1)}, s32[16]{0:T(128)}, u32[]{:S(2)}) copy-start(s32[16]{0:T(128)} %order_ref.3) | copy-start | bytes 196
  12.5 6.1 %collective-permute-start.6 = (bf16[224,576]{1,0:T(8,128)(2,1)S(1)}, bf16[224,576]{1,0:T(8,128)(2,1)S(1)}, u32[]{:S(2)}, u32[]{:S(2)}) collective-permute-start(bf16[224,576]{1,0:T(8,128)(2,1)S(1)} %collective-permute-done.rest_10_), channel_id=1, source_target_pairs={{0,4},{4,0},{8,12},{12,8},{16,20},{20,16},{24,28},{28,24},{1,5},{5... | collective-permute-start | bytes 774152 | tf_op jit(solution)/shard_map/ppermute | solution.py:340
  18.1 1.6 %collective-permute-start.3 = (bf16[224,576]{1,0:T(8,128)(2,1)S(1)}, bf16[224,576]{1,0:T(8,128)(2,1)S(1)}, u32[]{:S(2)}, u32[]{:S(2)}) collective-permute-start(bf16[224,576]{1,0:T(8,128)(2,1)S(1)} %collective-permute-done.2.rest_6_), channel_id=1, source_target_pairs={{0,4},{4,0},{8,12},{12,8},{16,20},{20,16},{24,28},{28,24},{1,5},{5... | collective-permute-start | bytes 774152 | tf_op jit(solution)/shard_map/ppermute | solution.py:340
  18.1 2.0 %collective-permute-start.5 = (bf16[224,576]{1,0:T(8,128)(2,1)S(1)}, bf16[224,576]{1,0:T(8,128)(2,1)S(1)}, u32[]{:S(2)}, u32[]{:S(2)}) collective-permute-start(bf16[224,576]{1,0:T(8,128)(2,1)S(1)} %collective-permute-done.4.rest_8_), channel_id=1, source_target_pairs={{0,4},{4,0},{8,12},{12,8},{16,20},{20,16},{24,28},{28,24},{1,5},{5... | collective-permute-start | bytes 774152 | tf_op jit(solution)/shard_map/ppermute | solution.py:340
  30.2 8.6 %collective-permute-start.7 = (bf16[4,224,640]{2,1,0:T(8,128)(2,1)S(1)}, bf16[4,224,640]{2,1,0:T(8,128)(2,1)S(1)}, u32[]{:S(2)}, u32[]{:S(2)}) collective-permute-start(bf16[4,224,640]{2,1,0:T(8,128)(2,1)S(1)} %get-tuple-element.28), channel_id=1, source_target_pairs={{0,4},{4,0},{8,12},{12,8},{16,20},{20,16},{24,28},{28,24},{1,5},{5... | collective-permute-start | bytes 3440648 | tf_op jit(solution)/shard_map/ppermute | solution.py:340
  39.1 13.7 %collective-permute-start.8 = (bf16[2,224,640]{2,1,0:T(8,128)(2,1)S(1)}, bf16[2,224,640]{2,1,0:T(8,128)(2,1)S(1)}, u32[]{:S(2)}, u32[]{:S(2)}) collective-permute-start(bf16[2,224,640]{2,1,0:T(8,128)(2,1)S(1)} %slice.56), channel_id=1, source_target_pairs={{0,16},{4,12},{8,24},{12,4},{16,0},{20,28},{24,8},{28,20},{1,17},{... | collective-permute-start | bytes 1720328 | tf_op jit(solution)/shard_map/ppermute | solution.py:393
  53.0 8.8 %collective-permute-start.9 = (bf16[1,224,640]{2,1,0:T(8,128)(2,1)S(1)}, bf16[1,224,640]{2,1,0:T(8,128)(2,1)S(1)}, u32[]{:S(2)}, u32[]{:S(2)}) collective-permute-start(bf16[1,224,640]{2,1,0:T(8,128)(2,1)S(1)} %slice.57), channel_id=1, source_target_pairs={{0,8},{4,20},{8,0},{12,28},{16,24},{20,4},{24,16},{28,12},{1,9},{5... | collective-permute-start | bytes 860168 | tf_op jit(solution)/shard_map/ppermute | solution.py:393
  61.9 5.2 %collective-permute-start.10 = (bf16[112,640]{1,0:T(8,128)(2,1)S(1)}, bf16[112,640]{1,0:T(8,128)(2,1)S(1)}, u32[]{:S(2)}, u32[]{:S(2)}) collective-permute-start(bf16[112,640]{1,0:T(8,128)(2,1)S(1)} %fusion.2), channel_id=1, source_target_pairs={{0,1},{1,0},{2,3},{3,2},{4,5},{5,4},{6,7},{7,6},{8,9},{9,8},{10,11... | collective-permute-start | bytes 430088 | tf_op jit(solution)/shard_map/ppermute | solution.py:340
  67.1 7.7 %collective-permute-start.11 = (bf16[112,640]{1,0:T(8,128)(2,1)S(1)}, bf16[112,640]{1,0:T(8,128)(2,1)S(1)}, u32[]{:S(2)}, u32[]{:S(2)}) collective-permute-start(bf16[112,640]{1,0:T(8,128)(2,1)S(1)} %fusion.1), channel_id=1, source_target_pairs={{0,2},{1,3},{2,0},{3,1},{4,6},{5,7},{6,4},{7,5},{8,10},{9,11},{10,... | collective-permute-start | bytes 430088 | tf_op jit(solution)/shard_map/ppermute | solution.py:340
  74.8 5.2 %collective-permute-start.12 = (bf16[112,640]{1,0:T(8,128)(2,1)S(1)}, bf16[112,640]{1,0:T(8,128)(2,1)S(1)}, u32[]{:S(2)}, u32[]{:S(2)}) collective-permute-start(bf16[112,640]{1,0:T(8,128)(2,1)S(1)} %add_convert_fusion), channel_id=1, source_target_pairs={{0,1},{1,0},{2,3},{3,2},{4,5},{5,4},{6,7},{7,6},{8,9},{9,8},{10,11... | collective-permute-start | bytes 430088 | tf_op jit(solution)/shard_map/ppermute | solution.py:340

commit v4 on v3

--- a/solution.py
+++ b/solution.py
@@ -69,15 +69,13 @@
 def attention_kernel(direct, ctx_size, block_rows, heads, latent, width, order_ref, *rest):
     q, do, qt, dot = rest[:4]
     key_refs = rest[4 : 4 + ctx_size]
-    keep_ref, send_ref = rest[4 + ctx_size : 6 + ctx_size]
+    outs = rest[4 + ctx_size : 8 + ctx_size]
+    rest = rest[8 + ctx_size :]
     if direct:
-        keys, *ds_refs = rest[6 + ctx_size : 9 + ctx_size]
-        stage, probs, gprobs, marks, peak, total, weighted, dkt = rest[9 + ctx_size :]
+        keys, *ds_refs = rest[:3]
+        stage, probs, gprobs, marks, peak, total, weighted, dkt = rest[3:]
     else:
-        dq_ref = rest[6 + ctx_size]
-        stage, probs, gprobs, marks, peak, total, weighted, dkt, keys, dq_acc, move_sem = rest[
-            7 + ctx_size :
-        ]
+        dq_ref, stage, probs, gprobs, marks, peak, total, weighted, dkt, keys, dq_acc, move_sem = rest
     seq = keys.shape[0]
     tiles = seq // tile
     rows = block_rows * heads
@@ -230,10 +228,11 @@
         masks = [chip_mask(label, c, ctx_size) for c in range(2)]
         kept = jnp.where(core == 0, masks[0], masks[1])
         sent = jnp.where(core == 0, masks[1], masks[0]) + 1
-        for mask, out in ((kept, keep_ref), (sent, send_ref)):
+        upper, slot = divmod(label, ctx_size // 4)
+        for mask, out in ((kept, outs[upper]), (sent, outs[2 + upper])):
             for sub in range(2):
                 source = stage.at[sorted_rows(mask, sub), :]
-                leaving.append((source, out.at[label, sub_rows(sub), :]))
+                leaving.append((source, out.at[slot, sub_rows(sub), :]))
     move(leaving)
 
 
@@ -294,7 +293,6 @@
     latent = do.shape[1]
     rows = block_rows * heads
     seq = 2 * block_rows * ctx_size
-    half = ctx_size // 2
     tiles = seq // tile
     vmem = pl.BlockSpec(memory_space=pltpu.VMEM)
     f32, bf16 = jnp.float32, jnp.bfloat16
@@ -309,7 +307,7 @@
         ((rows, lanes), f32),
         ((tiles, width, tile), f32),
     ]
-    out_shape = [jax.ShapeDtypeStruct((half, 2 * block_rows, wide), bf16)] * 2
+    out_shape = [jax.ShapeDtypeStruct((ctx_size // 4, 2 * block_rows, wide), bf16)] * 4
     if direct:
         out_shape += [
             jax.ShapeDtypeStruct((seq, wide), bf16),
@@ -326,7 +324,7 @@
         functools.partial(attention_kernel, direct, ctx_size, block_rows, heads, latent, width),
         out_shape=tuple(out_shape),
         in_specs=[pl.BlockSpec(memory_space=pltpu.SMEM)] + [vmem] * 4 + [blocks] * ctx_size,
-        out_specs=(blocks, blocks) + (vmem,) * (len(out_shape) - 2),
+        out_specs=(blocks,) * 4 + (vmem,) * (len(out_shape) - 4),
         scratch_shapes=[pltpu.VMEM(shape, dtype) for shape, dtype in buffers] + scratch,
         compiler_params=pltpu.CompilerParams(
             vmem_limit_bytes=(32 if direct else 63) * mebibyte
@@ -377,25 +375,32 @@
     key_list = []
     for block in same_core:
         key_list += [block, swap(block, "ctx", 1)]
-    keep, send, *found = attention(
+    low, high, low_sent, high_sent, *found = attention(
         block_order, qp, grad_rows, qt, dot, key_list, block_rows, head_count, key_width, direct
     )
-    sums = keep.astype(jnp.float32) + swap(send, "ctx", 1).astype(jnp.float32)
+
+    def exchange(sums):
+        step = sums.shape[0].bit_length() - 1
+        pairs = [(i, i ^ chip_axes(i % 2, ctx_size)[step]) for i in range(ctx_size)]
+        return lax.ppermute(sums.astype(jnp.bfloat16), "ctx", pairs).astype(jnp.float32)
+
+    def both_cores(kept, sent):
+        return kept.astype(jnp.float32) + swap(sent, "ctx", 1).astype(jnp.float32)
+
+    high = both_cores(high, high_sent).astype(jnp.bfloat16)
+    high, low, low_sent, *found = lax.optimization_barrier((high, low, low_sent, *found))
+    arrived = exchange(high)
+    sums = both_cores(low, low_sent)
+    grad_query = found[0]
     if direct:
-        sums, *found = lax.optimization_barrier((sums, *found))
         grad_query = query_gradient(block_order, *found, block_rows, head_count, key_width)
-    else:
-        grad_query = found[0]
+        arrived, grad_query = lax.optimization_barrier((arrived, grad_query))
+    grad_queries = grad_query.reshape(token_count, head_count, key_width)
+    sums = sums + arrived
     while sums.shape[0] > 1:
         half = sums.shape[0] // 2
-        step = half.bit_length() - 1
-        pairs = [(i, i ^ chip_axes(i % 2, ctx_size)[step]) for i in range(ctx_size)]
-        arrived = lax.ppermute(sums[half:].astype(jnp.bfloat16), "ctx", pairs)
-        if direct and sums.shape[0] == ctx_size // 2:
-            arrived, grad_query = lax.optimization_barrier((arrived, grad_query))
-        sums = sums[:half] + arrived.astype(jnp.float32)
+        sums = sums[:half] + exchange(sums[half:])
     own = sums[0]
-    grad_queries = grad_query.reshape(token_count, head_count, key_width)
     return (grad_queries, sum_over_heads(own)[:, :key_width])
 
 

time: 81.1 us -> 81.1 us (level)
  starting transfers between devices: 26.4 us -> 18.2 us
  Pallas kernels: 16.3 us -> 24.3 us
  waiting for transfers between devices: 32.8 us -> 33.8 us
    ppermute x2, starting transfers between devices: 10.2 us -> 0.14 us  [exchange(): lax.ppermute(sums.astype(jnp.bfloat16), 'ctx', pairs).astype(jnp.float32)]
    pallas_call x1, Pallas kernels: 10.2 us -> 16.3 us  [attention(): pl.pallas_call(functools.partial(attention_kernel, direct, ctx_size, bloc...]
    ppermute x11 -> x12, starting transfers between devices: 16.2 us -> 18.1 us  [swap(): return lax.ppermute(x, axis, [(i, i ^ mask) for i in range(size)])]
    pallas_call x1, Pallas kernels: 4.87 us -> 6.66 us  [query_gradient(): pl.pallas_call(functools.partial(query_kernel, block_rows, heads), out_sh...]
    ppermute x2, waiting for transfers between devices: 7.44 us -> 9.21 us  [exchange(): lax.ppermute(sums.astype(jnp.bfloat16), 'ctx', pairs).astype(jnp.float32)]
    ppermute x11 -> x12, waiting for transfers between devices: 25.4 us -> 24.5 us  [swap(): return lax.ppermute(x, axis, [(i, i ^ mask) for i in range(size)])]
  transfers between devices with their start and end apart: 13 -> 14, of which waited for: 10 -> 10; matrix products, arithmetic and copies ran while one was open for 0% -> 0% of each run, Pallas kernels for 8% -> 10%
where the time goes in v4:
time: 81.1 us; the launch traced here: 81.6 us
  waiting for transfers between devices  33.8 us (42%)
  Pallas kernels  24.3 us (30%)
  starting transfers between devices  18.2 us (22%)
  local copies, waits for them, and re-layouts  3.19 us (4%)
  other arithmetic  1.43 us (2%)
    ppermute x12, waiting for transfers between devices, swap(): return lax.ppermute(x, axis, [(i, i ^ mask) for i in range(size)])  24.5 us
    ppermute x12, starting transfers between devices, swap(): return lax.ppermute(x, axis, [(i, i ^ mask) for i in range(size)])  18.1 us
    pallas_call x1, Pallas kernels, attention(): pl.pallas_call(functools.partial(attention_kernel, direct, ctx_size, bloc...  16.3 us
    ppermute x2, waiting for transfers between devices, exchange(): lax.ppermute(sums.astype(jnp.bfloat16), 'ctx', pairs).astype(jnp.float32)  9.21 us
    pallas_call x1, Pallas kernels, query_gradient(): pl.pallas_call(functools.partial(query_kernel, block_rows, heads), out_sh...  6.66 us
    unnamed x10, local copies, waits for them, and re-layouts  3.16 us
  transfers between devices with their start and end apart: 14, of which 10 were waited for; matrix products, arithmetic and copies ran while one was open for 0% of the time, Pallas kernels for 10%

profile of v4, /device:TPU:0, one launch (start us, length us, event | category | flops | bytes accessed | tf_op | source)
XLA Modules:
  0.0 81.6 jit_solution(12564649893213593639)
XLA Ops:
  0.6 4.0 %collective-permute-start = (bf16[224,576]{1,0:T(8,128)(2,1)}, bf16[224,576]{1,0:T(8,128)(2,1)S(1)}, u32[]{:S(2)}, u32[]{:S(2)}) collective-permute-start(bf16[224,576]{1,0:T(8,128)(2,1)} %rest_4_.1), channel_id=1, source_target_pairs={{0,24},{4,28},{8,16},{12,20},{16,8},{20,12},{24,0},{28,4},{1,25},{... | collective-permute-start | bytes 774152 | tf_op jit(solution)/shard_map/ppermute | solution.py:338
  4.6 0.5 collective-permute-start.2
  5.1 0.1 collective-permute-start.4
  5.2 0.0 collective-permute-start.1
  5.2 0.0 copy-start
  5.2 1.5 %copy-done = bf16[224,8,512]{2,1,0:T(8,128)(2,1)S(1)} copy-done((bf16[224,8,512]{2,1,0:T(8,128)(2,1)S(1)}, bf16[224,8,512]{2,1,0:T(8,128)(2,1)}, u32[]{:S(2)}) %copy-start) | copy-done | bytes 1835032
  6.7 0.0 copy-start.2
  6.7 1.6 %copy-done.2 = bf16[224,8,576]{2,1,0:T(8,128)(2,1)S(1)} copy-done((bf16[224,8,576]{2,1,0:T(8,128)(2,1)S(1)}, bf16[224,8,576]{2,1,0:T(8,128)(2,1)}, u32[]{:S(2)}) %copy-start.2) | copy-done | bytes 2064408
  8.4 0.0 copy-start.1
  8.4 0.0 copy-start.3
  8.4 0.0 copy-start.4
  8.4 1.3 %row_layouts.1 = (bf16[1792,640]{1,0:T(8,128)(2,1)S(1)}, bf16[2,576,896]{2,1,0:T(8,128)(2,1)S(1)}, bf16[2,512,896]{2,1,0:T(8,128)(2,1)S(1)}) custom-call(bf16[1792,576]{1,0:T(8,128)(2,1)S(1)} %bitcast.11, bf16[1792,512]{1,0:T(8,128)(2,1)S(1)} %bitcast.9), custom_call_target="tpu_custom_call" | custom-call | tf_op jit(solution)/shard_map/row_layouts/pallas_call | solution.py:243
  9.7 2.8 %collective-permute-done.rest_10_ = bf16[224,576]{1,0:T(8,128)(2,1)S(1)} collective-permute-done((bf16[224,576]{1,0:T(8,128)(2,1)}, bf16[224,576]{1,0:T(8,128)(2,1)S(1)}, u32[]{:S(2)}, u32[]{:S(2)}) %collective-permute-start) | collective-permute-done | bytes 258080 | tf_op jit(solution)/shard_map/ppermute | solution.py:338
  12.5 0.0 collective-permute-start.6
  12.5 5.6 %collective-permute-done.2.rest_6_ = bf16[224,576]{1,0:T(8,128)(2,1)S(1)} collective-permute-done((bf16[224,576]{1,0:T(8,128)(2,1)}, bf16[224,576]{1,0:T(8,128)(2,1)S(1)}, u32[]{:S(2)}, u32[]{:S(2)}) %collective-permute-start.2) | collective-permute-done | bytes 258080 | tf_op jit(solution)/shard_map/ppermute | solution.py:338
  18.1 0.0 collective-permute-start.3
  18.1 0.0 collective-permute-done.4.rest_8_
  18.1 0.5 collective-permute-start.5
  18.6 0.0 collective-permute-done.1.rest_5_
  18.6 0.0 collective-permute-done.6.rest_11_
  18.6 1.1 %collective-permute-done.3.rest_7_ = bf16[224,576]{1,0:T(8,128)(2,1)S(1)} collective-permute-done((bf16[224,576]{1,0:T(8,128)(2,1)S(1)}, bf16[224,576]{1,0:T(8,128)(2,1)S(1)}, u32[]{:S(2)}, u32[]{:S(2)}) %collective-permute-start.3) | collective-permute-done | bytes 258080 | tf_op jit(solution)/shard_map/ppermute | solution.py:338
  19.6 0.4 collective-permute-done.5.rest_9_
  20.1 0.0 copy-done.1
  20.1 0.0 copy-done.3
  20.1 0.0 copy-done.4
  20.1 16.3 %attention_backward.1 = (bf16[2,224,640]{2,1,0:T(8,128)(2,1)S(1)}, bf16[2,224,640]{2,1,0:T(8,128)(2,1)S(1)}, bf16[2,224,640]{2,1,0:T(8,128)(2,1)S(1)}, bf16[2,22...) custom-call(s32[16]{0:T(128)S(1)} %copy-done.4, ...), custom_call_target="tpu_custom_call" | custom-call | tf_op jit(solution)/shard_map/attention_backward/pallas_call | solution.py:323
  36.4 7.6 %collective-permute-start.7 = (bf16[2,224,640]{2,1,0:T(8,128)(2,1)S(1)}, bf16[2,224,640]{2,1,0:T(8,128)(2,1)S(1)}, u32[]{:S(2)}, u32[]{:S(2)}) collective-permute-start(bf16[2,224,640]{2,1,0:T(8,128)(2,1)S(1)} %get-tuple-element.32), channel_id=1, source_target_pairs={{0,4},{4,0},{8,12},{12,8},{16,20},{20,16},{24,28},{28,24},{1,5},{5... | collective-permute-start | bytes 1720328 | tf_op jit(solution)/shard_map/ppermute | solution.py:338
  44.0 1.6 %collective-permute-done.7 = bf16[2,224,640]{2,1,0:T(8,128)(2,1)S(1)} collective-permute-done((bf16[2,224,640]{2,1,0:T(8,128)(2,1)S(1)}, bf16[2,224,640]{2,1,0:T(8,128)(2,1)S(1)}, u32[]{:S(2)}, u32[]{:S(2)}) %collective-permute-start.7) | collective-permute-done | bytes 573472 | tf_op jit(solution)/shard_map/ppermute | solution.py:338
  45.6 0.1 add_convert_fusion
  45.7 0.1 collective-permute-start.8
  45.8 0.4 collective-permute-start.9
  46.2 6.7 %query_gradient.1 = bf16[1792,576]{1,0:T(8,128)(2,1)} custom-call(s32[16]{0:T(128)S(1)} %copy-done.4, bf16[1792,640]{1,0:T(8,128)(2,1)S(1)} %get-tuple-element.39.keys, bf16[7,896,256]{2,1,0:T(8,128)(2,1)S(1)} %get-tuple-element.40.ds0, bf16[7,896,256]{2,1,0:T(8,128)(2,1)S(1)} %get-tuple-element.41.ds1), custom_call_target="tpu_custom_call" | custom-call | flops 3699376128 | tf_op jit(solution)/shard_map/query_gradient/pallas_call | solution.py:276
  52.9 2.6 %collective-permute-done.8 = bf16[2,224,640]{2,1,0:T(8,128)(2,1)S(1)} collective-permute-done((bf16[2,224,640]{2,1,0:T(8,128)(2,1)S(1)}, bf16[2,224,640]{2,1,0:T(8,128)(2,1)S(1)}, u32[]{:S(2)}, u32[]{:S(2)}) %collective-permute-start.8) | collective-permute-done | bytes 573472 | tf_op jit(solution)/shard_map/ppermute | solution.py:385
  55.5 0.1 convert_element_type.47
  55.6 0.0 collective-permute-done.9
  55.6 0.2 add_add_fusion
  55.8 0.1 collective-permute-start.10
  55.9 6.6 %collective-permute-done.10 = bf16[1,224,640]{2,1,0:T(8,128)(2,1)S(1)} collective-permute-done((bf16[1,224,640]{2,1,0:T(8,128)(2,1)S(1)}, bf16[1,224,640]{2,1,0:T(8,128)(2,1)S(1)}, u32[]{:S(2)}, u32[]{:S(2)}) %collective-permute-start.10) | collective-permute-done | bytes 286752 | tf_op jit(solution)/shard_map/ppermute | solution.py:385
  62.5 0.1 slice_add_fusion
  62.6 1.6 %collective-permute-start.11 = (bf16[112,640]{1,0:T(8,128)(2,1)S(1)}, bf16[112,640]{1,0:T(8,128)(2,1)S(1)}, u32[]{:S(2)}, u32[]{:S(2)}) collective-permute-start(bf16[112,640]{1,0:T(8,128)(2,1)S(1)} %fusion.2), channel_id=1, source_target_pairs={{0,1},{1,0},{2,3},{3,2},{4,5},{5,4},{6,7},{7,6},{8,9},{9,8},{10,11... | collective-permute-start | bytes 430088 | tf_op jit(solution)/shard_map/ppermute | solution.py:338
  64.2 3.5 %collective-permute-done.11 = bf16[112,640]{1,0:T(8,128)(2,1)S(1)} collective-permute-done((bf16[112,640]{1,0:T(8,128)(2,1)S(1)}, bf16[112,640]{1,0:T(8,128)(2,1)S(1)}, u32[]{:S(2)}, u32[]{:S(2)}) %collective-permute-start.11) | collective-permute-done | bytes 143392 | tf_op jit(solution)/shard_map/ppermute | solution.py:338
  67.8 2.6 %collective-permute-start.12 = (bf16[112,640]{1,0:T(8,128)(2,1)S(1)}, bf16[112,640]{1,0:T(8,128)(2,1)S(1)}, u32[]{:S(2)}, u32[]{:S(2)}) collective-permute-start(bf16[112,640]{1,0:T(8,128)(2,1)S(1)} %fusion.1), channel_id=1, source_target_pairs={{0,2},{1,3},{2,0},{3,1},{4,6},{5,7},{6,4},{7,5},{8,10},{9,11},{10,... | collective-permute-start | bytes 430088 | tf_op jit(solution)/shard_map/ppermute | solution.py:338
  70.5 5.1 %collective-permute-done.12 = bf16[112,640]{1,0:T(8,128)(2,1)S(1)} collective-permute-done((bf16[112,640]{1,0:T(8,128)(2,1)S(1)}, bf16[112,640]{1,0:T(8,128)(2,1)S(1)}, u32[]{:S(2)}, u32[]{:S(2)}) %collective-permute-start.12) | collective-permute-done | bytes 143392 | tf_op jit(solution)/shard_map/ppermute | solution.py:338
  75.6 0.6 collective-permute-start.13
  76.2 4.5 %collective-permute-done.13 = bf16[112,640]{1,0:T(8,128)(2,1)S(1)} collective-permute-done((bf16[112,640]{1,0:T(8,128)(2,1)S(1)}, bf16[112,640]{1,0:T(8,128)(2,1)S(1)}, u32[]{:S(2)}, u32[]{:S(2)}) %collective-permute-start.13) | collective-permute-done | bytes 143392 | tf_op jit(solution)/shard_map/ppermute | solution.py:338
  80.8 0.8 %fusion = f32[224,576]{1,0:T(8,128)} fusion(bf16[112,640]{1,0:T(8,128)(2,1)S(1)} %get-tuple-element.47, bf16[112,640]{1,0:T(8,128)(2,1)S(1)} %get-tuple-element.46), kind=kLoop, calls=%fused_computation.5 | loop fusion | flops 516096 | bytes 802816 | tf_op jit(solution)/shard_map/slice | solution.py:404
  (5 shorter events, 0.2 us)
Async XLA Ops:
  0.6 11.9 %collective-permute-start = (bf16[224,576]{1,0:T(8,128)(2,1)}, bf16[224,576]{1,0:T(8,128)(2,1)S(1)}, u32[]{:S(2)}, u32[]{:S(2)}) collective-permute-start(bf16[224,576]{1,0:T(8,128)(2,1)} %rest_4_.1), channel_id=1, source_target_pairs={{0,24},{4,28},{8,16},{12,20},{16,8},{20,12},{24,0},{28,4},{1,25},{... | collective-permute-start | bytes 774152 | tf_op jit(solution)/shard_map/ppermute | solution.py:338
  4.6 13.5 %collective-permute-start.2 = (bf16[224,576]{1,0:T(8,128)(2,1)}, bf16[224,576]{1,0:T(8,128)(2,1)S(1)}, u32[]{:S(2)}, u32[]{:S(2)}) collective-permute-start(bf16[224,576]{1,0:T(8,128)(2,1)} %rest_4_.1), channel_id=1, source_target_pairs={{0,8},{4,12},{8,0},{12,4},{16,24},{20,28},{24,16},{28,20},{1,9},{5... | collective-permute-start | bytes 774152 | tf_op jit(solution)/shard_map/ppermute | solution.py:338
  5.1 12.9 %collective-permute-start.4 = (bf16[224,576]{1,0:T(8,128)(2,1)}, bf16[224,576]{1,0:T(8,128)(2,1)S(1)}, u32[]{:S(2)}, u32[]{:S(2)}) collective-permute-start(bf16[224,576]{1,0:T(8,128)(2,1)} %rest_4_.1), channel_id=1, source_target_pairs={{0,16},{4,20},{8,24},{12,28},{16,0},{20,4},{24,8},{28,12},{1,17},{... | collective-permute-start | bytes 774152 | tf_op jit(solution)/shard_map/ppermute | solution.py:338
  5.2 13.4 %collective-permute-start.1 = (bf16[224,576]{1,0:T(8,128)(2,1)}, bf16[224,576]{1,0:T(8,128)(2,1)S(1)}, u32[]{:S(2)}, u32[]{:S(2)}) collective-permute-start(bf16[224,576]{1,0:T(8,128)(2,1)} %rest_4_.1), channel_id=1, source_target_pairs={{0,4},{4,0},{8,12},{12,8},{16,20},{20,16},{24,28},{28,24},{1,5},{5... | collective-permute-start | bytes 774152 | tf_op jit(solution)/shard_map/ppermute | solution.py:338
  5.2 1.5 %copy-start = (bf16[224,8,512]{2,1,0:T(8,128)(2,1)S(1)}, bf16[224,8,512]{2,1,0:T(8,128)(2,1)}, u32[]{:S(2)}) copy-start(bf16[224,8,512]{2,1,0:T(8,128)(2,1)} %param.7) | copy-start | bytes 5505028
  6.7 1.6 %copy-start.2 = (bf16[224,8,576]{2,1,0:T(8,128)(2,1)S(1)}, bf16[224,8,576]{2,1,0:T(8,128)(2,1)}, u32[]{:S(2)}) copy-start(bf16[224,8,576]{2,1,0:T(8,128)(2,1)} %param.5) | copy-start | bytes 6193156
  8.4 11.7 %copy-start.1 = (bf16[224,8,512]{2,1,0:T(8,128)(2,1)S(1)}, bf16[224,8,512]{2,1,0:T(8,128)(2,1)}, u32[]{:S(2)}) copy-start(bf16[224,8,512]{2,1,0:T(8,128)(2,1)} %param.7) | copy-start | bytes 5505028
  8.4 11.7 %copy-start.3 = (bf16[224,576]{1,0:T(8,128)(2,1)S(1)}, bf16[224,576]{1,0:T(8,128)(2,1)}, u32[]{:S(2)}) copy-start(bf16[224,576]{1,0:T(8,128)(2,1)} %rest_4_.1) | copy-start | bytes 774148
  8.4 11.7 %copy-start.4 = (s32[16]{0:T(128)S(1)}, s32[16]{0:T(128)}, u32[]{:S(2)}) copy-start(s32[16]{0:T(128)} %order_ref.3) | copy-start | bytes 196
  12.5 6.1 %collective-permute-start.6 = (bf16[224,576]{1,0:T(8,128)(2,1)S(1)}, bf16[224,576]{1,0:T(8,128)(2,1)S(1)}, u32[]{:S(2)}, u32[]{:S(2)}) collective-permute-start(bf16[224,576]{1,0:T(8,128)(2,1)S(1)} %collective-permute-done.rest_10_), channel_id=1, source_target_pairs={{0,4},{4,0},{8,12},{12,8},{16,20},{20,16},{24,28},{28,24},{1,5},{5... | collective-permute-start | bytes 774152 | tf_op jit(solution)/shard_map/ppermute | solution.py:338
  18.1 1.6 %collective-permute-start.3 = (bf16[224,576]{1,0:T(8,128)(2,1)S(1)}, bf16[224,576]{1,0:T(8,128)(2,1)S(1)}, u32[]{:S(2)}, u32[]{:S(2)}) collective-permute-start(bf16[224,576]{1,0:T(8,128)(2,1)S(1)} %collective-permute-done.2.rest_6_), channel_id=1, source_target_pairs={{0,4},{4,0},{8,12},{12,8},{16,20},{20,16},{24,28},{28,24},{1,5},{5... | collective-permute-start | bytes 774152 | tf_op jit(solution)/shard_map/ppermute | solution.py:338
  18.1 2.0 %collective-permute-start.5 = (bf16[224,576]{1,0:T(8,128)(2,1)S(1)}, bf16[224,576]{1,0:T(8,128)(2,1)S(1)}, u32[]{:S(2)}, u32[]{:S(2)}) collective-permute-start(bf16[224,576]{1,0:T(8,128)(2,1)S(1)} %collective-permute-done.4.rest_8_), channel_id=1, source_target_pairs={{0,4},{4,0},{8,12},{12,8},{16,20},{20,16},{24,28},{28,24},{1,5},{5... | collective-permute-start | bytes 774152 | tf_op jit(solution)/shard_map/ppermute | solution.py:338
  36.4 9.2 %collective-permute-start.7 = (bf16[2,224,640]{2,1,0:T(8,128)(2,1)S(1)}, bf16[2,224,640]{2,1,0:T(8,128)(2,1)S(1)}, u32[]{:S(2)}, u32[]{:S(2)}) collective-permute-start(bf16[2,224,640]{2,1,0:T(8,128)(2,1)S(1)} %get-tuple-element.32), channel_id=1, source_target_pairs={{0,4},{4,0},{8,12},{12,8},{16,20},{20,16},{24,28},{28,24},{1,5},{5... | collective-permute-start | bytes 1720328 | tf_op jit(solution)/shard_map/ppermute | solution.py:338
  45.7 9.8 %collective-permute-start.8 = (bf16[2,224,640]{2,1,0:T(8,128)(2,1)S(1)}, bf16[2,224,640]{2,1,0:T(8,128)(2,1)S(1)}, u32[]{:S(2)}, u32[]{:S(2)}) collective-permute-start(bf16[2,224,640]{2,1,0:T(8,128)(2,1)S(1)} %add_convert_fusion), channel_id=1, source_target_pairs={{0,16},{4,12},{8,24},{12,4},{16,0},{20,28},{24,8},{28,20},{1,17},{... | collective-permute-start | bytes 1720328 | tf_op jit(solution)/shard_map/ppermute | solution.py:385
  45.8 9.8 %collective-permute-start.9 = (bf16[2,224,640]{2,1,0:T(8,128)(2,1)S(1)}, bf16[2,224,640]{2,1,0:T(8,128)(2,1)S(1)}, u32[]{:S(2)}, u32[]{:S(2)}) collective-permute-start(bf16[2,224,640]{2,1,0:T(8,128)(2,1)S(1)} %get-tuple-element.44), channel_id=1, source_target_pairs={{0,4},{4,0},{8,12},{12,8},{16,20},{20,16},{24,28},{28,24},{1,5},{5... | collective-permute-start | bytes 1720328 | tf_op jit(solution)/shard_map/ppermute | solution.py:338
  55.8 6.7 %collective-permute-start.10 = (bf16[1,224,640]{2,1,0:T(8,128)(2,1)S(1)}, bf16[1,224,640]{2,1,0:T(8,128)(2,1)S(1)}, u32[]{:S(2)}, u32[]{:S(2)}) collective-permute-start(bf16[1,224,640]{2,1,0:T(8,128)(2,1)S(1)} %slice.44), channel_id=1, source_target_pairs={{0,8},{4,20},{8,0},{12,28},{16,24},{20,4},{24,16},{28,12},{1,9},{5... | collective-permute-start | bytes 860168 | tf_op jit(solution)/shard_map/ppermute | solution.py:385
  62.6 5.2 %collective-permute-start.11 = (bf16[112,640]{1,0:T(8,128)(2,1)S(1)}, bf16[112,640]{1,0:T(8,128)(2,1)S(1)}, u32[]{:S(2)}, u32[]{:S(2)}) collective-permute-start(bf16[112,640]{1,0:T(8,128)(2,1)S(1)} %fusion.2), channel_id=1, source_target_pairs={{0,1},{1,0},{2,3},{3,2},{4,5},{5,4},{6,7},{7,6},{8,9},{9,8},{10,11... | collective-permute-start | bytes 430088 | tf_op jit(solution)/shard_map/ppermute | solution.py:338
  67.8 7.7 %collective-permute-start.12 = (bf16[112,640]{1,0:T(8,128)(2,1)S(1)}, bf16[112,640]{1,0:T(8,128)(2,1)S(1)}, u32[]{:S(2)}, u32[]{:S(2)}) collective-permute-start(bf16[112,640]{1,0:T(8,128)(2,1)S(1)} %fusion.1), channel_id=1, source_target_pairs={{0,2},{1,3},{2,0},{3,1},{4,6},{5,7},{6,4},{7,5},{8,10},{9,11},{10,... | collective-permute-start | bytes 430088 | tf_op jit(solution)/shard_map/ppermute | solution.py:338
  75.6 5.2 %collective-permute-start.13 = (bf16[112,640]{1,0:T(8,128)(2,1)S(1)}, bf16[112,640]{1,0:T(8,128)(2,1)S(1)}, u32[]{:S(2)}, u32[]{:S(2)}) collective-permute-start(bf16[112,640]{1,0:T(8,128)(2,1)S(1)} %add_convert_fusion.1), channel_id=1, source_target_pairs={{0,1},{1,0},{2,3},{3,2},{4,5},{5,4},{6,7},{7,6},{8,9},{9,8},{10,11... | collective-permute-start | bytes 430088 | tf_op jit(solution)/shard_map/ppermute | solution.py:338

commit v5 on v4

--- a/solution.py
+++ b/solution.py
@@ -56,40 +56,185 @@
     return order, places, counts
 
 
-def layout_kernel(rows, q_ref, do_ref, qp_ref, qt_ref, dot_ref):
-    width = q_ref.shape[1]
-    qp_ref[:, :width] = q_ref[...]
-    qp_ref[:, width:] = jnp.zeros((qp_ref.shape[0], qp_ref.shape[1] - width), qp_ref.dtype)
-    for b in range(2):
-        span = slice(b * rows, b * rows + rows)
-        qt_ref[b] = q_ref[span, :].T
-        dot_ref[b] = do_ref[span, :].T
-
-
-def attention_kernel(direct, ctx_size, block_rows, heads, latent, width, order_ref, *rest):
+def layout_kernel(reorder, block_rows, order_ref, q_ref, do_ref, qp_ref, qt_ref, dot_ref):
+    total_rows, width = q_ref.shape
+    latent = do_ref.shape[1]
+    rows = total_rows // 2
+    order = range(2)
+    if reorder:
+        order, _, _ = query_blocks(order_ref, lax.axis_index("ctx"), block_rows)
+        whole, rest = divmod(width, tile)
+        for i in range(latent // tile):
+            qp_ref[i] = do_ref[:, i * tile : i * tile + tile]
+        for i in range(whole):
+            qp_ref[latent // tile + i] = q_ref[:, i * tile : i * tile + tile]
+        last = latent // tile + whole
+        qp_ref[last, :, :rest] = q_ref[:, whole * tile :]
+        qp_ref[last, :, rest:] = jnp.zeros((total_rows, tile - rest), qp_ref.dtype)
+    else:
+        qp_ref[:, :width] = q_ref[...]
+        qp_ref[:, width:] = jnp.zeros((total_rows, qp_ref.shape[1] - width), qp_ref.dtype)
+    for turn, b in enumerate(order):
+        span = pl.ds(pl.multiple_of(b * rows, lanes), rows)
+        qt_ref[:, turn * rows : turn * rows + rows] = q_ref[span, :].T
+        dot_ref[:, turn * rows : turn * rows + rows] = do_ref[span, :].T
+
+
+def sorted_block(order_ref, me, mask, sub, block_rows):
+    position = order_ref[2 * jnp.bitwise_xor(me, mask) + sub]
+    return pl.ds(pl.multiple_of(position * block_rows, 16), block_rows)
+
+
+def sort_keys(order_ref, me, key_refs, keys, block_rows):
+    width = key_refs[0].shape[1]
+    keys[:, width:] = jnp.zeros((keys.shape[0], keys.shape[1] - width), keys.dtype)
+    for mask, ref in enumerate(key_refs):
+        for sub in range(2):
+            keys[sorted_block(order_ref, me, mask, sub, block_rows), :width] = ref[
+                sub * block_rows : sub * block_rows + block_rows, :
+            ]
+
+
+def leaving_blocks(me, ctx_size, outs):
+    core = me % 2
+    targets = []
+    for label in range(ctx_size // 2):
+        masks = [chip_mask(label, c, ctx_size) for c in range(2)]
+        kept = jnp.where(core == 0, masks[0], masks[1])
+        sent = jnp.where(core == 0, masks[1], masks[0]) + 1
+        upper, slot = divmod(label, ctx_size // 4)
+        for mask, out in ((kept, outs[upper]), (sent, outs[2 + upper])):
+            targets += [(mask, sub, out, slot) for sub in range(2)]
+    return targets
+
+
+def short_kernel(ctx_size, block_rows, heads, latent, width, order_ref, work, qt, dot, *rest):
+    key_refs, outs, rest = rest[:ctx_size], rest[ctx_size : ctx_size + 4], rest[ctx_size + 4 :]
+    ds_ref, keys, scores, gprobs, peak, total, weighted = rest
+    stage = keys
+    seq = keys.shape[0]
+    rows = block_rows * heads
+    me = lax.axis_index("ctx")
+
+    sort_keys(order_ref, me, key_refs, keys, block_rows)
+
+    order, places, counts = query_blocks(order_ref, me, block_rows)
+    spans = [pl.ds(pl.multiple_of(b * rows, lanes), rows) for b in order]
+
+    def piece(h):
+        return slice(h % 2 * lanes, h % 2 * lanes + lanes)
+
+    for turn in range(2):
+        span, place = spans[turn], places[turn]
+        peak[turn] = jnp.full(peak.shape[1:], masked_value, jnp.float32)
+        total[turn] = jnp.zeros(total.shape[1:], jnp.float32)
+        weighted[turn] = jnp.zeros(weighted.shape[1:], jnp.float32)
+
+        def score_visit(j, n):
+            block = keys[key_rows(j, n), :]
+            whole = range(latent // tile, (latent + width) // tile)
+            q = jnp.concatenate(
+                [work[i, span, :] for i in whole] + [work[whole.stop, span, :lanes]], axis=1
+            )
+            do = jnp.concatenate([work[i, span, :] for i in range(latent // tile)], axis=1)
+            s = lax.dot_general(q, block, nt_dims, preferred_element_type=jnp.float32)
+            g = lax.dot_general(
+                do, block[:, :latent], nt_dims, preferred_element_type=jnp.float32
+            )
+            row_pos = (
+                place * block_rows
+                - j * tile
+                + lax.broadcasted_iota(jnp.int32, (rows, lanes), 0) // heads
+            )
+            col = lax.broadcasted_iota(jnp.int32, (rows, lanes), 1)
+            parts = []
+            for h in range(2 * n):
+                u = s[:, h * lanes : h * lanes + lanes] * (softmax_scale * log2_e)
+                parts.append(jnp.where(col + h * lanes <= row_pos, u, masked_value))
+            old = peak[turn]
+            m = functools.reduce(jnp.maximum, parts, old)
+            alpha = jnp.exp2(old - m)
+            acc = total[turn] * alpha
+            wacc = weighted[turn] * alpha
+            for h in range(2 * n):
+                p = jnp.exp2(parts[h] - m)
+                gh = g[:, h * lanes : h * lanes + lanes]
+                scores[turn, j + h // 2, :, piece(h)] = parts[h]
+                gprobs[turn, j + h // 2, :, piece(h)] = gh
+                acc += p
+                wacc += p * gh
+            peak[turn] = m
+            total[turn] = acc
+            weighted[turn] = wacc
+
+        visits(counts[turn], score_visit, 2)
+
+        top = jnp.max(peak[turn], axis=1, keepdims=True)
+        share = jnp.exp2(peak[turn] - top)
+        inverse = 1.0 / jnp.sum(total[turn] * share, axis=1, keepdims=True)
+        delta = jnp.sum(weighted[turn] * share, axis=1, keepdims=True) * inverse
+        peak[turn] = jnp.broadcast_to(top, peak.shape[1:])
+        total[turn] = jnp.broadcast_to(inverse, total.shape[1:])
+        weighted[turn] = jnp.broadcast_to(delta, weighted.shape[1:])
+
+    def row_gradients(turn, j, n):
+        grads, probs = [], []
+        for h in range(2 * n):
+            p = jnp.exp2(scores[turn, j + h // 2, :, piece(h)] - peak[turn]) * total[turn]
+            g = gprobs[turn, j + h // 2, :, piece(h)]
+            probs.append(p.astype(jnp.bfloat16))
+            grads.append((p * (g - weighted[turn])).astype(jnp.bfloat16))
+        ds, ph = jnp.concatenate(grads, axis=1), jnp.concatenate(probs, axis=1)
+        for t in range(n):
+            ds_ref[j + t, turn * rows : turn * rows + rows, :] = ds[:, t * tile : t * tile + tile]
+        return ds, ph
+
+    def key_sums(j, n, left, right, ds, ph):
+        kt = jnp.dot(left, ds, preferred_element_type=jnp.float32) * softmax_scale
+        vt = jnp.dot(right, ph, preferred_element_type=jnp.float32)
+        for t in range(n):
+            cols = slice(t * tile, t * tile + tile)
+            out = key_rows(j + t, 1)
+            stage[out, :latent] = (kt[:latent, cols] + vt[:, cols]).T.astype(jnp.bfloat16)
+            stage[out, latent:width] = kt[latent:, cols].T.astype(jnp.bfloat16)
+            stage[out, width:] = jnp.zeros((tile, stage.shape[1] - width), stage.dtype)
+
+    def both_visit(j, n):
+        pairs = zip(row_gradients(0, j, n), row_gradients(1, j, n))
+        key_sums(j, n, qt[...], dot[...], *(jnp.concatenate(pair, axis=0) for pair in pairs))
+
+    def later_visit(j, n):
+        j = counts[0] + j
+        key_sums(j, n, qt[:, rows:], dot[:, rows:], *row_gradients(1, j, n))
+
+    visits(counts[0], both_visit, 2)
+    visits(counts[1] - counts[0], later_visit, 2)
+
+    @pl.loop(counts[1], seq // tile)
+    def _(j):
+        stage[key_rows(j, 1), :] = jnp.zeros((tile, stage.shape[1]), stage.dtype)
+
+    for mask, sub, out, slot in leaving_blocks(me, ctx_size, outs):
+        out[slot, sub * block_rows : sub * block_rows + block_rows, :] = stage[
+            sorted_block(order_ref, me, mask, sub, block_rows), :
+        ]
+
+
+def long_kernel(ctx_size, block_rows, heads, latent, width, order_ref, *rest):
     q, do, qt, dot = rest[:4]
     key_refs = rest[4 : 4 + ctx_size]
     outs = rest[4 + ctx_size : 8 + ctx_size]
     rest = rest[8 + ctx_size :]
-    if direct:
-        keys, *ds_refs = rest[:3]
-        stage, probs, gprobs, marks, peak, total, weighted, dkt = rest[3:]
-    else:
-        dq_ref, stage, probs, gprobs, marks, peak, total, weighted, dkt, keys, dq_acc, move_sem = rest
+    dq_ref, stage, probs, gprobs, marks, peak, total, weighted, dkt, keys, dq_acc, move_sem = rest
     seq = keys.shape[0]
     tiles = seq // tile
     rows = block_rows * heads
     me = lax.axis_index("ctx")
 
     def sorted_rows(mask, sub):
-        position = order_ref[2 * jnp.bitwise_xor(me, mask) + sub]
-        return pl.ds(pl.multiple_of(position * block_rows, 16), block_rows)
+        return sorted_block(order_ref, me, mask, sub, block_rows)
 
     def move(pairs):
-        if direct:
-            for source, target in pairs:
-                target[...] = source[...]
-            return
         copies = [
             pltpu.make_async_copy(source, target, move_sem.at[i])
             for i, (source, target) in enumerate(pairs)
@@ -104,17 +249,12 @@
     def sub_rows(sub):
         return pl.ds(sub * block_rows, block_rows)
 
-    if direct:
-        keys[:, width:] = jnp.zeros((seq, keys.shape[1] - width), keys.dtype)
-        for mask, sub in blocks:
-            keys[sorted_rows(mask, sub), :width] = key_refs[mask][sub_rows(sub), :]
-    else:
-        move(
-            [
-                (key_refs[mask].at[sub_rows(sub), :], keys.at[sorted_rows(mask, sub), :])
-                for mask, sub in blocks
-            ]
-        )
+    move(
+        [
+            (key_refs[mask].at[sub_rows(sub), :], keys.at[sorted_rows(mask, sub), :])
+            for mask, sub in blocks
+        ]
+    )
 
     order, places, counts = query_blocks(order_ref, me, block_rows)
 
@@ -128,7 +268,7 @@
 
     for turn in range(2):
         b, place = order[turn], places[turn]
-        span = pl.ds(pl.multiple_of(b * rows, rows), rows)
+        span = pl.ds(pl.multiple_of(b * rows, lanes), rows)
         peak[...] = jnp.full_like(peak, masked_value)
         total[...] = jnp.zeros_like(total)
         weighted[...] = jnp.zeros_like(weighted)
@@ -175,8 +315,7 @@
         peak[...] = jnp.broadcast_to(top, peak.shape)
         total[...] = jnp.broadcast_to(inverse, total.shape)
         weighted[...] = jnp.broadcast_to(delta, weighted.shape)
-        if not direct:
-            dq_acc[...] = jnp.zeros_like(dq_acc)
+        dq_acc[...] = jnp.zeros_like(dq_acc)
 
         def grad_visit(j, n):
             factor = jnp.exp2(marks[j // 2] - peak[...]) * total[...]
@@ -189,15 +328,9 @@
                 grads.append((p * (g - delta)).astype(jnp.bfloat16))
             ds = jnp.concatenate(grads, axis=1)
             ph = jnp.concatenate(halves, axis=1)
-            if direct:
-                for t in range(n):
-                    ds_refs[turn][j + t] = ds[:, t * tile : t * tile + tile]
-            else:
-                dq_acc[...] += jnp.dot(
-                    ds, keys[key_rows(j, n), :], preferred_element_type=jnp.float32
-                )
-            kt = jnp.dot(qt[b], ds, preferred_element_type=jnp.float32) * softmax_scale
-            vt = jnp.dot(dot[b], ph, preferred_element_type=jnp.float32)
+            dq_acc[...] += jnp.dot(ds, keys[key_rows(j, n), :], preferred_element_type=jnp.float32)
+            kt = jnp.dot(qt[:, span], ds, preferred_element_type=jnp.float32) * softmax_scale
+            vt = jnp.dot(dot[:, span], ph, preferred_element_type=jnp.float32)
             for t in range(n):
                 cols = slice(t * tile, t * tile + tile)
                 low = kt[:latent, cols] + vt[:, cols]
@@ -215,122 +348,118 @@
                     )
 
         visits(counts[turn], grad_visit, 2)
-        if not direct:
-            dq_ref[span, :] = (dq_acc[:, :width] * softmax_scale).astype(jnp.bfloat16)
+        dq_ref[span, :] = (dq_acc[:, :width] * softmax_scale).astype(jnp.bfloat16)
 
     @pl.loop(counts[1], tiles)
     def _(j):
         stage[key_rows(j, 1), :] = jnp.zeros((tile, stage.shape[1]), stage.dtype)
 
-    core = me % 2
-    leaving = []
-    for label in range(ctx_size // 2):
-        masks = [chip_mask(label, c, ctx_size) for c in range(2)]
-        kept = jnp.where(core == 0, masks[0], masks[1])
-        sent = jnp.where(core == 0, masks[1], masks[0]) + 1
-        upper, slot = divmod(label, ctx_size // 4)
-        for mask, out in ((kept, outs[upper]), (sent, outs[2 + upper])):
-            for sub in range(2):
-                source = stage.at[sorted_rows(mask, sub), :]
-                leaving.append((source, out.at[slot, sub_rows(sub), :]))
-    move(leaving)
-
-
-def row_layouts(q, do, rows):
+    targets = leaving_blocks(me, ctx_size, outs)
+    move([(stage.at[sorted_rows(mask, sub), :], out.at[slot, sub_rows(sub), :]) for mask, sub, out, slot in targets])
+
+
+def row_layouts(order, q, do, block_rows, reorder, tiles):
     total_rows, width = q.shape
     latent = do.shape[1]
     vmem = pl.BlockSpec(memory_space=pltpu.VMEM)
     return pl.pallas_call(
-        functools.partial(layout_kernel, rows),
+        functools.partial(layout_kernel, reorder, block_rows),
         out_shape=(
-            jax.ShapeDtypeStruct((total_rows, padded(width)), q.dtype),
-            jax.ShapeDtypeStruct((2, width, rows), q.dtype),
-            jax.ShapeDtypeStruct((2, latent, rows), q.dtype),
+            jax.ShapeDtypeStruct(
+                (tiles, total_rows, tile) if reorder else (total_rows, padded(width)), q.dtype
+            ),
+            jax.ShapeDtypeStruct((width, total_rows), q.dtype),
+            jax.ShapeDtypeStruct((latent, total_rows), q.dtype),
         ),
-        in_specs=[vmem] * 2,
+        in_specs=[pl.BlockSpec(memory_space=pltpu.SMEM)] + [vmem] * 2,
         out_specs=(vmem,) * 3,
         compiler_params=pltpu.CompilerParams(vmem_limit_bytes=24 * mebibyte),
         name="row_layouts",
-    )(q, do)
-
-
-def query_kernel(block_rows, heads, order_ref, keys, ds0, ds1, dq_ref, acc):
-    rows = block_rows * heads
-    width = dq_ref.shape[1]
-    order, places, counts = query_blocks(order_ref, lax.axis_index("ctx"), block_rows)
+    )(order, q, do)
+
+
+def query_kernel(block_rows, order_ref, ds, *rest):
+    *key_refs, dq_ref, keys, acc = rest
+    me = lax.axis_index("ctx")
+    sort_keys(order_ref, me, key_refs, keys, block_rows)
+    order, _, counts = query_blocks(order_ref, me, block_rows)
+    rows, width = dq_ref.shape[0] // 2, dq_ref.shape[1]
+    acc[...] = jnp.zeros_like(acc)
+
+    def add(j, n, span):
+        left = jnp.concatenate([ds[j + t, span, :] for t in range(n)], axis=1)
+        acc[span, :] += jnp.dot(left, keys[key_rows(j, n), :], preferred_element_type=jnp.float32)
+
+    visits(counts[0], lambda j, n: add(j, n, slice(None)), 4)
+    visits(counts[1] - counts[0], lambda j, n: add(counts[0] + j, n, slice(rows, 2 * rows)), 2)
     for turn in range(2):
-        acc[...] = jnp.zeros_like(acc)
-
-        def visit(j, n, ds=(ds0, ds1)[turn]):
-            left = jnp.concatenate([ds[j + t] for t in range(n)], axis=1)
-            acc[...] += jnp.dot(left, keys[key_rows(j, n), :], preferred_element_type=jnp.float32)
-
-        visits(counts[turn], visit, 4)
-        span = pl.ds(pl.multiple_of(order[turn] * rows, rows), rows)
-        dq_ref[span, :] = (acc[:, :width] * softmax_scale).astype(jnp.bfloat16)
-
-
-def query_gradient(order, keys, ds0, ds1, block_rows, heads, width):
-    total_rows = 2 * block_rows * heads
+        span = pl.ds(pl.multiple_of(order[turn] * rows, lanes), rows)
+        dq_ref[span, :] = (
+            acc[turn * rows : turn * rows + rows, :width] * softmax_scale
+        ).astype(jnp.bfloat16)
+
+
+def query_gradient(order, ds, key_list, block_rows):
+    total_rows = ds.shape[1]
+    block, width = key_list[0].shape
+    keys = (len(key_list) * block, padded(width))
     vmem = pl.BlockSpec(memory_space=pltpu.VMEM)
     return pl.pallas_call(
-        functools.partial(query_kernel, block_rows, heads),
+        functools.partial(query_kernel, block_rows),
         out_shape=jax.ShapeDtypeStruct((total_rows, width), jnp.bfloat16),
-        in_specs=[pl.BlockSpec(memory_space=pltpu.SMEM)] + [vmem] * 3,
+        in_specs=[pl.BlockSpec(memory_space=pltpu.SMEM)] + [vmem] * (1 + len(key_list)),
         out_specs=vmem,
-        scratch_shapes=[pltpu.VMEM((block_rows * heads, keys.shape[1]), jnp.float32)],
-        compiler_params=pltpu.CompilerParams(vmem_limit_bytes=24 * mebibyte),
+        scratch_shapes=[
+            pltpu.VMEM(keys, jnp.bfloat16),
+            pltpu.VMEM((total_rows, keys[1]), jnp.float32),
+        ],
+        compiler_params=pltpu.CompilerParams(vmem_limit_bytes=32 * mebibyte),
         cost_estimate=pl.CostEstimate(
-            flops=2 * total_rows * keys.shape[0] * width, bytes_accessed=0, transcendentals=0
+            flops=2 * total_rows * keys[0] * width, bytes_accessed=0, transcendentals=0
         ),
         name="query_gradient",
-    )(order, keys, ds0, ds1)
-
-
-def attention(order, qp, do, qt, dot, key_list, block_rows, heads, width, direct):
+    )(order, ds, *key_list)
+
+
+def attention(order, row_arrays, key_list, block_rows, heads, width, direct):
     ctx_size = len(key_list)
-    total_rows = qp.shape[0]
-    latent = do.shape[1]
+    latent, total_rows = row_arrays[-1].shape
     rows = block_rows * heads
     seq = 2 * block_rows * ctx_size
     tiles = seq // tile
     vmem = pl.BlockSpec(memory_space=pltpu.VMEM)
     f32, bf16 = jnp.float32, jnp.bfloat16
     wide = padded(width)
-    buffers = [
-        ((seq, wide), bf16),
-        ((tiles, rows, tile), f32),
-        ((tiles, rows, tile), f32),
-        (((tiles + 1) // 2, rows, lanes), f32),
-        ((rows, lanes), f32),
-        ((rows, lanes), f32),
-        ((rows, lanes), f32),
-        ((tiles, width, tile), f32),
-    ]
     out_shape = [jax.ShapeDtypeStruct((ctx_size // 4, 2 * block_rows, wide), bf16)] * 4
+    buffers = [((seq, wide), bf16)]
+    scratch = []
     if direct:
-        out_shape += [
-            jax.ShapeDtypeStruct((seq, wide), bf16),
-            jax.ShapeDtypeStruct((tiles, rows, tile), bf16),
-            jax.ShapeDtypeStruct((tiles, rows, tile), bf16),
-        ]
-        scratch = []
+        out_shape += [jax.ShapeDtypeStruct((tiles, total_rows, tile), bf16)]
+        buffers += [((2, tiles, rows, tile), f32)] * 2
+        buffers += [((2, rows, lanes), f32)] * 3
     else:
         out_shape += [jax.ShapeDtypeStruct((total_rows, width), bf16)]
+        buffers += [((tiles, rows, tile), f32)] * 2 + [(((tiles + 1) // 2, rows, lanes), f32)]
+        buffers += [((rows, lanes), f32)] * 3 + [((tiles, width, tile), f32)]
         buffers += [((seq, wide), bf16), ((rows, wide), f32)]
         scratch = [pltpu.SemaphoreType.DMA((2 * ctx_size,))]
     blocks = vmem if direct else pl.BlockSpec(memory_space=pl.ANY)
     return pl.pallas_call(
-        functools.partial(attention_kernel, direct, ctx_size, block_rows, heads, latent, width),
+        functools.partial(
+            short_kernel if direct else long_kernel, ctx_size, block_rows, heads, latent, width
+        ),
         out_shape=tuple(out_shape),
-        in_specs=[pl.BlockSpec(memory_space=pltpu.SMEM)] + [vmem] * 4 + [blocks] * ctx_size,
+        in_specs=[pl.BlockSpec(memory_space=pltpu.SMEM)]
+        + [vmem] * len(row_arrays)
+        + [blocks] * ctx_size,
         out_specs=(blocks,) * 4 + (vmem,) * (len(out_shape) - 4),
+        input_output_aliases={1: 4} if direct else {},
         scratch_shapes=[pltpu.VMEM(shape, dtype) for shape, dtype in buffers] + scratch,
         compiler_params=pltpu.CompilerParams(
-            vmem_limit_bytes=(32 if direct else 63) * mebibyte
+            vmem_limit_bytes=(37 if direct else 63) * mebibyte
         ),
         name="attention_backward",
-    )(order, qp, do, qt, dot, *key_list)
+    )(order, *row_arrays, *key_list)
 
 
 def swap(x, axis, mask):
@@ -366,8 +495,9 @@
 
     query_rows = queries.reshape(token_count * head_count, key_width)
     grad_rows = dout.reshape(token_count * head_count, latent_width)
-    qp, qt, dot = row_layouts(query_rows, grad_rows, block_rows * head_count)
     direct = token_count * ctx_size <= 2048
+    tiles = token_count * ctx_size // tile
+    qp, qt, dot = row_layouts(block_order, query_rows, grad_rows, block_rows, direct, tiles)
     if not direct:
         keys = jnp.pad(keys, ((0, 0), (0, padded(key_width) - key_width)))
     same_core = [keys] + [swap(keys, "ctx", mask) for mask in range(2, ctx_size, 2)]
@@ -376,7 +506,13 @@
     for block in same_core:
         key_list += [block, swap(block, "ctx", 1)]
     low, high, low_sent, high_sent, *found = attention(
-        block_order, qp, grad_rows, qt, dot, key_list, block_rows, head_count, key_width, direct
+        block_order,
+        (qp, qt, dot) if direct else (qp, grad_rows, qt, dot),
+        key_list,
+        block_rows,
+        head_count,
+        key_width,
+        direct,
     )
 
     def exchange(sums):
@@ -393,7 +529,7 @@
     sums = both_cores(low, low_sent)
     grad_query = found[0]
     if direct:
-        grad_query = query_gradient(block_order, *found, block_rows, head_count, key_width)
+        grad_query = query_gradient(block_order, *found, key_list, block_rows)
         arrived, grad_query = lax.optimization_barrier((arrived, grad_query))
     grad_queries = grad_query.reshape(token_count, head_count, key_width)
     sums = sums + arrived

time: 81.1 us -> 76.6 us (0.945)
  starting transfers between devices: 18.2 us -> 10.6 us
  Pallas kernels: 24.3 us -> 29.5 us
  waiting for transfers between devices: 33.8 us -> 31.7 us
    ppermute x12, starting transfers between devices: 18.1 us -> 10.5 us  [swap(): return lax.ppermute(x, axis, [(i, i ^ mask) for i in range(size)])]
    pallas_call x3, Pallas kernels: 24.3 us -> 29.5 us  [the longest x1 19.7 us: attention(): pl.pallas_call(functools.partial(short_kernel if direct else long_kernel,...]
    ppermute x12, waiting for transfers between devices: 24.5 us -> 23.4 us  [swap(): return lax.ppermute(x, axis, [(i, i ^ mask) for i in range(size)])]
    ppermute x2, waiting for transfers between devices: 9.21 us -> 8.33 us  [exchange(): lax.ppermute(sums.astype(jnp.bfloat16), 'ctx', pairs).astype(jnp.float32)]
  transfers between devices with their start and end apart: 14 -> 14, of which waited for: 10 -> 10; matrix products, arithmetic and copies ran while one was open for 0% -> 0% of each run, Pallas kernels for 10% -> 13%
where the time goes in v5:
time: 76.6 us; the launch traced here: 77.9 us
  waiting for transfers between devices  31.7 us (41%)
  Pallas kernels  29.5 us (39%)
  starting transfers between devices  10.6 us (14%)
  local copies, waits for them, and re-layouts  3.84 us (5%)
  other arithmetic  1.43 us (2%)
    ppermute x12, waiting for transfers between devices, swap(): return lax.ppermute(x, axis, [(i, i ^ mask) for i in range(size)])  23.4 us
    pallas_call x1, Pallas kernels, attention(): pl.pallas_call(functools.partial(short_kernel if direct else long_kernel,...  19.7 us
    ppermute x12, starting transfers between devices, swap(): return lax.ppermute(x, axis, [(i, i ^ mask) for i in range(size)])  10.5 us
    ppermute x2, waiting for transfers between devices, exchange(): lax.ppermute(sums.astype(jnp.bfloat16), 'ctx', pairs).astype(jnp.float32)  8.33 us
    pallas_call x1, Pallas kernels, query_gradient(): pl.pallas_call(functools.partial(query_kernel, block_rows), out_shape=jax...  7.77 us
    unnamed x10, local copies, waits for them, and re-layouts  3.81 us
    pallas_call x1, Pallas kernels, row_layouts(): pl.pallas_call(functools.partial(layout_kernel, reorder, block_rows), out...  1.99 us
  transfers between devices with their start and end apart: 14, of which 10 were waited for; matrix products, arithmetic and copies ran while one was open for 0% of the time, Pallas kernels for 13%

profile of v5, /device:TPU:0, one launch (start us, length us, event | category | flops | bytes accessed | tf_op | source)
XLA Modules:
  0.0 77.9 jit_solution(8027297310536037694)
XLA Ops:
  0.6 4.0 %collective-permute-start = (bf16[224,576]{1,0:T(8,128)(2,1)}, bf16[224,576]{1,0:T(8,128)(2,1)S(1)}, u32[]{:S(2)}, u32[]{:S(2)}) collective-permute-start(bf16[224,576]{1,0:T(8,128)(2,1)} %rest_0_.3), channel_id=1, source_target_pairs={{0,24},{4,28},{8,16},{12,20},{16,8},{20,12},{24,0},{28,4},{1,25},{... | collective-permute-start | bytes 774152 | tf_op jit(solution)/shard_map/ppermute | solution.py:467
  4.6 0.5 collective-permute-start.2
  5.1 0.1 collective-permute-start.4
  5.2 0.0 collective-permute-start.1
  5.2 0.0 copy-start
  5.2 1.6 %copy-done = bf16[224,8,576]{2,1,0:T(8,128)(2,1)S(1)} copy-done((bf16[224,8,576]{2,1,0:T(8,128)(2,1)S(1)}, bf16[224,8,576]{2,1,0:T(8,128)(2,1)}, u32[]{:S(2)}) %copy-start) | copy-done | bytes 2064408
  6.9 0.0 copy-start.1
  6.9 1.5 %copy-done.1 = bf16[224,8,512]{2,1,0:T(8,128)(2,1)S(1)} copy-done((bf16[224,8,512]{2,1,0:T(8,128)(2,1)S(1)}, bf16[224,8,512]{2,1,0:T(8,128)(2,1)}, u32[]{:S(2)}) %copy-start.1) | copy-done | bytes 1835032
  8.4 0.0 copy-start.3
  8.4 0.7 copy-done.3
  9.0 0.0 copy-start.2
  9.0 0.0 copy-start.4
  9.0 2.0 %row_layouts.1 = (bf16[7,1792,256]{2,1,0:T(8,128)(2,1)S(1)}, bf16[576,1792]{1,0:T(8,128)(2,1)S(1)}, bf16[512,1792]{1,0:T(8,128)(2,1)S(1)}) custom-call(s32[16]{0:T(128)S(1)} %copy-done.3, bf16[1792,576]{1,0:T(8,128)(2,1)S(1)} %bitcast.9, bf16[1792,512]{1,0:T(8,128)(2,1)S(1)} %bitcast.10), custom_call_target="tpu_custom_call" | custom-call | tf_op jit(solution)/shard_map/row_layouts/pallas_call | solution.py:365
  11.0 1.5 %collective-permute-done.rest_6_ = bf16[224,576]{1,0:T(8,128)(2,1)S(1)} collective-permute-done((bf16[224,576]{1,0:T(8,128)(2,1)}, bf16[224,576]{1,0:T(8,128)(2,1)S(1)}, u32[]{:S(2)}, u32[]{:S(2)}) %collective-permute-start) | collective-permute-done | bytes 258080 | tf_op jit(solution)/shard_map/ppermute | solution.py:467
  12.5 0.0 collective-permute-start.6
  12.5 5.6 %collective-permute-done.2.rest_2_ = bf16[224,576]{1,0:T(8,128)(2,1)S(1)} collective-permute-done((bf16[224,576]{1,0:T(8,128)(2,1)}, bf16[224,576]{1,0:T(8,128)(2,1)S(1)}, u32[]{:S(2)}, u32[]{:S(2)}) %collective-permute-start.2) | collective-permute-done | bytes 258080 | tf_op jit(solution)/shard_map/ppermute | solution.py:467
  18.1 0.0 collective-permute-start.3
  18.1 0.0 collective-permute-done.4.rest_4_
  18.1 0.5 collective-permute-start.5
  18.6 0.0 collective-permute-done.1.rest_1_
  18.6 0.0 collective-permute-done.6.rest_7_
  18.6 1.1 %collective-permute-done.3.rest_3_ = bf16[224,576]{1,0:T(8,128)(2,1)S(1)} collective-permute-done((bf16[224,576]{1,0:T(8,128)(2,1)S(1)}, bf16[224,576]{1,0:T(8,128)(2,1)S(1)}, u32[]{:S(2)}, u32[]{:S(2)}) %collective-permute-start.3) | collective-permute-done | bytes 258080 | tf_op jit(solution)/shard_map/ppermute | solution.py:467
  19.6 0.4 collective-permute-done.5.rest_5_
  20.1 0.0 copy-done.2
  20.1 0.0 copy-done.4
  20.1 19.7 %attention_backward.1 = (bf16[2,224,640]{2,1,0:T(8,128)(2,1)S(1)}, bf16[2,224,640]{2,1,0:T(8,128)(2,1)S(1)}, bf16[2,224,640]{2,1,0:T(8,128)(2,1)S(1)}, bf16[2,22...) custom-call(s32[16]{0:T(128)S(1)} %copy-done.4, ...), custom_call_target="tpu_custom_call", output_to_operand_aliasing={{4}: (1, {})} | custom-call | tf_op jit(solution)/shard_map/attention_backward/pallas_call | solution.py:447
  39.8 0.1 collective-permute-start.7
  39.9 2.0 %collective-permute-done.7 = bf16[2,224,640]{2,1,0:T(8,128)(2,1)S(1)} collective-permute-done((bf16[2,224,640]{2,1,0:T(8,128)(2,1)S(1)}, bf16[2,224,640]{2,1,0:T(8,128)(2,1)S(1)}, u32[]{:S(2)}, u32[]{:S(2)}) %collective-permute-start.7) | collective-permute-done | bytes 573472 | tf_op jit(solution)/shard_map/ppermute | solution.py:467
  41.8 0.1 add_convert_fusion
  42.0 0.1 collective-permute-start.8
  42.1 0.2 collective-permute-start.9
  42.3 7.8 %query_gradient.1 = bf16[1792,576]{1,0:T(8,128)(2,1)} custom-call(s32[16]{0:T(128)S(1)} %copy-done.4, bf16[7,1792,256]{2,1,0:T(8,128)(2,1)S(1)} %get-tuple-element.33.ds, bf16[224,576]{1,0:T(8,128)(2,1)S(1)} %copy-done.2, bf16[224,576]{1,0:T(8,128)(2,1)S(1)} %collective-permute-done.1.rest_1_, bf16[224,576]{1,0:T(8,128)(2,1)S(1)} %collective-permute-done.2.rest_2_, ...), custom_call_target="tpu_custom_call" | custom-call | flops 3699376128 | tf_op jit(solution)/shard_map/query_gradient/pallas_call | solution.py:407
  50.0 1.7 %collective-permute-done.8 = bf16[2,224,640]{2,1,0:T(8,128)(2,1)S(1)} collective-permute-done((bf16[2,224,640]{2,1,0:T(8,128)(2,1)S(1)}, bf16[2,224,640]{2,1,0:T(8,128)(2,1)S(1)}, u32[]{:S(2)}, u32[]{:S(2)}) %collective-permute-start.8) | collective-permute-done | bytes 573472 | tf_op jit(solution)/shard_map/ppermute | solution.py:521
  51.8 0.1 convert_element_type.47
  51.8 0.0 collective-permute-done.9
  51.8 0.2 add_add_fusion
  52.0 0.1 collective-permute-start.10
  52.1 6.6 %collective-permute-done.10 = bf16[1,224,640]{2,1,0:T(8,128)(2,1)S(1)} collective-permute-done((bf16[1,224,640]{2,1,0:T(8,128)(2,1)S(1)}, bf16[1,224,640]{2,1,0:T(8,128)(2,1)S(1)}, u32[]{:S(2)}, u32[]{:S(2)}) %collective-permute-start.10) | collective-permute-done | bytes 286752 | tf_op jit(solution)/shard_map/ppermute | solution.py:521
  58.7 0.1 slice_add_fusion
  58.9 1.6 %collective-permute-start.11 = (bf16[112,640]{1,0:T(8,128)(2,1)S(1)}, bf16[112,640]{1,0:T(8,128)(2,1)S(1)}, u32[]{:S(2)}, u32[]{:S(2)}) collective-permute-start(bf16[112,640]{1,0:T(8,128)(2,1)S(1)} %fusion.2), channel_id=1, source_target_pairs={{0,1},{1,0},{2,3},{3,2},{4,5},{5,4},{6,7},{7,6},{8,9},{9,8},{10,11... | collective-permute-start | bytes 430088 | tf_op jit(solution)/shard_map/ppermute | solution.py:467
  60.5 3.5 %collective-permute-done.11 = bf16[112,640]{1,0:T(8,128)(2,1)S(1)} collective-permute-done((bf16[112,640]{1,0:T(8,128)(2,1)S(1)}, bf16[112,640]{1,0:T(8,128)(2,1)S(1)}, u32[]{:S(2)}, u32[]{:S(2)}) %collective-permute-start.11) | collective-permute-done | bytes 143392 | tf_op jit(solution)/shard_map/ppermute | solution.py:467
  64.1 2.7 %collective-permute-start.12 = (bf16[112,640]{1,0:T(8,128)(2,1)S(1)}, bf16[112,640]{1,0:T(8,128)(2,1)S(1)}, u32[]{:S(2)}, u32[]{:S(2)}) collective-permute-start(bf16[112,640]{1,0:T(8,128)(2,1)S(1)} %fusion.1), channel_id=1, source_target_pairs={{0,2},{1,3},{2,0},{3,1},{4,6},{5,7},{6,4},{7,5},{8,10},{9,11},{10,... | collective-permute-start | bytes 430088 | tf_op jit(solution)/shard_map/ppermute | solution.py:467
  66.8 5.0 %collective-permute-done.12 = bf16[112,640]{1,0:T(8,128)(2,1)S(1)} collective-permute-done((bf16[112,640]{1,0:T(8,128)(2,1)S(1)}, bf16[112,640]{1,0:T(8,128)(2,1)S(1)}, u32[]{:S(2)}, u32[]{:S(2)}) %collective-permute-start.12) | collective-permute-done | bytes 143392 | tf_op jit(solution)/shard_map/ppermute | solution.py:467
  71.8 0.7 collective-permute-start.13
  72.6 4.4 %collective-permute-done.13 = bf16[112,640]{1,0:T(8,128)(2,1)S(1)} collective-permute-done((bf16[112,640]{1,0:T(8,128)(2,1)S(1)}, bf16[112,640]{1,0:T(8,128)(2,1)S(1)}, u32[]{:S(2)}, u32[]{:S(2)}) %collective-permute-start.13) | collective-permute-done | bytes 143392 | tf_op jit(solution)/shard_map/ppermute | solution.py:467
  77.0 0.8 %fusion = f32[224,576]{1,0:T(8,128)} fusion(bf16[112,640]{1,0:T(8,128)(2,1)S(1)} %get-tuple-element.39, bf16[112,640]{1,0:T(8,128)(2,1)S(1)} %get-tuple-element.38), kind=kLoop, calls=%fused_computation.5 | loop fusion | flops 516096 | bytes 802816 | tf_op jit(solution)/shard_map/slice | solution.py:540
  (5 shorter events, 0.2 us)
Async XLA Ops:
  0.6 11.9 %collective-permute-start = (bf16[224,576]{1,0:T(8,128)(2,1)}, bf16[224,576]{1,0:T(8,128)(2,1)S(1)}, u32[]{:S(2)}, u32[]{:S(2)}) collective-permute-start(bf16[224,576]{1,0:T(8,128)(2,1)} %rest_0_.3), channel_id=1, source_target_pairs={{0,24},{4,28},{8,16},{12,20},{16,8},{20,12},{24,0},{28,4},{1,25},{... | collective-permute-start | bytes 774152 | tf_op jit(solution)/shard_map/ppermute | solution.py:467
  4.6 13.5 %collective-permute-start.2 = (bf16[224,576]{1,0:T(8,128)(2,1)}, bf16[224,576]{1,0:T(8,128)(2,1)S(1)}, u32[]{:S(2)}, u32[]{:S(2)}) collective-permute-start(bf16[224,576]{1,0:T(8,128)(2,1)} %rest_0_.3), channel_id=1, source_target_pairs={{0,8},{4,12},{8,0},{12,4},{16,24},{20,28},{24,16},{28,20},{1,9},{5... | collective-permute-start | bytes 774152 | tf_op jit(solution)/shard_map/ppermute | solution.py:467
  5.1 12.9 %collective-permute-start.4 = (bf16[224,576]{1,0:T(8,128)(2,1)}, bf16[224,576]{1,0:T(8,128)(2,1)S(1)}, u32[]{:S(2)}, u32[]{:S(2)}) collective-permute-start(bf16[224,576]{1,0:T(8,128)(2,1)} %rest_0_.3), channel_id=1, source_target_pairs={{0,16},{4,20},{8,24},{12,28},{16,0},{20,4},{24,8},{28,12},{1,17},{... | collective-permute-start | bytes 774152 | tf_op jit(solution)/shard_map/ppermute | solution.py:467
  5.2 13.4 %collective-permute-start.1 = (bf16[224,576]{1,0:T(8,128)(2,1)}, bf16[224,576]{1,0:T(8,128)(2,1)S(1)}, u32[]{:S(2)}, u32[]{:S(2)}) collective-permute-start(bf16[224,576]{1,0:T(8,128)(2,1)} %rest_0_.3), channel_id=1, source_target_pairs={{0,4},{4,0},{8,12},{12,8},{16,20},{20,16},{24,28},{28,24},{1,5},{5... | collective-permute-start | bytes 774152 | tf_op jit(solution)/shard_map/ppermute | solution.py:467
  5.2 1.6 %copy-start = (bf16[224,8,576]{2,1,0:T(8,128)(2,1)S(1)}, bf16[224,8,576]{2,1,0:T(8,128)(2,1)}, u32[]{:S(2)}) copy-start(bf16[224,8,576]{2,1,0:T(8,128)(2,1)} %param.5) | copy-start | bytes 6193156
  6.9 1.5 %copy-start.1 = (bf16[224,8,512]{2,1,0:T(8,128)(2,1)S(1)}, bf16[224,8,512]{2,1,0:T(8,128)(2,1)}, u32[]{:S(2)}) copy-start(bf16[224,8,512]{2,1,0:T(8,128)(2,1)} %param.7) | copy-start | bytes 5505028
  8.4 0.7 copy-start.3
  9.0 11.0 %copy-start.2 = (bf16[224,576]{1,0:T(8,128)(2,1)S(1)}, bf16[224,576]{1,0:T(8,128)(2,1)}, u32[]{:S(2)}) copy-start(bf16[224,576]{1,0:T(8,128)(2,1)} %rest_0_.3) | copy-start | bytes 774148
  9.0 11.0 %copy-start.4 = (s32[16]{0:T(128)S(1)}, s32[16]{0:T(128)}, u32[]{:S(2)}) copy-start(s32[16]{0:T(128)} %order_ref.5) | copy-start | bytes 196
  12.5 6.1 %collective-permute-start.6 = (bf16[224,576]{1,0:T(8,128)(2,1)S(1)}, bf16[224,576]{1,0:T(8,128)(2,1)S(1)}, u32[]{:S(2)}, u32[]{:S(2)}) collective-permute-start(bf16[224,576]{1,0:T(8,128)(2,1)S(1)} %collective-permute-done.rest_6_), channel_id=1, source_target_pairs={{0,4},{4,0},{8,12},{12,8},{16,20},{20,16},{24,28},{28,24},{1,5},{5... | collective-permute-start | bytes 774152 | tf_op jit(solution)/shard_map/ppermute | solution.py:467
  18.1 1.6 %collective-permute-start.3 = (bf16[224,576]{1,0:T(8,128)(2,1)S(1)}, bf16[224,576]{1,0:T(8,128)(2,1)S(1)}, u32[]{:S(2)}, u32[]{:S(2)}) collective-permute-start(bf16[224,576]{1,0:T(8,128)(2,1)S(1)} %collective-permute-done.2.rest_2_), channel_id=1, source_target_pairs={{0,4},{4,0},{8,12},{12,8},{16,20},{20,16},{24,28},{28,24},{1,5},{5... | collective-permute-start | bytes 774152 | tf_op jit(solution)/shard_map/ppermute | solution.py:467
  18.1 2.0 %collective-permute-start.5 = (bf16[224,576]{1,0:T(8,128)(2,1)S(1)}, bf16[224,576]{1,0:T(8,128)(2,1)S(1)}, u32[]{:S(2)}, u32[]{:S(2)}) collective-permute-start(bf16[224,576]{1,0:T(8,128)(2,1)S(1)} %collective-permute-done.4.rest_4_), channel_id=1, source_target_pairs={{0,4},{4,0},{8,12},{12,8},{16,20},{20,16},{24,28},{28,24},{1,5},{5... | collective-permute-start | bytes 774152 | tf_op jit(solution)/shard_map/ppermute | solution.py:467
  39.8 2.0 %collective-permute-start.7 = (bf16[2,224,640]{2,1,0:T(8,128)(2,1)S(1)}, bf16[2,224,640]{2,1,0:T(8,128)(2,1)S(1)}, u32[]{:S(2)}, u32[]{:S(2)}) collective-permute-start(bf16[2,224,640]{2,1,0:T(8,128)(2,1)S(1)} %get-tuple-element.28), channel_id=1, source_target_pairs={{0,4},{4,0},{8,12},{12,8},{16,20},{20,16},{24,28},{28,24},{1,5},{5... | collective-permute-start | bytes 1720328 | tf_op jit(solution)/shard_map/ppermute | solution.py:467
  42.0 9.8 %collective-permute-start.8 = (bf16[2,224,640]{2,1,0:T(8,128)(2,1)S(1)}, bf16[2,224,640]{2,1,0:T(8,128)(2,1)S(1)}, u32[]{:S(2)}, u32[]{:S(2)}) collective-permute-start(bf16[2,224,640]{2,1,0:T(8,128)(2,1)S(1)} %add_convert_fusion), channel_id=1, source_target_pairs={{0,16},{4,12},{8,24},{12,4},{16,0},{20,28},{24,8},{28,20},{1,17},{... | collective-permute-start | bytes 1720328 | tf_op jit(solution)/shard_map/ppermute | solution.py:521
  42.1 9.8 %collective-permute-start.9 = (bf16[2,224,640]{2,1,0:T(8,128)(2,1)S(1)}, bf16[2,224,640]{2,1,0:T(8,128)(2,1)S(1)}, u32[]{:S(2)}, u32[]{:S(2)}) collective-permute-start(bf16[2,224,640]{2,1,0:T(8,128)(2,1)S(1)} %get-tuple-element.36), channel_id=1, source_target_pairs={{0,4},{4,0},{8,12},{12,8},{16,20},{20,16},{24,28},{28,24},{1,5},{5... | collective-permute-start | bytes 1720328 | tf_op jit(solution)/shard_map/ppermute | solution.py:467
  52.0 6.7 %collective-permute-start.10 = (bf16[1,224,640]{2,1,0:T(8,128)(2,1)S(1)}, bf16[1,224,640]{2,1,0:T(8,128)(2,1)S(1)}, u32[]{:S(2)}, u32[]{:S(2)}) collective-permute-start(bf16[1,224,640]{2,1,0:T(8,128)(2,1)S(1)} %slice.44), channel_id=1, source_target_pairs={{0,8},{4,20},{8,0},{12,28},{16,24},{20,4},{24,16},{28,12},{1,9},{5... | collective-permute-start | bytes 860168 | tf_op jit(solution)/shard_map/ppermute | solution.py:521
  58.9 5.2 %collective-permute-start.11 = (bf16[112,640]{1,0:T(8,128)(2,1)S(1)}, bf16[112,640]{1,0:T(8,128)(2,1)S(1)}, u32[]{:S(2)}, u32[]{:S(2)}) collective-permute-start(bf16[112,640]{1,0:T(8,128)(2,1)S(1)} %fusion.2), channel_id=1, source_target_pairs={{0,1},{1,0},{2,3},{3,2},{4,5},{5,4},{6,7},{7,6},{8,9},{9,8},{10,11... | collective-permute-start | bytes 430088 | tf_op jit(solution)/shard_map/ppermute | solution.py:467
  64.1 7.7 %collective-permute-start.12 = (bf16[112,640]{1,0:T(8,128)(2,1)S(1)}, bf16[112,640]{1,0:T(8,128)(2,1)S(1)}, u32[]{:S(2)}, u32[]{:S(2)}) collective-permute-start(bf16[112,640]{1,0:T(8,128)(2,1)S(1)} %fusion.1), channel_id=1, source_target_pairs={{0,2},{1,3},{2,0},{3,1},{4,6},{5,7},{6,4},{7,5},{8,10},{9,11},{10,... | collective-permute-start | bytes 430088 | tf_op jit(solution)/shard_map/ppermute | solution.py:467
  71.8 5.2 %collective-permute-start.13 = (bf16[112,640]{1,0:T(8,128)(2,1)S(1)}, bf16[112,640]{1,0:T(8,128)(2,1)S(1)}, u32[]{:S(2)}, u32[]{:S(2)}) collective-permute-start(bf16[112,640]{1,0:T(8,128)(2,1)S(1)} %add_convert_fusion.1), channel_id=1, source_target_pairs={{0,1},{1,0},{2,3},{3,2},{4,5},{5,4},{6,7},{7,6},{8,9},{9,8},{10,11... | collective-permute-start | bytes 430088 | tf_op jit(solution)/shard_map/ppermute | solution.py:467
